TPU v7x, 32 devices: a whole 2x2x4 slice. The times are simulated.
32 devices in a mesh: dp: 8 (over z, core), seq: 4 (over y, x).
Axes of the slice: x: 2, y: 2, z: 4, core: 2. Of those that a mesh axis runs over, the one named last changes fastest.
Arguments:
- tokens_in: bfloat16 [8, 2048, 2048], P('dp', 'seq'), may hold values from -6 to 6
- grad_out: bfloat16 [8, 2048, 2048], P('dp', 'seq'), may hold values from -6 to 6
- seq_lengths: int32 [8], P('dp'), may hold values from 512 to 2048, as said below
- stretch_order: int32 [8, 8], P('dp'), may hold values from 0 to 7, each once within a row
- attn_gain: bfloat16 [2048], P(('dp', 'seq')), may hold values from 0.5 to 1.5
- query_w: bfloat16 [2048, 2048], P(('dp', 'seq')), may hold values from -0.125 to 0.125
- key_w: bfloat16 [2048, 512], P(('dp', 'seq')), may hold values from -0.125 to 0.125
- value_w: bfloat16 [2048, 512], P(('dp', 'seq')), may hold values from -0.125 to 0.125
- output_w: bfloat16 [2048, 2048], P(('dp', 'seq')), may hold values from -0.75 to 0.75
- mlp_gain: bfloat16 [2048], P(('dp', 'seq')), may hold values from 0.5 to 1.5
- gate_w: bfloat16 [2048, 8192], P(('dp', 'seq')), may hold values from -0.125 to 0.125
- up_w: bfloat16 [2048, 8192], P(('dp', 'seq')), may hold values from -0.125 to 0.125
- down_w: bfloat16 [2048, 8192], P(('dp', 'seq')), may hold values from -0.0625 to 0.0625
Outputs:
- tokens_out: bfloat16 [8, 2048, 2048], P('dp', 'seq')
- tokens_grad: float32 [8, 2048, 2048], P('dp', 'seq')
- attn_gain_grad: float32 [2048], P(('dp', 'seq'))
- query_grad: float32 [2048, 2048], P(('dp', 'seq'))
- key_grad: float32 [2048, 512], P(('dp', 'seq'))
- value_grad: float32 [2048, 512], P(('dp', 'seq'))
- output_grad: float32 [2048, 2048], P(('dp', 'seq'))
- mlp_gain_grad: float32 [2048], P(('dp', 'seq'))
- gate_grad: float32 [2048, 8192], P(('dp', 'seq'))
- up_grad: float32 [2048, 8192], P(('dp', 'seq'))
- down_grad: float32 [2048, 8192], P(('dp', 'seq'))
Inputs may be any that keep to these rules, and one draw needn't show every extreme that they name: `seq_lengths`: in every draw some sequence is full. Each row is a permutation; stored block c of sequence s holds positions stretch_order[s, c] * 256 to stretch_order[s, c] * 256 + 255.
All inputs are finite; a program needn't handle non-finite values.
Results may differ from a plain program's by a relative error of at most 0.017.
Values may be sent and summed in bfloat16 or wider, within the bound.
A program may use at most 704 MiB of HBM per device.

v0:
```python
import math

import jax
import jax.numpy as jnp
from jax import lax
from jax.sharding import PartitionSpec as P

HEADS = 32
KVH = 8
HD = 64


epsilon = 1e-05
masked_score = -1e30
floor_score = -1e29


def frequencies():
    steps_even = jnp.arange(0, HD, 2).astype(jnp.float32) / HD
    base_freq = 1.0 / 500000.0**steps_even
    wavelength = 2.0 * math.pi / base_freq
    smooth = (8192.0 / wavelength - 1.0) / 3.0
    blended = (1.0 - smooth) * base_freq / 32.0 + smooth * base_freq
    return jnp.where(
        wavelength < 2048.0, base_freq, jnp.where(wavelength > 8192.0, base_freq / 32.0, blended)
    )


def rotate(vectors, cos_table, sin_table):
    middle_at = vectors.shape[-1] // 2
    first_half = vectors[..., :middle_at]
    second_half = vectors[..., middle_at:]
    return jnp.concatenate(
        [
            first_half * cos_table - second_half * sin_table,
            second_half * cos_table + first_half * sin_table,
        ],
        axis=-1,
    )


def rotate_back(gradients, cos_table, sin_table):
    middle_at = gradients.shape[-1] // 2
    first_half = gradients[..., :middle_at]
    second_half = gradients[..., middle_at:]
    return jnp.concatenate(
        [
            first_half * cos_table + second_half * sin_table,
            second_half * cos_table - first_half * sin_table,
        ],
        axis=-1,
    )


def allowed_mask(pos_query, pos_slab, seq_length):
    return (pos_slab[None, :] <= pos_query[:, None]) & (pos_slab[None, :] < seq_length)


def block_scores(queries, key_slab, allowed):
    scores = (
        jnp.einsum("qgrd,kgd->grqk", queries, key_slab, preferred_element_type=jnp.float32) * 0.125
    )
    return jnp.where(allowed[None, None], scores, masked_score)


def attention(queries, key_rows, value_rows, pos_query, pos_keys, seq_length, key_block):
    query_rows = queries.shape[0]
    kv_heads = queries.shape[1]
    repeat = queries.shape[2]
    count = key_rows.shape[0] // key_block
    key_slabs = key_rows.reshape(count, key_block, kv_heads, HD)
    value_slabs = value_rows.reshape(count, key_block, kv_heads, HD)
    pos_slabs = pos_keys.reshape(count, key_block)

    def first_pass(carried, block_item):
        key_slab, pos_slab = block_item
        allowed = allowed_mask(pos_query, pos_slab, seq_length)
        running_max, running_sum = carried
        scores = block_scores(queries, key_slab, allowed)
        new_max = jnp.maximum(running_max, jnp.max(scores, axis=-1))
        running_sum = running_sum * jnp.exp(running_max - new_max) + jnp.sum(
            jnp.exp(scores - new_max[..., None]), axis=-1
        )
        return ((new_max, running_sum), None)

    start = (
        jnp.full((kv_heads, repeat, query_rows), floor_score, jnp.float32),
        jnp.zeros((kv_heads, repeat, query_rows), jnp.float32),
    )
    (running_max, running_sum), _ = lax.scan(first_pass, start, (key_slabs, pos_slabs))
    log_total = running_max + jnp.log(running_sum)

    def second_pass(accumulated, block_item):
        key_slab, value_slab, pos_slab = block_item
        allowed = allowed_mask(pos_query, pos_slab, seq_length)
        probs = jnp.exp(block_scores(queries, key_slab, allowed) - log_total[..., None]).astype(
            jnp.bfloat16
        )
        return (
            accumulated
            + jnp.einsum("grqk,kgd->qgrd", probs, value_slab, preferred_element_type=jnp.float32),
            None,
        )

    attended, _ = lax.scan(
        second_pass,
        jnp.zeros((query_rows, kv_heads, repeat, HD), jnp.float32),
        (key_slabs, value_slabs, pos_slabs),
    )
    return (attended, log_total)


def attention_back(
    queries,
    key_rows,
    value_rows,
    pos_query,
    pos_keys,
    seq_length,
    key_block,
    log_total,
    grad_heads,
    row_delta,
):
    query_rows = queries.shape[0]
    kv_heads = queries.shape[1]
    repeat = queries.shape[2]
    count = key_rows.shape[0] // key_block
    key_slabs = key_rows.reshape(count, key_block, kv_heads, HD)
    value_slabs = value_rows.reshape(count, key_block, kv_heads, HD)
    pos_slabs = pos_keys.reshape(count, key_block)

    def step_back(grad_query, block_item):
        key_slab, value_slab, pos_slab = block_item
        allowed = allowed_mask(pos_query, pos_slab, seq_length)
        grad_sofar = grad_query
        probs = jnp.exp(block_scores(queries, key_slab, allowed) - log_total[..., None])
        grad_probs = jnp.einsum(
            "qgrd,kgd->grqk", grad_heads, value_slab, preferred_element_type=jnp.float32
        )
        grad_scores = (probs * (grad_probs - row_delta[..., None])).astype(jnp.bfloat16)
        grad_sofar = (
            grad_sofar
            + jnp.einsum(
                "grqk,kgd->qgrd", grad_scores, key_slab, preferred_element_type=jnp.float32
            )
            * 0.125
        )
        grad_keyslab = (
            jnp.einsum("grqk,qgrd->kgd", grad_scores, queries, preferred_element_type=jnp.float32)
            * 0.125
        )
        grad_valueslab = jnp.einsum(
            "grqk,qgrd->kgd",
            probs.astype(jnp.bfloat16),
            grad_heads,
            preferred_element_type=jnp.float32,
        )
        return (grad_sofar, (grad_keyslab, grad_valueslab))

    grad_query, (grad_keys, grad_values) = lax.scan(
        step_back,
        jnp.zeros((query_rows, kv_heads, repeat, HD), jnp.float32),
        (key_slabs, value_slabs, pos_slabs),
    )
    return (
        grad_query,
        grad_keys.reshape(count * key_block, kv_heads * HD),
        grad_values.reshape(count * key_block, kv_heads * HD),
    )


def fsdp_layer(
    tokens_in, grad_out, seq_lengths, shards, positions, local_pos, live_rows, key_block, gate_w
):
    weights = (
        lax.all_gather(shards[0], ("dp", "seq"), axis=0, tiled=True),
        lax.all_gather(shards[1], ("dp", "seq"), axis=0, tiled=True),
        lax.all_gather(shards[2], ("dp", "seq"), axis=0, tiled=True),
        lax.all_gather(shards[3], ("dp", "seq"), axis=0, tiled=True),
        lax.all_gather(shards[4], ("dp", "seq"), axis=0, tiled=True),
        lax.all_gather(shards[5], ("dp", "seq"), axis=0, tiled=True),
        lax.all_gather(shards[6], ("dp", "seq"), axis=0, tiled=True),
        lax.all_gather(shards[7], ("dp", "seq"), axis=0, tiled=True),
        lax.all_gather(shards[8], ("dp", "seq"), axis=0, tiled=True),
    )
    groups, row_count, model_width = tokens_in.shape
    repeat = HEADS // KVH
    kv_width = KVH * HD
    total_rows = groups * row_count
    angles = local_pos.reshape(total_rows).astype(jnp.float32)[:, None] * frequencies()[None, :]
    cos_table = jnp.cos(angles)[:, None, :]
    sin_table = jnp.sin(angles)[:, None, :]
    gain_one = weights[0].astype(jnp.float32)
    gain_two = weights[5].astype(jnp.float32)
    inputs = tokens_in.reshape(total_rows, model_width).astype(jnp.float32)
    scale_one = lax.rsqrt(jnp.mean(inputs * inputs, axis=1, keepdims=True) + epsilon)
    unit_one = inputs * scale_one
    normed_one = (unit_one * gain_one).astype(jnp.bfloat16)
    queries = jnp.dot(normed_one, weights[1], preferred_element_type=jnp.float32).reshape(
        total_rows, HEADS, HD
    )
    key_pre = jnp.dot(normed_one, weights[2], preferred_element_type=jnp.float32).reshape(
        total_rows, KVH, HD
    )
    value_rows = jnp.dot(normed_one, weights[3], preferred_element_type=jnp.float32).astype(
        jnp.bfloat16
    )
    query_rot = (
        rotate(queries, cos_table, sin_table)
        .astype(jnp.bfloat16)
        .reshape(groups, row_count, KVH, repeat, HD)
    )
    key_rot = (
        rotate(key_pre, cos_table, sin_table)
        .astype(jnp.bfloat16)
        .reshape(groups, row_count, kv_width)
    )
    all_keys, all_values = (
        lax.all_gather(key_rot, "seq", axis=1, tiled=True),
        lax.all_gather(value_rows.reshape(groups, row_count, kv_width), "seq", axis=1, tiled=True),
    )
    member = 0
    attended, log_total = attention(
        query_rot[member],
        all_keys[member],
        all_values[member],
        local_pos[member],
        positions[member],
        seq_lengths[member],
        key_block,
    )
    attended_list = [attended]
    total_list = [log_total]
    attn_low = jnp.stack(attended_list).reshape(total_rows, model_width).astype(jnp.bfloat16)
    branch_one = jnp.einsum("ti,oi->to", attn_low, weights[4], preferred_element_type=jnp.float32)
    middle = inputs + branch_one
    scale_two = lax.rsqrt(jnp.mean(middle * middle, axis=1, keepdims=True) + epsilon)
    unit_two = middle * scale_two
    normed_two = (unit_two * gain_two).astype(jnp.bfloat16)
    gate_pre = jnp.dot(normed_two, weights[6], preferred_element_type=jnp.float32)
    up_pre = jnp.dot(normed_two, weights[7], preferred_element_type=jnp.float32)
    sigmoid_gate = jax.nn.sigmoid(gate_pre)
    silu_gate = gate_pre * sigmoid_gate
    hidden = (silu_gate * up_pre).astype(jnp.bfloat16)
    branch_two = jnp.einsum("tf,of->to", hidden, weights[8], preferred_element_type=jnp.float32)
    result = (
        ((middle + branch_two) * live_rows)
        .astype(jnp.bfloat16)
        .reshape(groups, row_count, model_width)
    )
    weights_back = (
        lax.all_gather(shards[0], ("dp", "seq"), axis=0, tiled=True),
        lax.all_gather(shards[1], ("dp", "seq"), axis=0, tiled=True),
        lax.all_gather(shards[2], ("dp", "seq"), axis=0, tiled=True),
        lax.all_gather(shards[3], ("dp", "seq"), axis=0, tiled=True),
        lax.all_gather(shards[4], ("dp", "seq"), axis=0, tiled=True),
        lax.all_gather(shards[5], ("dp", "seq"), axis=0, tiled=True),
        lax.all_gather(shards[6], ("dp", "seq"), axis=0, tiled=True),
        lax.all_gather(shards[7], ("dp", "seq"), axis=0, tiled=True),
        lax.all_gather(shards[8], ("dp", "seq"), axis=0, tiled=True),
    )
    grad_rows = grad_out.reshape(total_rows, model_width).astype(jnp.float32) * live_rows
    grad_low = grad_rows.astype(jnp.bfloat16)
    grad_hidden = jnp.dot(grad_low, weights_back[8], preferred_element_type=jnp.float32)
    grad_gate = (
        grad_hidden * up_pre * sigmoid_gate * (1.0 + gate_pre * (1.0 - sigmoid_gate))
    ).astype(jnp.bfloat16)
    grad_up = (grad_hidden * silu_gate).astype(jnp.bfloat16)
    grad_norm_two = jnp.einsum(
        "tf,df->td", grad_gate, weights_back[6], preferred_element_type=jnp.float32
    )
    grad_norm_two = grad_norm_two + jnp.einsum(
        "tf,df->td", grad_up, weights_back[7], preferred_element_type=jnp.float32
    )
    gain_two_grad = jnp.sum(grad_norm_two * unit_two, axis=0)
    scaled_two = grad_norm_two * gain_two
    grad_middle = grad_rows + scale_two * (
        scaled_two - unit_two * jnp.mean(scaled_two * unit_two, axis=1, keepdims=True)
    )
    mlp_sums = lax.psum_scatter(
        jnp.concatenate(
            [
                jnp.einsum("tc,tf->cf", normed_two, grad_gate, preferred_element_type=jnp.float32),
                jnp.einsum("tc,tf->cf", normed_two, grad_up, preferred_element_type=jnp.float32),
                jnp.einsum("tc,tf->cf", grad_low, hidden, preferred_element_type=jnp.float32),
            ],
            axis=1,
        ),
        ("dp", "seq"),
        scatter_dimension=0,
        tiled=True,
    )
    ff_width = gate_w.shape[1]
    gate_grad = mlp_sums[:, :ff_width]
    up_grad = mlp_sums[:, ff_width : 2 * ff_width]
    down_grad = mlp_sums[:, 2 * ff_width :]
    grad_branch = grad_middle.astype(jnp.bfloat16)
    output_grad = jnp.einsum("to,ti->oi", grad_branch, attn_low, preferred_element_type=jnp.float32)
    grad_attn = (
        jnp.dot(grad_branch, weights_back[4], preferred_element_type=jnp.float32)
        .astype(jnp.bfloat16)
        .reshape(groups, row_count, KVH, repeat, HD)
    )
    member = 0
    row_delta = jnp.einsum(
        "qgrd,qgrd->grq", grad_attn[member].astype(jnp.float32), attended_list[member]
    )
    grad_query, grad_keys, grad_values = attention_back(
        query_rot[member],
        all_keys[member],
        all_values[member],
        local_pos[member],
        positions[member],
        seq_lengths[member],
        key_block,
        total_list[member],
        grad_attn[member],
        row_delta,
    )
    query_list = [grad_query]
    key_list = [grad_keys]
    value_list = [grad_values]
    key_sum, value_sum = (
        lax.psum_scatter(
            jnp.stack(key_list).astype(jnp.bfloat16), "seq", scatter_dimension=1, tiled=True
        ).astype(jnp.float32),
        lax.psum_scatter(
            jnp.stack(value_list).astype(jnp.bfloat16), "seq", scatter_dimension=1, tiled=True
        ).astype(jnp.float32),
    )
    grad_qpre = (
        rotate_back(jnp.stack(query_list).reshape(total_rows, HEADS, HD), cos_table, sin_table)
        .reshape(total_rows, model_width)
        .astype(jnp.bfloat16)
    )
    grad_kpre = (
        rotate_back(key_sum.reshape(total_rows, KVH, HD), cos_table, sin_table)
        .reshape(total_rows, kv_width)
        .astype(jnp.bfloat16)
    )
    grad_vpre = value_sum.reshape(total_rows, kv_width).astype(jnp.bfloat16)
    query_grad = jnp.einsum("td,tf->df", normed_one, grad_qpre, preferred_element_type=jnp.float32)
    key_grad = jnp.einsum("td,tf->df", normed_one, grad_kpre, preferred_element_type=jnp.float32)
    value_grad = jnp.einsum("td,tf->df", normed_one, grad_vpre, preferred_element_type=jnp.float32)
    grad_norm_one = jnp.einsum(
        "tf,df->td", grad_qpre, weights_back[1], preferred_element_type=jnp.float32
    )
    grad_norm_one = grad_norm_one + jnp.einsum(
        "tf,df->td", grad_kpre, weights_back[2], preferred_element_type=jnp.float32
    )
    grad_norm_one = grad_norm_one + jnp.einsum(
        "tf,df->td", grad_vpre, weights_back[3], preferred_element_type=jnp.float32
    )
    gain_one_grad = jnp.sum(grad_norm_one * unit_one, axis=0)
    scaled_one = grad_norm_one * gain_one
    grad_inputs = grad_middle + scale_one * (
        scaled_one - unit_one * jnp.mean(scaled_one * unit_one, axis=1, keepdims=True)
    )
    summed_back = (
        lax.psum_scatter(gain_one_grad, ("dp", "seq"), scatter_dimension=0, tiled=True),
        lax.psum_scatter(query_grad, ("dp", "seq"), scatter_dimension=0, tiled=True),
        lax.psum_scatter(key_grad, ("dp", "seq"), scatter_dimension=0, tiled=True),
        lax.psum_scatter(value_grad, ("dp", "seq"), scatter_dimension=0, tiled=True),
        lax.psum_scatter(output_grad, ("dp", "seq"), scatter_dimension=0, tiled=True),
        lax.psum_scatter(gain_two_grad, ("dp", "seq"), scatter_dimension=0, tiled=True),
    )
    return (
        result,
        grad_inputs.reshape(groups, row_count, model_width),
        summed_back[0],
        summed_back[1],
        summed_back[2],
        summed_back[3],
        summed_back[4],
        summed_back[5],
        gate_grad,
        up_grad,
        down_grad,
    )


def body(
    tokens_in,
    grad_out,
    seq_lengths,
    stretch_order,
    attn_gain,
    query_w,
    key_w,
    value_w,
    output_w,
    mlp_gain,
    gate_w,
    up_w,
    down_w,
):
    shards = (attn_gain, query_w, key_w, value_w, output_w, mlp_gain, gate_w, up_w, down_w)
    groups, row_count, model_width = tokens_in.shape
    seq_parts = lax.axis_size("seq")
    length_all = row_count * seq_parts
    piece_rows = row_count // 2
    key_block = min(length_all, 512)
    total_rows = groups * row_count
    offsets = jnp.arange(piece_rows, dtype=jnp.int32)
    positions = (stretch_order[:, :, None] * piece_rows + offsets[None, None, :]).reshape(
        groups, length_all
    )
    local_pos = lax.dynamic_slice_in_dim(positions, lax.axis_index("seq") * row_count, row_count, 1)
    live_rows = (local_pos < seq_lengths[:, None]).astype(jnp.float32).reshape(total_rows, 1)
    outputs = fsdp_layer(
        tokens_in, grad_out, seq_lengths, shards, positions, local_pos, live_rows, key_block, gate_w
    )
    return outputs


def solution(mesh):
    return jax.shard_map(
        body,
        mesh=mesh,
        in_specs=(
            P("dp", "seq", None),
            P("dp", "seq", None),
            P("dp"),
            P("dp", None),
            P(("dp", "seq")),
            P(("dp", "seq"), None),
            P(("dp", "seq"), None),
            P(("dp", "seq"), None),
            P(("dp", "seq"), None),
            P(("dp", "seq")),
            P(("dp", "seq"), None),
            P(("dp", "seq"), None),
            P(("dp", "seq"), None),
        ),
        out_specs=(
            P("dp", "seq", None),
            P("dp", "seq", None),
            P(("dp", "seq")),
            P(("dp", "seq"), None),
            P(("dp", "seq"), None),
            P(("dp", "seq"), None),
            P(("dp", "seq"), None),
            P(("dp", "seq")),
            P(("dp", "seq"), None),
            P(("dp", "seq"), None),
            P(("dp", "seq"), None),
        ),
        check_vma=False,
    )
```

profile of v0, /device:TPU:0, one launch (start us, length us, event | category | flops | bytes accessed | tf_op | source)
XLA Modules:
  0.0 4158.0 jit_solution(843973192059612948)
XLA Ops:
  10.4 42.1 %all-reduce.5 = (bf16[2048]{0:T(1024)(128)(2,1)S(1)}, bf16[2048]{0:T(1024)(128)(2,1)S(1)}) all-reduce(bf16[2048]{0:T(1024)(128)(2,1)S(1)} %dynamic-update-slice, bf16[2048]{0:T(1024)(128)(2,1)S(1)} %dynamic-update-slice.1), channel_id=1, replica_groups=mesh['dp'=8,'seq'=4] {'dp','seq'}, use_global_device_ids=true, to_apply=%add | all-reduce | flops 4096 | bytes 16384
  76.3 51.9 %all-gather.13.cloned.1.call-done = bf16[2048,512]{1,0:T(8,128)(2,1)} async-done(((bf16[64,512]{1,0:T(8,128)(2,1)}), bf16[2048,512]{1,0:T(8,128)(2,1)}) %all-gather.13.cloned.1.call-update) | async-done | bytes 2097168 | tf_op jit(solution)/shard_map/all_gather | solution.py:179
  210.1 72.5 %all-gather.17.cloned.1.call-done = bf16[2048,2048]{1,0:T(8,128)(2,1)} async-done(((bf16[64,2048]{1,0:T(8,128)(2,1)}), bf16[2048,2048]{1,0:T(8,128)(2,1)}) %all-gather.17.cloned.1.call-update) | async-done | bytes 8388624 | tf_op jit(solution)/shard_map/all_gather | solution.py:178
  304.3 124.7 %while.39 = (s32[]{:T(128)}, f32[8,4,512]{2,1,0:T(4,128)S(1)}, f32[8,4,512]{2,1,0:T(4,128)S(1)}, s32[4,512]{1,0:T(4,128)S(1)}, s32[1,512]{1,0:T(1,128)S(1)}, /*i...) while((s32[]{:T(128)}, f32[8,4,512]{2,1,0:T(4,128)S(1)}, ...), condition=%wide.region_4.5_spmd.clone, body=%wide.region_1.4_spmd.clone.sunk | while | flops 1133068800 | bytes 71378048 | solution.py:90
  429.0 62.4 %while.40 = (s32[]{:T(128)}, f32[512,8,4,64]{0,3,2,1:T(8,128)}, bf16[4,512,8,64]{1,3,2,0:T(8,128)(2,1)}, s32[4,512]{1,0:T(4,128)S(1)}, s32[1,512]{1,0:T(1,128)S(...) while((s32[]{:T(128)}, f32[512,8,4,64]{0,3,2,1:T(8,128)}, ...), condition=%wide.region_6.7_spmd.clone, body=%wide.region_5.6_spmd.clone.sunk | while | flops 2183660032 | bytes 12135046 | solution.py:105
  505.9 51.9 %all-gather.23.cloned.1.call-done = bf16[2048,8192]{1,0:T(8,128)(2,1)} async-done(((bf16[64,8192]{1,0:T(8,128)(2,1)}), bf16[2048,8192]{1,0:T(8,128)(2,1)}) %all-gather.23.cloned.1.call-update) | async-done | bytes 33554448 | tf_op jit(solution)/shard_map/all_gather | solution.py:184
  557.8 26.7 fusion.110
  584.5 169.1 %all-gather.21.cloned.1.call-done = bf16[2048,8192]{1,0:T(8,128)(2,1)} async-done(((bf16[64,8192]{1,0:T(8,128)(2,1)}), bf16[2048,8192]{1,0:T(8,128)(2,1)}) %all-gather.21.cloned.1.call-update) | async-done | bytes 33554448 | tf_op jit(solution)/shard_map/all_gather | solution.py:183
  753.6 26.8 fusion.109
  780.5 169.0 %all-gather.25.cloned.1.call-done = bf16[2048,8192]{1,0:T(8,128)(2,1)} async-done(((bf16[64,8192]{1,0:T(8,128)(2,1)}), bf16[2048,8192]{1,0:T(8,128)(2,1)}) %all-gather.25.cloned.1.call-update) | async-done | bytes 33554448 | tf_op jit(solution)/shard_map/all_gather | solution.py:185
  949.5 38.5 multiply_convert_fusion
  988.0 29.3 fusion.115
  1042.5 27.0 multiply_reduce_fusion
  1090.1 260.3 %while.41 = (s32[]{:T(128)}, f32[512,8,4,64]{0,3,2,1:T(8,128)}, bf16[4,512,8,64]{1,3,2,0:T(8,128)(2,1)}, bf16[4,512,8,64]{1,3,2,0:T(8,128)(2,1)}, bf16[4,512,8,6...) while((s32[]{:T(128)}, f32[512,8,4,64]{0,3,2,1:T(8,128)}, ...), condition=%wide.region_10.11_spmd.clone, body=%wide.region_9.10_spmd.clone.sunk | while | flops 5456527872 | bytes 172434608 | solution.py:161
  1362.5 32.0 fusion.97
  1394.5 29.1 fusion.114
  1423.7 130.8 %pad_maximum_fusion = f32[2048,24576]{1,0:T(8,128)} fusion(f32[2048,8192]{1,0:T(8,128)} %fusion.97, f32[2048,8192]{1,0:T(8,128)} %fusion.115, f32[2048,8192]{1,0:T(8,128)} %fusion.114), kind=kLoop, calls=%fused_computation.62 | loop fusion | flops 100663296 | bytes 402653184 | tf_op jit(solution)/shard_map/concatenate | solution.py:282
  1615.2 29.3 fusion.76
  1654.8 39.5 all-reduce.4
  1704.0 1441.3 %reduce-scatter.20.cloned.1.call-done = f32[64,24576]{1,0:T(8,128)} async-done(((f32[2048,24576]{1,0:T(8,128)}), f32[64,24576]{1,0:T(8,128)}) %reduce-scatter.20.cloned.1.call-update) | async-done | bytes 6291472 | tf_op jit(solution)/shard_map/reduce_scatter | solution.py:281
  3151.1 137.9 %reduce-scatter.16.cloned.1.call-done = f32[64,512]{1,0:T(8,128)} async-done(((f32[2048,512]{1,0:T(8,128)}), f32[64,512]{1,0:T(8,128)}) %reduce-scatter.16.cloned.1.call-update) | async-done | bytes 131088 | tf_op jit(solution)/shard_map/reduce_scatter | solution.py:364
  3289.0 142.2 %reduce-scatter.14.cloned.1.call-done = f32[64,512]{1,0:T(8,128)} async-done(((f32[2048,512]{1,0:T(8,128)}), f32[64,512]{1,0:T(8,128)}) %reduce-scatter.14.cloned.1.call-update) | async-done | bytes 131088 | tf_op jit(solution)/shard_map/reduce_scatter | solution.py:363
  3431.2 358.3 %reduce-scatter.18.cloned.1.call-done = f32[64,2048]{1,0:T(8,128)} async-done(((f32[2048,2048]{1,0:T(8,128)}), f32[64,2048]{1,0:T(8,128)}) %reduce-scatter.18.cloned.1.call-update) | async-done | bytes 524304 | tf_op jit(solution)/shard_map/reduce_scatter | solution.py:365
  3789.5 361.8 %reduce-scatter.12.cloned.1.call-done = f32[64,2048]{1,0:T(8,128)} async-done(((f32[2048,2048]{1,0:T(8,128)}), f32[64,2048]{1,0:T(8,128)}) %reduce-scatter.12.cloned.1.call-update) | async-done | bytes 524304 | tf_op jit(solution)/shard_map/reduce_scatter | solution.py:362
  (249 shorter events, 733.9 us)
Async XLA Ops:
  7.2 62.9 %all-gather.11.cloned.1.call-start = ((), (), s32[]{:S(2)}) async-start(), calls=%async_computation.7 | async-start | bytes 2162688 | tf_op jit(solution)/shard_map/all_gather | solution.py:180
  7.9 120.3 %all-gather.13.cloned.1.call-start = ((), (), s32[]{:S(2)}) async-start(), calls=%async_computation.8 | async-start | bytes 2162688 | tf_op jit(solution)/shard_map/all_gather | solution.py:179
  8.7 156.2 %all-gather.27.cloned.1.call-start = ((), (), s32[]{:S(2)}) async-start(), calls=%async_computation.22 | async-start | bytes 2621440 | tf_op jit(solution)/shard_map/all_gather | solution.py:221
  52.6 242.3 %copy-start.20 = (f32[2048]{0:T(1024)}, f32[2048]{0:T(1024)S(1)}, u32[]{:S(2)}) copy-start(f32[2048]{0:T(1024)S(1)} %convert_element_type.174) | copy-start | bytes 24580
  54.7 240.3 %copy-start.25 = (f32[512]{0:T(512)}, f32[512]{0:T(512)S(1)}, u32[]{:S(2)}) copy-start(f32[512]{0:T(512)S(1)} %add_rsqrt_fusion.1) | copy-start | bytes 6148
  74.3 57.8 %copy-start = (bf16[1,512,2048]{2,1,0:T(8,128)(2,1)S(1)}, bf16[1,512,2048]{2,1,0:T(8,128)(2,1)}, u32[]{:S(2)}) copy-start(bf16[1,512,2048]{2,1,0:T(8,128)(2,1)} %param.19) | copy-start | bytes 6291460
  74.4 127.9 %all-gather.15.cloned.1.call-start = ((), (), s32[]{:S(2)}) async-start(), calls=%async_computation.9 | async-start | bytes 2621440 | tf_op jit(solution)/shard_map/all_gather | solution.py:220
  76.3 225.8 %copy-start.13 = (f32[512,32]{0,1:T(8,128)}, f32[512,32]{0,1:T(8,128)S(1)}, u32[]{:S(2)}) copy-start(f32[512,32]{0,1:T(8,128)S(1)} %get-tuple-element.449) | copy-start | bytes 196612
  76.3 225.8 %copy-start.15 = (f32[512,32]{0,1:T(8,128)}, f32[512,32]{0,1:T(8,128)S(1)}, u32[]{:S(2)}) copy-start(f32[512,32]{0,1:T(8,128)S(1)} %get-tuple-element.450) | copy-start | bytes 196612
  136.1 146.5 %all-gather.17.cloned.1.call-start = ((), (), s32[]{:S(2)}) async-start(), calls=%async_computation.10 | async-start | bytes 8650752 | tf_op jit(solution)/shard_map/all_gather | solution.py:178
  136.7 358.8 %all-gather.19.cloned.1.call-start = ((), (), s32[]{:S(2)}) async-start(), calls=%async_computation.11 | async-start | bytes 8650752 | tf_op jit(solution)/shard_map/all_gather | solution.py:181
  137.2 420.5 %all-gather.23.cloned.1.call-start = ((), (), s32[]{:S(2)}) async-start(), calls=%async_computation.13 | async-start | bytes 34603008 | tf_op jit(solution)/shard_map/all_gather | solution.py:184
  138.0 615.7 %all-gather.21.cloned.1.call-start = ((), (), s32[]{:S(2)}) async-start(), calls=%async_computation.12 | async-start | bytes 34603008 | tf_op jit(solution)/shard_map/all_gather | solution.py:183
  138.7 810.8 %all-gather.25.cloned.1.call-start = ((), (), s32[]{:S(2)}) async-start(), calls=%async_computation.14 | async-start | bytes 34603008 | tf_op jit(solution)/shard_map/all_gather | solution.py:185
  139.5 1415.3 %reduce-scatter.10.cloned.1.call-start = ((), (), s32[]{:S(2)}) async-start(), calls=%async_computation.16 | async-start | bytes 2621440 | tf_op jit(solution)/shard_map/reduce_scatter | solution.py:328
  505.9 482.1 %copy-start.3 = (bf16[512,2048]{1,0:T(8,128)(2,1)}, bf16[512,2048]{1,0:T(8,128)(2,1)S(1)}, u32[]{:S(2)}) copy-start(bf16[512,2048]{1,0:T(8,128)(2,1)S(1)} %multiply_convert_fusion.4) | copy-start | bytes 6291460
  584.5 365.0 %copy-start.17 = (f32[1,512]{1,0:T(1,128)S(1)}, f32[1,512]{1,0:T(1,128)}, u32[]{:S(2)}) copy-start(f32[1,512]{1,0:T(1,128)} %get-tuple-element.431) | copy-start | bytes 6148
  1356.4 204.4 %reduce-scatter.8.cloned.1.call-start = ((), (), s32[]{:S(2)}) async-start(), calls=%async_computation.15 | async-start | bytes 2621440 | tf_op jit(solution)/shard_map/reduce_scatter | solution.py:325
  1362.5 32.0 copy-start.4
  1423.6 1721.8 %reduce-scatter.20.cloned.1.call-start = ((), (), s32[]{:S(2)}) async-start(), calls=%async_computation.21 | async-start | bytes 207618048 | tf_op jit(solution)/shard_map/reduce_scatter | solution.py:281
  1554.5 1734.4 %reduce-scatter.16.cloned.1.call-start = ((), (), s32[]{:S(2)}) async-start(), calls=%async_computation.19 | async-start | bytes 4325376 | tf_op jit(solution)/shard_map/reduce_scatter | solution.py:364
  1560.8 1870.4 %reduce-scatter.14.cloned.1.call-start = ((), (), s32[]{:S(2)}) async-start(), calls=%async_computation.18 | async-start | bytes 4325376 | tf_op jit(solution)/shard_map/reduce_scatter | solution.py:363
  1566.3 2223.2 %reduce-scatter.18.cloned.1.call-start = ((), (), s32[]{:S(2)}) async-start(), calls=%async_computation.20 | async-start | bytes 17301504 | tf_op jit(solution)/shard_map/reduce_scatter | solution.py:365
  1584.6 2566.6 %reduce-scatter.12.cloned.1.call-start = ((), (), s32[]{:S(2)}) async-start(), calls=%async_computation.17 | async-start | bytes 17301504 | tf_op jit(solution)/shard_map/reduce_scatter | solution.py:362
  (27 other events, 220.3 us)
Sparse Core Ops, SparseCore 0:
  10.9 59.1 all-gather.10
  72.9 55.2 all-gather.12
  130.6 34.1 all-gather.26
  167.1 35.1 all-gather.14
  205.0 77.5 all-gather.16
  285.3 76.1 all-gather.18
  364.4 193.3 all-gather.22
  560.7 192.9 all-gather.20
  756.5 192.9 all-gather.24
  1356.5 33.3 reduce-scatter.9
  1423.8 33.6 reduce-scatter.7
  1554.7 1590.6 reduce-scatter.19
  3148.2 140.6 reduce-scatter.15
  3291.7 139.4 reduce-scatter.13
  3433.9 355.5 reduce-scatter.17
  3792.2 358.9 reduce-scatter.11
where the time goes:
time: 4160 us
  waiting for transfers between devices  3030 us (73%)
  matrix products  726 us (17%)
  other arithmetic  238 us (6%)
  blocking collectives  81.6 us (2%)
  local copies, waits for them, and re-layouts  67.9 us (2%)
    reduce_scatter x1, waiting for transfers between devices, fsdp_layer(): lax.psum_scatter(jnp.concatenate([jnp.einsum('tc,tf->cf', normed_two, gra...  1440 us
    reduce_scatter x1, waiting for transfers between devices, fsdp_layer(): lax.psum_scatter(query_grad, ('dp', 'seq'), scatter_dimension=0, tiled=True)  362 us
    reduce_scatter x1, waiting for transfers between devices, fsdp_layer(): lax.psum_scatter(output_grad, ('dp', 'seq'), scatter_dimension=0, tiled=T...  358 us
    all_gather x1, waiting for transfers between devices, fsdp_layer(): lax.all_gather(shards[6], ('dp', 'seq'), axis=0, tiled=True)  169 us
    all_gather x1, waiting for transfers between devices, fsdp_layer(): lax.all_gather(shards[8], ('dp', 'seq'), axis=0, tiled=True)  169 us
    reduce_scatter x1, waiting for transfers between devices, fsdp_layer(): lax.psum_scatter(key_grad, ('dp', 'seq'), scatter_dimension=0, tiled=True)  142 us
    reduce_scatter x1, waiting for transfers between devices, fsdp_layer(): lax.psum_scatter(value_grad, ('dp', 'seq'), scatter_dimension=0, tiled=True)  138 us
    concatenate x1, other arithmetic, fsdp_layer(): jnp.concatenate([jnp.einsum('tc,tf->cf', normed_two, grad_gate, preferred...  131 us
  transfers between devices with their start and end apart: 16, of which 13 were waited for; matrix products, arithmetic and copies ran while one was open for 15% of the time, Pallas kernels for 0%

commit v1 on v0

v1 whole, which is shorter than its diff:
```python
import functools
import math

import jax
import jax.numpy as jnp
from jax import lax
from jax.experimental import pallas as pl
from jax.experimental.pallas import tpu as pltpu
from jax.sharding import Mesh
from jax.sharding import PartitionSpec as P

HEADS = 32
KVH = 8
HD = 64
REP = HEADS // KVH

epsilon = 1e-05
masked_score = -1e30
floor_score = -1e29

bf16 = jnp.bfloat16
f32 = jnp.float32


def frequencies():
    steps_even = jnp.arange(0, HD, 2).astype(f32) / HD
    base_freq = 1.0 / 500000.0**steps_even
    wavelength = 2.0 * math.pi / base_freq
    smooth = (8192.0 / wavelength - 1.0) / 3.0
    blended = (1.0 - smooth) * base_freq / 32.0 + smooth * base_freq
    return jnp.where(
        wavelength < 2048.0, base_freq, jnp.where(wavelength > 8192.0, base_freq / 32.0, blended)
    )


def shift(value, axis, steps):
    size = lax.axis_size(axis)
    return lax.ppermute(value, axis, [(i, (i + steps) % size) for i in range(size)])


def in_order(own, other, index, axis):
    return jnp.where(
        index == 0,
        jnp.concatenate([own, other], axis=axis),
        jnp.concatenate([other, own], axis=axis),
    )


def halves(value, index, axis):
    size = value.shape[axis] // 2
    return (
        lax.dynamic_slice_in_dim(value, index * size, size, axis),
        lax.dynamic_slice_in_dim(value, (1 - index) * size, size, axis),
    )


def spread_columns(shard, c, x, earlier=(), later=()):
    own, other = halves(shard, x, 1)
    if earlier:
        other = hold(other, *earlier)
    both = in_order(own, after(shift(other, "x", 1), *later), x, 0)
    own, other = halves(both, c, 1)
    return in_order(own, shift(other, "c", 1), c, 0)


def join_columns(unit, c, x):
    own, other = halves(unit, c, 0)
    both = in_order(own, shift(other, "c", 1), c, 1)
    own, other = halves(both, x, 0)
    return in_order(own, shift(other, "x", 1), x, 1)


def after(value, *others):
    return lax.optimization_barrier((value,) + others)[0]


def hold_body(*refs):
    del refs


def hold(value, *others):
    return pl.pallas_call(
        hold_body,
        in_specs=[pl.BlockSpec(memory_space=pl.ANY)] * (1 + len(others)),
        out_specs=pl.BlockSpec(memory_space=pl.ANY),
        out_shape=jax.ShapeDtypeStruct(value.shape, value.dtype),
        input_output_aliases={0: 0},
        name="hold",
    )(value, *others)


def gather_column(unit):
    return lax.all_gather(unit, "z", axis=0, tiled=True)


def gather_slots(column):
    return [column] + [shift(column, "y", k) for k in range(1, lax.axis_size("y"))]


def send_slots(terms):
    return [shift(term, "y", -(k + 1)) for k, term in enumerate(terms)]


def gather_whole(unit, y):
    zs, ys = lax.axis_size("z"), lax.axis_size("y")
    size = zs * unit.shape[0]
    whole = lax.all_gather(unit, ("y", "z"), axis=0, tiled=True)
    return [lax.dynamic_slice_in_dim(whole, ((y - k) % ys) * size, size, 0) for k in range(ys)]


def scatter_whole(terms):
    return lax.psum_scatter(terms, ("y", "z"), scatter_dimension=0, tiled=True)


def scatter_column(total):
    return lax.psum_scatter(total, "z", scatter_dimension=0, tiled=True)


def gather_gains(unit):
    zs, ys = lax.axis_size("z"), lax.axis_size("y")
    row = jnp.stack([unit] + [shift(unit, "y", k) for k in range(1, ys)], axis=1)
    z = lax.axis_index("z")
    out = jnp.zeros((2, ys, zs, unit.shape[1]), unit.dtype)
    for j in range(zs):
        got = row if j == 0 else shift(row, "z", j)
        out = lax.dynamic_update_slice(out, got[:, :, None], (0, 0, (z - j) % zs, 0))
    return out.reshape(2, -1)


def scatter_gains(terms, unit):
    zs, ys = lax.axis_size("z"), lax.axis_size("y")
    z = lax.axis_index("z")
    terms = terms.reshape(ys, zs * unit)
    total = terms[0]
    for k in range(1, ys):
        total = total + shift(terms[k], "y", -k)
    total = total.reshape(zs, unit)
    out = lax.dynamic_index_in_dim(total, z, 0, keepdims=False)
    for j in range(1, zs):
        out = out + shift(lax.dynamic_index_in_dim(total, (z - j) % zs, 0, keepdims=False), "z", -j)
    return out


def gather_tokens(own, *others):
    beside = after(shift(own, "x", 1), *others)
    sibling = shift(own, "c", 1)
    return jnp.concatenate([own, beside, sibling, shift(beside, "c", 1)], axis=0)


def scatter_tokens(partials):
    sums = []
    for partial in partials:
        count = partial.shape[0] // 4
        half = partial[: 2 * count].astype(f32) + shift(partial[2 * count :], "c", 1).astype(f32)
        sums.append(half[:count] + shift(half[count:].astype(bf16), "x", 1).astype(f32))
    return jnp.concatenate(sums, axis=1)


def move_columns_body(zs, ys, forth, y_ref, in_ref, out_ref):
    block = in_ref.shape[1] // (zs * 2 * ys)
    y = y_ref[0]
    for i in range(zs * 2):
        for k in range(ys):
            natural = i * ys + lax.rem(y - k + ys, ys)
            natural = pl.ds(pl.multiple_of(natural * block, block), block)
            slot = pl.ds((k * zs * 2 + i) * block, block)
            if forth:
                out_ref[:, slot] = in_ref[:, natural]
            else:
                out_ref[:, natural] = in_ref[:, slot]


def move_columns(value, y, zs, ys, forth):
    rows, width = value.shape
    tall = rows // 4
    spec = pl.BlockSpec((tall, width), lambda i, *_: (i, 0))
    return pl.pallas_call(
        functools.partial(move_columns_body, zs, ys, forth),
        grid_spec=pltpu.PrefetchScalarGridSpec(
            num_scalar_prefetch=1, grid=(4,), in_specs=[spec], out_specs=spec
        ),
        out_shape=jax.ShapeDtypeStruct(value.shape, value.dtype),
        cost_estimate=pl.CostEstimate(
            flops=0, bytes_accessed=2 * value.size * value.dtype.itemsize, transcendentals=0
        ),
        name="move_columns",
    )(y, value)


VMEM_BYTES = 56 * 1024 * 1024
EASE = 1


def estimate(flops, moved, exps=0):
    return pl.CostEstimate(
        flops=int(flops) // EASE, bytes_accessed=int(moved) // EASE, transcendentals=int(exps) // EASE
    )


def fit(size, most):
    return size if size <= most else fit(size // 2, most)


def rows_product(left, parts, extras, finish, n_out, name):
    t, d = left.shape
    n = parts[0].shape[1]
    depth = parts[0].shape[0]
    bm, bn = fit(t, 512), fit(n, 1024)
    n_parts, n_extra = len(parts), len(extras)

    def kernel(*refs):
        left_ref = refs[0]
        product = None
        for p in range(n_parts):
            term = jnp.dot(
                left_ref[:, p * depth : (p + 1) * depth], refs[1 + p][...], preferred_element_type=f32
            )
            product = term if product is None else product + term
        got = finish(product, *(r[...] for r in refs[1 + n_parts : 1 + n_parts + n_extra]))
        for ref, value in zip(refs[1 + n_parts + n_extra :], got):
            ref[...] = value.astype(bf16)

    tile = pl.BlockSpec((bm, bn), lambda j, i: (i, j))
    return pl.pallas_call(
        kernel,
        grid=(n // bn, t // bm),
        in_specs=[pl.BlockSpec((bm, d), lambda j, i: (i, 0))]
        + [pl.BlockSpec((depth, bn), lambda j, i: (0, j))] * n_parts
        + [tile] * n_extra,
        out_specs=[tile] * n_out,
        out_shape=[jax.ShapeDtypeStruct((t, n), bf16)] * n_out,
        compiler_params=pltpu.CompilerParams(vmem_limit_bytes=VMEM_BYTES),
        cost_estimate=estimate(2 * t * d * n, 2 * (t * d + d * n + t * n)),
        name=name,
    )(left, *parts, *extras)


def turned_product(lefts, rights, name):
    t, f = lefts[0].shape
    n = rights[0].shape[0]
    bm, bn = fit(t, 512), fit(n, 1024)
    count = len(lefts)

    def kernel(*refs):
        product = None
        for p in range(count):
            term = lax.dot_general(
                refs[p][...], refs[count + p][...], (((1,), (1,)), ((), ())), preferred_element_type=f32
            )
            product = term if product is None else product + term
        refs[2 * count][...] = product.astype(bf16)

    return pl.pallas_call(
        kernel,
        grid=(n // bn, t // bm),
        in_specs=[pl.BlockSpec((bm, f), lambda j, i: (i, 0))] * count
        + [pl.BlockSpec((bn, f), lambda j, i: (j, 0))] * count,
        out_specs=pl.BlockSpec((bm, bn), lambda j, i: (i, j)),
        out_shape=jax.ShapeDtypeStruct((t, n), bf16),
        compiler_params=pltpu.CompilerParams(vmem_limit_bytes=VMEM_BYTES),
        cost_estimate=estimate(2 * count * t * f * n, 2 * count * (t * f + f * n)),
        name=name,
    )(*lefts, *rights)


def columns_product(left, slots, n_parts, right, others, name):
    t, d = left.shape
    m = d // n_parts
    f = right.shape[1]
    bm, bn = fit(m, 512), fit(f, 1024)
    per = m // bm
    count = len(others)

    def kernel(slots_ref, left_ref, right_ref, *refs):
        turned_ref = refs[-1]

        @pl.when(pl.program_id(1) == 0)
        def _():
            turned_ref[...] = left_ref[...].T

        product = jnp.dot(turned_ref[...], right_ref[...], preferred_element_type=f32)
        for ref in refs[:count]:
            product = product + ref[...].astype(f32)
        refs[count][...] = product.astype(bf16)

    rows = slots.shape[0] * m
    tile = pl.BlockSpec((bm, bn), lambda i, j, slots_ref: (i, j))
    return pl.pallas_call(
        kernel,
        grid_spec=pltpu.PrefetchScalarGridSpec(
            num_scalar_prefetch=1,
            grid=(rows // bm, f // bn),
            in_specs=[
                pl.BlockSpec((t, bm), lambda i, j, slots_ref: (0, slots_ref[i // per] * per + i % per)),
                pl.BlockSpec((t, bn), lambda i, j, slots_ref: (0, j)),
            ]
            + [tile] * count,
            out_specs=tile,
            scratch_shapes=[pltpu.VMEM((bm, t), bf16)],
        ),
        out_shape=jax.ShapeDtypeStruct((rows, f), bf16),
        compiler_params=pltpu.CompilerParams(vmem_limit_bytes=VMEM_BYTES),
        cost_estimate=estimate(2 * t * rows * f, 2 * (t * m + t * f + rows * f)),
        name=name,
    )(slots, left, right, *others)


def plain(product):
    return (product,)


def up_finish(product, gate):
    gate = gate.astype(f32)
    return product, gate * jax.nn.sigmoid(gate) * product


def hidden_back(grad, gate, up):
    gate, up = gate.astype(f32), up.astype(f32)
    sigmoid = jax.nn.sigmoid(gate)
    return grad * up * sigmoid * (1.0 + gate * (1.0 - sigmoid)), grad * gate * sigmoid


def attention_fwd_body(
    chunk, blocks, qpos_ref, kpos_ref, len_ref, q_ref, k_ref, v_ref, o_ref, lse_ref,
    kn_ref, m_ref, l_ref, acc_ref,
):
    s, qb = pl.program_id(0), pl.program_id(2)
    ys = k_ref.shape[0]

    @pl.when(qb == 0)
    def _():
        for yk in range(ys):
            for b in range(blocks):
                kn_ref[pl.ds((yk * blocks + b) * chunk, chunk), :] = (
                    k_ref[yk, :, pl.ds(b * chunk, chunk)].astype(f32).T.astype(bf16)
                )

    qp = qpos_ref[s, qb]
    length = len_ref[s]
    m_ref[...] = jnp.full_like(m_ref, floor_score)
    l_ref[...] = jnp.zeros_like(l_ref)
    acc_ref[...] = jnp.zeros_like(acc_ref)

    for yk in range(ys):

        def step(b, carry, yk=yk):
            kp = kpos_ref[s, yk * blocks + b]
            first = kp * chunk
            live = (kp <= qp) & (first < length)
            partly = (kp == qp) | (first + chunk > length)

            def work(masked):
                kn = kn_ref[pl.ds(pl.multiple_of((yk * blocks + b) * chunk, chunk), chunk), :]
                vt = v_ref[yk, :, pl.ds(pl.multiple_of(b * chunk, chunk), chunk)]
                if masked:
                    at_key = first + lax.broadcasted_iota(jnp.int32, (chunk, chunk), 0)
                    at_query = qp * chunk + lax.broadcasted_iota(jnp.int32, (chunk, chunk), 1)
                    allowed = (at_key <= at_query) & (at_key < length)
                for h in range(REP):
                    rows = slice(h * HD, (h + 1) * HD)
                    scores = jnp.dot(kn, q_ref[rows, :], preferred_element_type=f32)
                    if masked:
                        scores = jnp.where(allowed, scores, masked_score)
                    m_old = m_ref[h : h + 1, :]
                    m_new = jnp.maximum(m_old, jnp.max(scores, axis=0, keepdims=True))
                    alpha = jnp.exp(m_old - m_new)
                    probs = jnp.exp(scores - m_new)
                    m_ref[h : h + 1, :] = m_new
                    l_ref[h : h + 1, :] = l_ref[h : h + 1, :] * alpha + jnp.sum(
                        probs, axis=0, keepdims=True
                    )
                    acc_ref[rows, :] = acc_ref[rows, :] * alpha + jnp.dot(
                        vt, probs.astype(bf16), preferred_element_type=f32
                    )

            pl.when(live & partly)(lambda: work(True))
            pl.when(live & jnp.logical_not(partly))(lambda: work(False))
            return carry

        lax.fori_loop(0, blocks, step, 0)

    for h in range(REP):
        rows = slice(h * HD, (h + 1) * HD)
        o_ref[rows, :] = (acc_ref[rows, :] / l_ref[h : h + 1, :]).astype(bf16)
    lse_ref[0] = m_ref[0:REP, :] + jnp.log(l_ref[0:REP, :])


def attention_fwd(queries, keys, values, qpos, kpos, lengths, chunk):
    tokens = queries.shape[1]
    groups = queries.shape[0] // (REP * HD)
    ys = keys.shape[0]
    half = tokens // 2
    blocks = half // chunk
    grid = (2, groups, blocks)
    q_spec = pl.BlockSpec((REP * HD, chunk), lambda s, g, b, *_: (g, s * blocks + b))
    kv_spec = pl.BlockSpec((ys, HD, half), lambda s, g, b, *_: (0, g, s))
    lse_spec = pl.BlockSpec((1, REP, chunk), lambda s, g, b, *_: (g, 0, s * blocks + b))
    pairs = 2 * groups * blocks * blocks * ys
    return pl.pallas_call(
        functools.partial(attention_fwd_body, chunk, blocks),
        grid_spec=pltpu.PrefetchScalarGridSpec(
            num_scalar_prefetch=3,
            grid=grid,
            in_specs=[q_spec, kv_spec, kv_spec],
            out_specs=[q_spec, lse_spec],
            scratch_shapes=[
                pltpu.VMEM((ys * half, HD), bf16),
                pltpu.VMEM((8, chunk), f32),
                pltpu.VMEM((8, chunk), f32),
                pltpu.VMEM((REP * HD, chunk), f32),
            ],
        ),
        out_shape=[
            jax.ShapeDtypeStruct(queries.shape, bf16),
            jax.ShapeDtypeStruct((groups, REP, tokens), f32),
        ],
        cost_estimate=estimate(
            pairs * REP * chunk * chunk * HD * 4 * 2,
            queries.size * 4 + keys.size * 4,
            pairs * REP * chunk * chunk,
        ),
        name="attention_forward",
    )(qpos, kpos, lengths, queries, keys, values)


def attention_bwd_body(
    chunk, blocks, qpos_ref, kpos_ref, len_ref, q_ref, k_ref, v_ref, o_ref, do_ref, lse_ref,
    dq_ref, dk_ref, dv_ref, kn_ref, vn_ref, dqa_ref, dka_ref, dva_ref, delta_ref,
):
    s, qb = pl.program_id(0), pl.program_id(2)
    ys = k_ref.shape[0]

    @pl.when(qb == 0)
    def _():
        dka_ref[...] = jnp.zeros_like(dka_ref)
        dva_ref[...] = jnp.zeros_like(dva_ref)
        for yk in range(ys):
            for b in range(blocks):
                rows = pl.ds((yk * blocks + b) * chunk, chunk)
                cols = pl.ds(b * chunk, chunk)
                kn_ref[rows, :] = k_ref[yk, :, cols].astype(f32).T.astype(bf16)
                vn_ref[rows, :] = v_ref[yk, :, cols].astype(f32).T.astype(bf16)

    qp = qpos_ref[s, qb]
    length = len_ref[s]
    dqa_ref[...] = jnp.zeros_like(dqa_ref)
    for h in range(REP):
        rows = slice(h * HD, (h + 1) * HD)
        delta_ref[h : h + 1, :] = jnp.sum(
            do_ref[rows, :].astype(f32) * o_ref[rows, :].astype(f32), axis=0, keepdims=True
        )

    for yk in range(ys):

        def step(b, carry, yk=yk):
            kp = kpos_ref[s, yk * blocks + b]
            first = kp * chunk
            live = (kp <= qp) & (first < length)
            partly = (kp == qp) | (first + chunk > length)

            def work(masked):
                at = pl.ds(pl.multiple_of((yk * blocks + b) * chunk, chunk), chunk)
                cols = pl.ds(pl.multiple_of(b * chunk, chunk), chunk)
                kn, vn = kn_ref[at, :], vn_ref[at, :]
                kt = k_ref[yk, :, cols]
                if masked:
                    at_key = first + lax.broadcasted_iota(jnp.int32, (chunk, chunk), 0)
                    at_query = qp * chunk + lax.broadcasted_iota(jnp.int32, (chunk, chunk), 1)
                    allowed = (at_key <= at_query) & (at_key < length)
                dk = dka_ref[yk, :, cols]
                dv = dva_ref[yk, :, cols]
                for h in range(REP):
                    rows = slice(h * HD, (h + 1) * HD)
                    qt, dot = q_ref[rows, :], do_ref[rows, :]
                    scores = jnp.dot(kn, qt, preferred_element_type=f32)
                    if masked:
                        scores = jnp.where(allowed, scores, masked_score)
                    probs = jnp.exp(scores - lse_ref[0, h : h + 1, :])
                    grad_probs = jnp.dot(vn, dot, preferred_element_type=f32)
                    grad_scores = (probs * (grad_probs - delta_ref[h : h + 1, :])).astype(bf16)
                    dqa_ref[rows, :] += jnp.dot(kt, grad_scores, preferred_element_type=f32)
                    dk += lax.dot_general(
                        qt, grad_scores, (((1,), (1,)), ((), ())), preferred_element_type=f32
                    )
                    dv += lax.dot_general(
                        dot, probs.astype(bf16), (((1,), (1,)), ((), ())),
                        preferred_element_type=f32,
                    )
                dka_ref[yk, :, cols] = dk
                dva_ref[yk, :, cols] = dv

            pl.when(live & partly)(lambda: work(True))
            pl.when(live & jnp.logical_not(partly))(lambda: work(False))
            return carry

        lax.fori_loop(0, blocks, step, 0)

    dq_ref[...] = dqa_ref[...] * 0.125

    @pl.when(qb == blocks - 1)
    def _():
        dk_ref[...] = dka_ref[...].astype(bf16)
        dv_ref[...] = dva_ref[...].astype(bf16)


def attention_bwd(queries, keys, values, attended, grads, lse, qpos, kpos, lengths, chunk):
    tokens = queries.shape[1]
    groups = queries.shape[0] // (REP * HD)
    ys = keys.shape[0]
    half = tokens // 2
    blocks = half // chunk
    q_spec = pl.BlockSpec((REP * HD, chunk), lambda s, g, b, *_: (g, s * blocks + b))
    kv_spec = pl.BlockSpec((ys, HD, half), lambda s, g, b, *_: (0, g, s))
    lse_spec = pl.BlockSpec((1, REP, chunk), lambda s, g, b, *_: (g, 0, s * blocks + b))
    pairs = 2 * groups * blocks * blocks * ys
    return pl.pallas_call(
        functools.partial(attention_bwd_body, chunk, blocks),
        grid_spec=pltpu.PrefetchScalarGridSpec(
            num_scalar_prefetch=3,
            grid=(2, groups, blocks),
            in_specs=[q_spec, kv_spec, kv_spec, q_spec, q_spec, lse_spec],
            out_specs=[q_spec, kv_spec, kv_spec],
            scratch_shapes=[
                pltpu.VMEM((ys * half, HD), bf16),
                pltpu.VMEM((ys * half, HD), bf16),
                pltpu.VMEM((REP * HD, chunk), f32),
                pltpu.VMEM((ys, HD, half), f32),
                pltpu.VMEM((ys, HD, half), f32),
                pltpu.VMEM((8, chunk), f32),
            ],
        ),
        out_shape=[
            jax.ShapeDtypeStruct(queries.shape, f32),
            jax.ShapeDtypeStruct(keys.shape, bf16),
            jax.ShapeDtypeStruct(keys.shape, bf16),
        ],
        cost_estimate=estimate(
            pairs * REP * chunk * chunk * HD * 10 * 2,
            queries.size * 10 + keys.size * 8,
            pairs * REP * chunk * chunk,
        ),
        name="attention_backward",
    )(qpos, kpos, lengths, queries, keys, values, attended, grads, lse)


def rotate(vectors, cos_table, sin_table, back=False):
    heads = vectors.shape[0] // HD
    halves = vectors.reshape(heads, 2, HD // 2, vectors.shape[1])
    a, b = halves[:, 0], halves[:, 1]
    sin_table = -sin_table if back else sin_table
    turned = jnp.stack([a * cos_table - b * sin_table, b * cos_table + a * sin_table], axis=1)
    return turned.reshape(vectors.shape)


def contract(left, right, left_dim, right_dim):
    return lax.dot_general(
        left, right, (((left_dim,), (right_dim,)), ((), ())), preferred_element_type=f32
    )


def body(
    tokens_in, grad_out, seq_lengths, stretch_order, attn_gain, query_w, key_w, value_w,
    output_w, mlp_gain, gate_w, up_w, down_w,
):
    zs, ys = lax.axis_size("z"), lax.axis_size("y")
    z, c, y, x = (lax.axis_index(name) for name in ("z", "c", "y", "x"))
    rows, width = tokens_in.shape[1:]
    chunk = rows // 2
    unit = width // (zs * ys)

    def to_slots(value):
        if (unit // 2) % 128 == 0:
            return move_columns(value, y[None], zs, ys, True)
        parts = value.reshape(value.shape[0], zs, 2, ys, unit // 2)
        parts = [lax.dynamic_index_in_dim(parts, (y - k) % ys, 3) for k in range(ys)]
        return jnp.concatenate(
            [jnp.transpose(p, (0, 3, 1, 2, 4)).reshape(value.shape[0], width // ys) for p in parts],
            axis=1,
        )

    def from_slots(value):
        if (unit // 2) % 128 == 0:
            return move_columns(value, y[None], zs, ys, False)
        parts = value.reshape(value.shape[0], ys, zs, 2, unit // 2)
        parts = jnp.stack(
            [lax.dynamic_index_in_dim(parts, (y - k) % ys, 1, keepdims=False) for k in range(ys)], axis=3
        )
        return parts.reshape(value.shape[0], width)

    orders = jnp.stack([stretch_order[0], shift(stretch_order[0], "c", 1)])
    lengths = jnp.concatenate([seq_lengths, shift(seq_lengths, "c", 1)])
    slots = [
        2 * (((y - k) % ys) * 2 + (x if i == 0 else 1 - x)) + b
        for k in range(ys)
        for i in range(2)
        for b in range(2)
    ]
    kpos = jnp.stack([lax.dynamic_index_in_dim(orders, s, 1, keepdims=False) for s in slots], axis=1)
    qpos = kpos[:, :4]
    token_pos = (qpos[:, :, None] * chunk + jnp.arange(chunk, dtype=jnp.int32)).reshape(4 * rows)
    own_pos = token_pos[:rows]
    live = (own_pos < seq_lengths[0]).astype(f32)[:, None]
    angles = frequencies()[:, None] * token_pos.astype(f32)[None, :]
    cos_table, sin_table = jnp.cos(angles), jnp.sin(angles)

    gains = jnp.stack([attn_gain, mlp_gain])
    gains = in_order(gains, shift(gains, "x", 1), x, 1)
    gains = in_order(gains, shift(gains, "c", 1), c, 1)
    gains = gather_gains(gains).astype(f32)
    gain_one, gain_two = gains[0:1], gains[1:2]

    inputs = to_slots(tokens_in[0]).astype(f32)
    scale_one = lax.rsqrt(jnp.mean(inputs * inputs, axis=1, keepdims=True) + epsilon)
    unit_one = inputs * scale_one
    normed_own = (unit_one * gain_one).astype(bf16)

    def packed(*weights):
        return jnp.concatenate(
            [w[:, t * (w.shape[1] // 4) : (t + 1) * (w.shape[1] // 4)] for t in range(4) for w in weights],
            axis=1,
        )

    nq, nk = query_w.shape[1] // 4, key_w.shape[1] // 4
    nqkv = nq + 2 * nk
    attn_unit = spread_columns(packed(query_w, key_w, value_w, output_w), c, x)
    qkv_unit, out_unit = attn_unit[:, :nqkv], attn_unit[:, nqkv:]
    mlp_unit = spread_columns(packed(gate_w, up_w, down_w), c, x, (attn_unit,), (normed_own,))
    nf = gate_w.shape[1] // 4
    gate_unit, up_unit, down_unit = (mlp_unit[:, i * nf : (i + 1) * nf] for i in range(3))
    qkv_slots = gather_slots(gather_column(qkv_unit))
    out_column = hold(gather_column(hold(out_unit, qkv_unit)), *qkv_slots[1:])
    qkv_w = jnp.concatenate(qkv_slots, axis=0)
    out_w = jnp.concatenate(gather_slots(out_column), axis=0)
    gate_column = gather_column(hold(gate_unit, out_column))
    up_all, down_all = gather_whole(up_unit, y), gather_whole(down_unit, y)

    normed_one = gather_tokens(normed_own, *qkv_slots[1:])
    pre = contract(after(qkv_w, mlp_unit), normed_one, 0, 1)
    queries = (rotate(pre[:nq], cos_table, sin_table).astype(bf16)) * jnp.asarray(0.125, bf16)
    key_own = rotate(pre[nq : nq + nk], cos_table, sin_table).astype(bf16)
    value_own = pre[nq + nk :].astype(bf16)
    both_own = jnp.concatenate([key_own, value_own], axis=0)
    both = jnp.stack([both_own] + [shift(both_own, "y", k) for k in range(1, ys)])
    keys, values = both[:, :nk], both[:, nk:]
    gate_all = gather_slots(hold(gate_column, both))
    grad_own = to_slots(grad_out[0]) * live.astype(bf16)
    grad_rows = grad_own.astype(f32)
    grad_low = gather_tokens(after(grad_own, normed_one))
    attended, lse = attention_fwd(after(queries, grad_own, gate_all[0]), keys, values, qpos, kpos, lengths, chunk)
    middle = inputs + scatter_tokens([contract(after(attended, grad_low, *gate_all[1:]), out_w, 0, 1).astype(bf16)])
    scale_two = lax.rsqrt(jnp.mean(middle * middle, axis=1, keepdims=True) + epsilon)
    unit_two = middle * scale_two
    normed_two = gather_tokens((unit_two * gain_two).astype(bf16))

    (gate_pre,) = rows_product(normed_two, gate_all, [], plain, 1, "gate")
    up_pre, hidden = rows_product(normed_two, up_all, [gate_pre], up_finish, 2, "up")

    def finish(total):
        return join_columns(total, c, x)

    by_y = (y - jnp.arange(ys, dtype=jnp.int32)) % ys
    last = columns_product(grad_low, by_y, ys, hidden, [], "down_grad")
    down_grad = scatter_whole(last)
    grad_gate, grad_up = rows_product(
        after(grad_low, last), down_all, [gate_pre, up_pre], hidden_back, 2, "hidden_grad"
    )
    last = columns_product(normed_two, by_y, ys, grad_gate, [], "gate_grad")
    gate_grad = scatter_whole(last)
    last = columns_product(after(normed_two, last), by_y, ys, grad_up, [], "up_grad")
    up_grad = scatter_whole(last)
    norm_parts = []
    for g, u in zip(gate_all, up_all):
        last = turned_product([after(grad_gate, last), grad_up], [g, u], "norm_grad")
        norm_parts.append(last)
    grad_norm_two = scatter_tokens(norm_parts)
    branch_parts = []
    for w in down_all:
        last = turned_product([after(hidden, last)], [w], "down")
        branch_parts.append(last)
    gain_two_grad = jnp.sum(grad_norm_two * unit_two, axis=0)
    def gain_back(terms):
        own, other = halves(scatter_gains(terms, unit), c, 0)
        own, other = halves(own + shift(other, "c", 1), x, 0)
        return own + shift(other, "x", 1)

    scaled_two = grad_norm_two * gain_two
    grad_middle = grad_rows + scale_two * (
        scaled_two - unit_two * jnp.mean(scaled_two * unit_two, axis=1, keepdims=True)
    )

    def attn_terms(activations, grads, k):
        size = width // ys
        return contract(lax.dynamic_slice_in_dim(activations, k * size, size, 1), grads, 0, 1)

    grad_branch = gather_tokens(grad_middle.astype(bf16))
    branch_two = scatter_tokens([after(part, grad_branch) for part in branch_parts])
    result = from_slots(((middle + branch_two) * live).astype(bf16))[None]
    grad_attn = contract(out_w, after(grad_branch, last), 0, 1).astype(bf16)
    output_grad = scatter_whole(
        jnp.concatenate([attn_terms(grad_branch, attended, by_y[i]) for i in range(ys)], axis=0).astype(bf16)
    )
    grad_query, grad_keys, grad_values = attention_bwd(
        after(queries, down_grad), keys, values, attended, grad_attn, lse, qpos, kpos, lengths, chunk
    )
    gain_two_back = gain_back(hold(gain_two_grad, grad_query))
    grad_both = jnp.concatenate([grad_keys, grad_values], axis=1)
    grad_both = sum(
        [grad_both[0].astype(f32)]
        + [shift(grad_both[k], "y", -k).astype(f32) for k in range(1, ys)]
    )
    grad_qkv = jnp.concatenate(
        [
            rotate(grad_query, cos_table, sin_table, True).astype(bf16),
            rotate(grad_both[:nk], cos_table, sin_table, True).astype(bf16),
            grad_both[nk:].astype(bf16),
        ],
        axis=0,
    )
    qkv_sent = send_slots([attn_terms(normed_one, grad_qkv, k).astype(bf16) for k in range(1, ys)])
    down_grad = finish(down_grad)
    gate_grad = finish(after(gate_grad, grad_query))
    grad_norm_one = scatter_tokens(
        [contract(after(grad_qkv, down_grad, gate_grad, result), qkv_w, 0, 1).astype(bf16)]
    )
    qkv_grad = sum([attn_terms(normed_one, grad_qkv, 0)] + [t.astype(f32) for t in qkv_sent])
    qkv_grad = scatter_column(qkv_grad.astype(bf16))
    gain_one_grad = jnp.sum(grad_norm_one * unit_one, axis=0)
    scaled_one = grad_norm_one * gain_one
    up_grad = finish(up_grad)
    scaled_one = after(scaled_one, up_grad)
    grad_inputs = grad_middle + scale_one * (
        scaled_one - unit_one * jnp.mean(scaled_one * unit_one, axis=1, keepdims=True)
    )

    qkv_back = finish(qkv_grad)

    def columns(low, high):
        return jnp.concatenate(
            [qkv_back[:, t * nqkv + low : t * nqkv + high] for t in range(4)], axis=1
        ).astype(f32)

    return (
        result,
        from_slots(grad_inputs)[None],
        gain_back(gain_one_grad),
        columns(0, nq),
        columns(nq, nq + nk),
        columns(nq + nk, nqkv),
        finish(output_grad).astype(f32),
        gain_two_back,
        gate_grad.astype(f32),
        up_grad.astype(f32),
        down_grad.astype(f32),
    )


def solution(mesh):
    dp, seq = mesh.shape["dp"], mesh.shape["seq"]
    fine = Mesh(mesh.devices.reshape(dp // 2, 2, seq // 2, 2), ("z", "c", "y", "x"))
    every = ("z", "c", "y", "x")
    tokens = P(("z", "c"), ("y", "x"), None)
    vector, matrix = P(every), P(every, None)
    return jax.shard_map(
        body,
        mesh=fine,
        in_specs=(
            tokens, tokens, P(("z", "c")), P(("z", "c"), None), vector, matrix, matrix, matrix,
            matrix, vector, matrix, matrix, matrix,
        ),
        out_specs=(
            tokens, tokens, vector, matrix, matrix, matrix, matrix, vector, matrix, matrix, matrix,
        ),
        check_vma=False,
    )
```

time: 4160 us -> 1330 us (0.32)
  waiting for transfers between devices: 3030 us -> 582 us
  matrix products: 726 us -> 41.5 us
  Pallas kernels: 0 us -> 437 us
  other arithmetic: 238 us -> 102 us
  blocking collectives: 81.6 us -> 0 us
  starting transfers between devices: 1.32 us -> 54.5 us
    reduce_scatter x7 -> x5, waiting for transfers between devices: 2440 us -> 37 us  [the longest x1 36.9 us: scatter_column(): return lax.psum_scatter(total, 'z', scatter_dimension=0, tiled=True)]
    dot_general x49 -> x8, matrix products: 726 us -> 41.5 us  [contract(): lax.dot_general(left, right, (((left_dim,), (right_dim,)), ((), ())), pre...]
    all_gather x9 -> x5, waiting for transfers between devices: 580 us -> 33.8 us  [the longest x3 33.8 us: gather_column(): return lax.all_gather(unit, 'z', axis=0, tiled=True)]
    ppermute x0 -> x64, waiting for transfers between devices: none -> 511 us  [shift(): lax.ppermute(value, axis, [(i, (i + steps) % size) for i in range(size)])]
    pallas_call x0 -> x22, Pallas kernels: none -> 437 us  [the longest x1 93.8 us: attention_bwd(): pl.pallas_call(functools.partial(attention_bwd_body, chunk, blocks), grid...]
    concatenate x3 -> x8, other arithmetic: 133 us -> 27 us  [the longest x4 23.3 us: gather_tokens(): jnp.concatenate([own, beside, sibling, shift(beside, 'c', 1)], axis=0)]
    unnamed x2 -> x0, blocking collectives: 81.6 us -> none
    reduce_sum x5 -> x4, other arithmetic: 61.8 us -> 6.45 us  [the longest x1 2.1 us: body(): jnp.mean(inputs * inputs, axis=1, keepdims=True) + epsilon]
  transfers between devices with their start and end apart: 16 -> 74, of which waited for: 13 -> 36; matrix products, arithmetic and copies ran while one was open for 15% -> 16% of each run, Pallas kernels for 0% -> 33%
where the time goes in v1:
time: 1330 us
  waiting for transfers between devices  582 us (44%)
  Pallas kernels  437 us (33%)
  other arithmetic  102 us (8%)
  local copies, waits for them, and re-layouts  93.3 us (7%)
  starting transfers between devices  54.5 us (4%)
  matrix products  41.5 us (3%)
  between operations  17.6 us (1%)
    ppermute x64, waiting for transfers between devices, shift(): lax.ppermute(value, axis, [(i, (i + steps) % size) for i in range(size)])  511 us
    pallas_call x1, Pallas kernels, attention_bwd(): pl.pallas_call(functools.partial(attention_bwd_body, chunk, blocks), grid...  93.8 us
    pallas_call x3, Pallas kernels, columns_product(): pl.pallas_call(kernel, grid_spec=pltpu.PrefetchScalarGridSpec(num_scalar_...  86.8 us
    pallas_call x1, Pallas kernels, attention_fwd(): pl.pallas_call(functools.partial(attention_fwd_body, chunk, blocks), grid...  84.6 us
    pallas_call x3, Pallas kernels, rows_product(): pl.pallas_call(kernel, grid=(n // bn, t // bm), in_specs=[pl.BlockSpec((b...  80.4 us
    pallas_call x4, Pallas kernels, turned_product(): pl.pallas_call(kernel, grid=(n // bn, t // bm), in_specs=[pl.BlockSpec((b...  74.9 us
    ppermute x64, starting transfers between devices, shift(): lax.ppermute(value, axis, [(i, (i + steps) % size) for i in range(size)])  53.6 us
    dot_general x8, matrix products, contract(): lax.dot_general(left, right, (((left_dim,), (right_dim,)), ((), ())), pre...  41.5 us
  transfers between devices with their start and end apart: 74, of which 36 were waited for; matrix products, arithmetic and copies ran while one was open for 16% of the time, Pallas kernels for 33%

profile of v1, /device:TPU:0, one launch (start us, length us, event | category | flops | bytes accessed | tf_op | source)
XLA Modules:
  0.0 1328.2 jit_solution(5968981342724646966)
XLA Ops:
  108.4 22.2 %all-gather.8.cloned.1.call-done.refs_0_ = bf16[1024,512]{1,0:T(8,128)(2,1)} async-done(((bf16[256,512]{1,0:T(8,128)(2,1)}), bf16[1024,512]{1,0:T(8,128)(2,1)}) %all-gather.8.cloned.1.call-update) | async-done | bytes 1048592 | tf_op jit(solution)/shard_map/all_gather | solution.py:93
  139.5 45.2 %collective-permute-done.13 = bf16[512,2048]{1,0:T(8,128)(2,1)} collective-permute-done((bf16[512,2048]{1,0:T(8,128)(2,1)}, bf16[512,2048]{1,0:T(8,128)(2,1)}, u32[]{:S(2)}, u32[]{:S(2)}) %collective-permute-start.13) | collective-permute-done | bytes 2097184 | tf_op jit(solution)/shard_map/ppermute | solution.py:38
  216.4 28.9 %collective-permute-done.16 = bf16[256,2048]{1,0:T(8,128)(2,1)S(1)} collective-permute-done((bf16[256,2048]{1,0:T(8,128)(2,1)S(1)}, bf16[256,2048]{1,0:T(8,128)(2,1)S(1)}, u32[]{:S(2)}, u32[]{:S(2)}) %collective-permute-start.16) | collective-permute-done | bytes 1048608 | tf_op jit(solution)/shard_map/ppermute | solution.py:38
  265.6 84.6 %attention_forward.1 = (bf16[512,2048]{1,0:T(8,128)(2,1)}, f32[2,4,2048]{2,1,0:T(4,128)}) custom-call(s32[2,4]{1,0:T(2,128)} %get-tuple-element.84.qpos_ref, s32[2,8]{1,0:T(2,128)} %stack.71.kpos_ref, s32[2]{0:T(128)} %pad_add_fusion.2.len_ref, bf16[512,2048]{1,0:T(8,128)(2,1)} %bitcast.85, bf16[2,128,2048]{2,1,0:T(8,128)(2,1)} %get-tuple-element.101.k_ref, ...), custom_call_target="tpu_custom_call" | custom-call | flops 17179869184 | bytes 6291456 | tf_op jit(solution)/shard_map/attention_forward/pallas_call | solution.py:399
  357.8 29.2 %collective-permute-done.20.refs_2_ = bf16[1024,2048]{1,0:T(8,128)(2,1)} collective-permute-done((bf16[1024,2048]{1,0:T(8,128)(2,1)}, bf16[1024,2048]{1,0:T(8,128)(2,1)}, u32[]{:S(2)}, u32[]{:S(2)}) %collective-permute-start.20) | collective-permute-done | bytes 4194336 | tf_op jit(solution)/shard_map/ppermute | solution.py:38
  431.8 46.3 %collective-permute-done.23 = bf16[512,2048]{1,0:T(8,128)(2,1)S(1)} collective-permute-done((bf16[512,2048]{1,0:T(8,128)(2,1)S(1)}, bf16[512,2048]{1,0:T(8,128)(2,1)S(1)}, u32[]{:S(2)}, u32[]{:S(2)}) %collective-permute-start.23) | collective-permute-done | bytes 2097184 | tf_op jit(solution)/shard_map/ppermute | solution.py:38
  482.9 45.7 %collective-permute-done.24 = bf16[512,2048]{1,0:T(8,128)(2,1)} collective-permute-done((bf16[512,2048]{1,0:T(8,128)(2,1)S(1)}, bf16[512,2048]{1,0:T(8,128)(2,1)}, u32[]{:S(2)}, u32[]{:S(2)}) %collective-permute-start.24) | collective-permute-done | bytes 2097184 | tf_op jit(solution)/shard_map/ppermute | solution.py:38
  544.4 23.6 %gate.1.refs_3_ = bf16[2048,2048]{1,0:T(8,128)(2,1)} custom-call(bf16[2048,2048]{1,0:T(8,128)(2,1)} %pad_maximum_fusion.2.refs_0_.left_ref, bf16[1024,2048]{1,0:T(8,128)(2,1)} %hold.10.refs_1_.refs_2_, bf16[1024,2048]{1,0:T(8,128)(2,1)} %collective-permute-done.20.refs_2_), custom_call_target="tpu_custom_call" | custom-call | flops 17179869184 | bytes 25165824 | tf_op jit(solution)/shard_map/gate/pallas_call | solution.py:224
  568.0 26.4 %up.1 = (bf16[2048,2048]{1,0:T(8,128)(2,1)}, bf16[2048,2048]{1,0:T(8,128)(2,1)}) custom-call(bf16[2048,2048]{1,0:T(8,128)(2,1)} %pad_maximum_fusion.2.refs_0_.left_ref, bf16[1024,2048]{1,0:T(8,128)(2,1)} %get-tuple-element.88.refs_1_.refs_3_, bf16[1024,2048]{1,0:T(8,128)(2,1)} %get-tuple-element.87.refs_2_.refs_3_, bf16[2048,2048]{1,0:T(8,128)(2,1)} %gate.1.refs_3_), custom_call_target="tpu_custom_call" | custom-call | flops 17179869184 | bytes 25165824 | tf_op jit(solution)/shard_map/up/pallas_call | solution.py:224
  594.4 28.5 %down_grad.1 = bf16[2048,2048]{1,0:T(8,128)(2,1)} custom-call(s32[2]{0:T(128)} %and_select_fusion.slots_ref, bf16[2048,2048]{1,0:T(8,128)(2,1)} %pad_maximum_fusion.1.left_ref.refs_0_, bf16[2048,2048]{1,0:T(8,128)(2,1)} %get-tuple-element.56.right_ref.refs_0_), custom_call_target="tpu_custom_call" | custom-call | flops 17179869184 | bytes 20971520 | tf_op jit(solution)/shard_map/down_grad/pallas_call | solution.py:288
  631.6 30.4 %hidden_grad.1 = (bf16[2048,2048]{1,0:T(8,128)(2,1)}, bf16[2048,2048]{1,0:T(8,128)(2,1)}) custom-call(bf16[2048,2048]{1,0:T(8,128)(2,1)} %pad_maximum_fusion.1.left_ref.refs_0_, bf16[1024,2048]{1,0:T(8,128)(2,1)} %get-tuple-element.86.refs_1_, bf16[1024,2048]{1,0:T(8,128)(2,1)} %get-tuple-element.85.refs_2_.refs_1_, bf16[2048,2048]{1,0:T(8,128)(2,1)} %gate.1.refs_3_, ...), custom_call_target="tpu_custom_call" | custom-call | flops 17179869184 | bytes 25165824 | tf_op jit(solution)/shard_map/hidden_grad/pallas_call | solution.py:224
  662.0 28.7 %gate_grad.1 = bf16[2048,2048]{1,0:T(8,128)(2,1)} custom-call(s32[2]{0:T(128)} %and_select_fusion.slots_ref, bf16[2048,2048]{1,0:T(8,128)(2,1)} %pad_maximum_fusion.2.refs_0_.left_ref, bf16[2048,2048]{1,0:T(8,128)(2,1)} %get-tuple-element.53.right_ref.refs_0_), custom_call_target="tpu_custom_call" | custom-call | flops 17179869184 | bytes 20971520 | tf_op jit(solution)/shard_map/gate_grad/pallas_call | solution.py:288
  690.7 29.6 %up_grad.1 = bf16[2048,2048]{1,0:T(8,128)(2,1)} custom-call(s32[2]{0:T(128)} %and_select_fusion.slots_ref, bf16[2048,2048]{1,0:T(8,128)(2,1)} %pad_maximum_fusion.2.refs_0_.left_ref, bf16[2048,2048]{1,0:T(8,128)(2,1)} %get-tuple-element.51.right_ref.refs_1_), custom_call_target="tpu_custom_call" | custom-call | flops 17179869184 | bytes 20971520 | tf_op jit(solution)/shard_map/up_grad/pallas_call | solution.py:288
  720.3 23.9 %norm_grad.2 = bf16[2048,1024]{1,0:T(8,128)(2,1)} custom-call(bf16[2048,2048]{1,0:T(8,128)(2,1)} %get-tuple-element.53.right_ref.refs_0_, bf16[2048,2048]{1,0:T(8,128)(2,1)} %get-tuple-element.51.right_ref.refs_1_, bf16[1024,2048]{1,0:T(8,128)(2,1)} %hold.10.refs_1_.refs_2_, bf16[1024,2048]{1,0:T(8,128)(2,1)} %get-tuple-element.88.refs_1_.refs_3_), custom_call_target="tpu_custom_call" | custom-call | flops 17179869184 | bytes 25165824 | tf_op jit(solution)/shard_map/norm_grad/pallas_call | solution.py:253
  746.4 24.0 %norm_grad.3 = bf16[2048,1024]{1,0:T(8,128)(2,1)} custom-call(bf16[2048,2048]{1,0:T(8,128)(2,1)} %get-tuple-element.53.right_ref.refs_0_, bf16[2048,2048]{1,0:T(8,128)(2,1)} %get-tuple-element.51.right_ref.refs_1_, bf16[1024,2048]{1,0:T(8,128)(2,1)} %collective-permute-done.20.refs_2_, bf16[1024,2048]{1,0:T(8,128)(2,1)} %get-tuple-element.87.refs_2_.refs_3_), custom_call_target="tpu_custom_call" | custom-call | flops 17179869184 | bytes 25165824 | tf_op jit(solution)/shard_map/norm_grad/pallas_call | solution.py:253
  779.1 21.3 %collective-permute-done.28 = bf16[512,1024]{1,0:T(8,128)(2,1)S(1)} collective-permute-done((bf16[512,1024]{1,0:T(8,128)(2,1)S(1)}, bf16[512,1024]{1,0:T(8,128)(2,1)S(1)}, u32[]{:S(2)}, u32[]{:S(2)}) %collective-permute-start.28) | collective-permute-done | bytes 1048608 | tf_op jit(solution)/shard_map/ppermute | solution.py:38
  800.8 21.4 %collective-permute-done.30 = bf16[512,1024]{1,0:T(8,128)(2,1)S(1)} collective-permute-done((bf16[512,1024]{1,0:T(8,128)(2,1)S(1)}, bf16[512,1024]{1,0:T(8,128)(2,1)S(1)}, u32[]{:S(2)}, u32[]{:S(2)}) %collective-permute-start.30) | collective-permute-done | bytes 1048608 | tf_op jit(solution)/shard_map/ppermute | solution.py:38
  828.4 45.7 %collective-permute-done.31 = bf16[512,2048]{1,0:T(8,128)(2,1)} collective-permute-done((bf16[512,2048]{1,0:T(8,128)(2,1)S(1)}, bf16[512,2048]{1,0:T(8,128)(2,1)}, u32[]{:S(2)}, u32[]{:S(2)}) %collective-permute-start.31) | collective-permute-done | bytes 2097184 | tf_op jit(solution)/shard_map/ppermute | solution.py:38
  953.5 21.4 %collective-permute-done.37 = bf16[512,1024]{1,0:T(8,128)(2,1)} collective-permute-done((bf16[512,1024]{1,0:T(8,128)(2,1)}, bf16[512,1024]{1,0:T(8,128)(2,1)}, u32[]{:S(2)}, u32[]{:S(2)}) %collective-permute-start.37) | collective-permute-done | bytes 1048608 | tf_op jit(solution)/shard_map/ppermute | solution.py:38
  982.2 93.8 %attention_backward.1 = (f32[512,2048]{1,0:T(8,128)}, bf16[2,128,2048]{2,1,0:T(8,128)(2,1)}, bf16[2,128,2048]{2,1,0:T(8,128)(2,1)}) custom-call(s32[2,4]{1,0:T(2,128)} %get-tuple-element.84.qpos_ref, s32[2,8]{1,0:T(2,128)} %stack.71.kpos_ref, s32[2]{0:T(128)} %pad_add_fusion.2.len_ref, bf16[512,2048]{1,0:T(8,128)(2,1)} %bitcast.86, ...), custom_call_target="tpu_custom_call" | custom-call | flops 42949672960 | bytes 14680064 | tf_op jit(solution)/shard_map/attention_backward/pallas_call | solution.py:516
  1084.3 30.7 %collective-permute-done.38 = bf16[256,2048]{1,0:T(8,128)(2,1)S(1)} collective-permute-done((bf16[256,2048]{1,0:T(8,128)(2,1)S(1)}, bf16[256,2048]{1,0:T(8,128)(2,1)S(1)}, u32[]{:S(2)}, u32[]{:S(2)}) %collective-permute-start.38) | collective-permute-done | bytes 1048608 | tf_op jit(solution)/shard_map/ppermute | solution.py:38
  1137.4 32.1 %collective-permute-done.53 = bf16[1024,768]{1,0:T(8,128)(2,1)} collective-permute-done((bf16[1024,768]{1,0:T(8,128)(2,1)S(1)}, bf16[1024,768]{1,0:T(8,128)(2,1)}, u32[]{:S(2)}, u32[]{:S(2)}) %collective-permute-start.53) | collective-permute-done | bytes 1572896 | tf_op jit(solution)/shard_map/ppermute | solution.py:38
  1187.2 36.9 %reduce-scatter.12.cloned.1.call-done = bf16[256,768]{1,0:T(8,128)(2,1)} async-done(((bf16[1024,768]{1,0:T(8,128)(2,1)}), bf16[256,768]{1,0:T(8,128)(2,1)}) %reduce-scatter.12.cloned.1.call-update) | async-done | bytes 393232 | tf_op jit(solution)/shard_map/reduce_scatter | solution.py:116
  1234.8 48.4 %collective-permute-done.55 = bf16[64,1536]{1,0:T(8,128)(2,1)S(1)} collective-permute-done((bf16[64,1536]{1,0:T(8,128)(2,1)S(1)}, bf16[64,1536]{1,0:T(8,128)(2,1)S(1)}, u32[]{:S(2)}, u32[]{:S(2)}) %collective-permute-start.55) | collective-permute-done | bytes 196640 | tf_op jit(solution)/shard_map/ppermute | solution.py:38
  (457 shorter events, 441.6 us)
Async XLA Ops:
  7.2 94.4 %all-gather.6.cloned.1.call-start = ((), (), s32[]{:S(2)}) async-start(), calls=%async_computation.5 | async-start | bytes 1966080 | tf_op jit(solution)/shard_map/all_gather | solution.py:93
  64.5 66.1 %all-gather.8.cloned.1.call-start = ((), (), s32[]{:S(2)}) async-start(), calls=%async_computation.6 | async-start | bytes 1310720 | tf_op jit(solution)/shard_map/all_gather | solution.py:93
  89.9 157.9 %all-gather.10.cloned.1.call-start = ((), (), s32[]{:S(2)}) async-start(), calls=%async_computation.7 | async-start | bytes 5242880 | tf_op jit(solution)/shard_map/all_gather | solution.py:93
  138.0 391.2 %all-gather.12.cloned.1.call-start = ((), (), s32[]{:S(2)}) async-start(), calls=%async_computation.8 | async-start | bytes 9437184 | tf_op jit(solution)/shard_map/all_gather | solution.py:107
  139.5 57.4 %collective-permute-start.14 = (bf16[512,2048]{1,0:T(8,128)(2,1)}, bf16[512,2048]{1,0:T(8,128)(2,1)}, u32[]{:S(2)}, u32[]{:S(2)}) collective-permute-start(bf16[512,2048]{1,0:T(8,128)(2,1)} %fusion.4), channel_id=1, source_target_pairs={{0,4},{4,0},{1,5},{5,1},{2,6},{6,2},{3,7},{7,3},{8,12},{12,8},{9,1... | collective-permute-start | bytes 6291464 | tf_op jit(solution)/shard_map/ppermute | solution.py:38
  190.7 432.4 %all-gather.14.cloned.1.call-start = ((), (), s32[]{:S(2)}) async-start(), calls=%async_computation.9 | async-start | bytes 9437184 | tf_op jit(solution)/shard_map/all_gather | solution.py:107
  214.9 47.6 %collective-permute-start.17 = (bf16[512,2048]{1,0:T(8,128)(2,1)}, bf16[512,2048]{1,0:T(8,128)(2,1)}, u32[]{:S(2)}, u32[]{:S(2)}) collective-permute-start(bf16[512,2048]{1,0:T(8,128)(2,1)} %broadcast_multiply_fusion), channel_id=1, source_target_pairs={{0,1},{1,0},{2,3},{3,2},{4,5},{5,4},{6,7},{7,6},{8,9},{9,8},{10,11... | collective-permute-start | bytes 6291464 | tf_op jit(solution)/shard_map/ppermute | solution.py:38
  247.8 139.2 %collective-permute-start.20 = (bf16[1024,2048]{1,0:T(8,128)(2,1)}, bf16[1024,2048]{1,0:T(8,128)(2,1)}, u32[]{:S(2)}, u32[]{:S(2)}) collective-permute-start(bf16[1024,2048]{1,0:T(8,128)(2,1)} %hold.10.refs_1_.refs_2_), channel_id=1, source_target_pairs={{0,2},{2,0},{1,3},{3,1},{4,6},{6,4},{5,7},{7,5},{8,10},{10,8},{9,1... | collective-permute-start | bytes 12582920 | tf_op jit(solution)/shard_map/ppermute | solution.py:38
  253.5 152.6 %collective-permute-start.21 = (bf16[1024,512]{1,0:T(8,128)(2,1)}, bf16[1024,512]{1,0:T(8,128)(2,1)}, u32[]{:S(2)}, u32[]{:S(2)}) collective-permute-start(bf16[1024,512]{1,0:T(8,128)(2,1)} %hold.8.refs_1_), channel_id=1, source_target_pairs={{0,2},{2,0},{1,3},{3,1},{4,6},{6,4},{5,7},{7,5},{8,10},{10,8},{9,1... | collective-permute-start | bytes 3145736 | tf_op jit(solution)/shard_map/ppermute | solution.py:38
  253.5 96.7 %collective-permute-start.18 = (bf16[512,2048]{1,0:T(8,128)(2,1)}, bf16[512,2048]{1,0:T(8,128)(2,1)}, u32[]{:S(2)}, u32[]{:S(2)}) collective-permute-start(bf16[512,2048]{1,0:T(8,128)(2,1)} %broadcast_multiply_fusion), channel_id=1, source_target_pairs={{0,4},{4,0},{1,5},{5,1},{2,6},{6,2},{3,7},{7,3},{8,12},{12,8},{9,1... | collective-permute-start | bytes 6291464 | tf_op jit(solution)/shard_map/ppermute | solution.py:38
  262.5 87.7 %collective-permute-start.19 = (bf16[512,2048]{1,0:T(8,128)(2,1)}, bf16[512,2048]{1,0:T(8,128)(2,1)}, u32[]{:S(2)}, u32[]{:S(2)}) collective-permute-start(bf16[512,2048]{1,0:T(8,128)(2,1)} %collective-permute-done.17), channel_id=1, source_target_pairs={{0,4},{4,0},{1,5},{5,1},{2,6},{6,2},{3,7},{7,3},{8,12},{12,8},{9,1... | collective-permute-start | bytes 6291464 | tf_op jit(solution)/shard_map/ppermute | solution.py:38
  416.7 565.4 %reduce-scatter.6.cloned.1.call-start = ((), (), s32[]{:S(2)}) async-start(), calls=%async_computation.10 | async-start | bytes 9437184 | tf_op jit(solution)/shard_map/reduce_scatter | solution.py:112
  430.3 47.8 %collective-permute-start.23 = (bf16[512,2048]{1,0:T(8,128)(2,1)S(1)}, bf16[512,2048]{1,0:T(8,128)(2,1)S(1)}, u32[]{:S(2)}, u32[]{:S(2)}) collective-permute-start(bf16[512,2048]{1,0:T(8,128)(2,1)S(1)} %slice.553), channel_id=1, source_target_pairs={{0,1},{1,0},{2,3},{3,2},{4,5},{5,4},{6,7},{7,6},{8,9},{9,8},{10,11... | collective-permute-start | bytes 6291464 | tf_op jit(solution)/shard_map/ppermute | solution.py:38
  481.5 47.1 %collective-permute-start.24 = (bf16[512,2048]{1,0:T(8,128)(2,1)S(1)}, bf16[512,2048]{1,0:T(8,128)(2,1)}, u32[]{:S(2)}, u32[]{:S(2)}) collective-permute-start(bf16[512,2048]{1,0:T(8,128)(2,1)S(1)} %multiply_convert_fusion), channel_id=1, source_target_pairs={{0,1},{1,0},{2,3},{3,2},{4,5},{5,4},{6,7},{7,6},{8,9},{9,8},{10,11... | collective-permute-start | bytes 6291464 | tf_op jit(solution)/shard_map/ppermute | solution.py:38
  482.9 54.7 %collective-permute-start.25 = (bf16[512,2048]{1,0:T(8,128)(2,1)S(1)}, bf16[512,2048]{1,0:T(8,128)(2,1)}, u32[]{:S(2)}, u32[]{:S(2)}) collective-permute-start(bf16[512,2048]{1,0:T(8,128)(2,1)S(1)} %multiply_convert_fusion), channel_id=1, source_target_pairs={{0,4},{4,0},{1,5},{5,1},{2,6},{6,2},{3,7},{7,3},{8,12},{12,8},{9,1... | collective-permute-start | bytes 6291464 | tf_op jit(solution)/shard_map/ppermute | solution.py:38
  623.0 453.0 %reduce-scatter.8.cloned.1.call-start = ((), (), s32[]{:S(2)}) async-start(), calls=%async_computation.11 | async-start | bytes 9437184 | tf_op jit(solution)/shard_map/reduce_scatter | solution.py:112
  690.7 484.9 %reduce-scatter.14.cloned.1.call-start = ((), (), s32[]{:S(2)}) async-start(), calls=%async_computation.14 | async-start | bytes 2359296 | tf_op jit(solution)/shard_map/reduce_scatter | solution.py:112
  827.0 47.1 %collective-permute-start.31 = (bf16[512,2048]{1,0:T(8,128)(2,1)S(1)}, bf16[512,2048]{1,0:T(8,128)(2,1)}, u32[]{:S(2)}, u32[]{:S(2)}) collective-permute-start(bf16[512,2048]{1,0:T(8,128)(2,1)S(1)} %get-tuple-element.77), channel_id=1, source_target_pairs={{0,1},{1,0},{2,3},{3,2},{4,5},{5,4},{6,7},{7,6},{8,9},{9,8},{10,11... | collective-permute-start | bytes 6291464 | tf_op jit(solution)/shard_map/ppermute | solution.py:38
  828.4 47.6 %collective-permute-start.32 = (bf16[512,2048]{1,0:T(8,128)(2,1)S(1)}, bf16[512,2048]{1,0:T(8,128)(2,1)}, u32[]{:S(2)}, u32[]{:S(2)}) collective-permute-start(bf16[512,2048]{1,0:T(8,128)(2,1)S(1)} %get-tuple-element.77), channel_id=1, source_target_pairs={{0,4},{4,0},{1,5},{5,1},{2,6},{6,2},{3,7},{7,3},{8,12},{12,8},{9,1... | collective-permute-start | bytes 6291464 | tf_op jit(solution)/shard_map/ppermute | solution.py:38
  889.9 289.7 %reduce-scatter.10.cloned.1.call-start = ((), (), s32[]{:S(2)}) async-start(), calls=%async_computation.12 | async-start | bytes 9437184 | tf_op jit(solution)/shard_map/reduce_scatter | solution.py:112
  922.4 301.7 %reduce-scatter.12.cloned.1.call-start = ((), (), s32[]{:S(2)}) async-start(), calls=%async_computation.13 | async-start | bytes 1966080 | tf_op jit(solution)/shard_map/reduce_scatter | solution.py:116
  1137.4 87.9 %collective-permute-start.43 = (bf16[1024,2048]{1,0:T(8,128)(2,1)}, bf16[1024,2048]{1,0:T(8,128)(2,1)}, u32[]{:S(2)}, u32[]{:S(2)}) collective-permute-start(bf16[1024,2048]{1,0:T(8,128)(2,1)} %slice.440), channel_id=1, source_target_pairs={{0,4},{4,0},{1,5},{5,1},{2,6},{6,2},{3,7},{7,3},{8,12},{12,8},{9,1... | collective-permute-start | bytes 12582920 | tf_op jit(solution)/shard_map/ppermute | solution.py:38
  1231.0 54.0 %collective-permute-start.44 = (bf16[512,2048]{1,0:T(8,128)(2,1)S(1)}, bf16[512,2048]{1,0:T(8,128)(2,1)S(1)}, u32[]{:S(2)}, u32[]{:S(2)}) collective-permute-start(bf16[512,2048]{1,0:T(8,128)(2,1)S(1)} %slice.552), channel_id=1, source_target_pairs={{0,1},{1,0},{2,3},{3,2},{4,5},{5,4},{6,7},{7,6},{8,9},{9,8},{10,11... | collective-permute-start | bytes 6291464 | tf_op jit(solution)/shard_map/ppermute | solution.py:38
  1232.7 50.6 %collective-permute-start.55 = (bf16[64,1536]{1,0:T(8,128)(2,1)S(1)}, bf16[64,1536]{1,0:T(8,128)(2,1)S(1)}, u32[]{:S(2)}, u32[]{:S(2)}) collective-permute-start(bf16[64,1536]{1,0:T(8,128)(2,1)S(1)} %get-tuple-element.137), channel_id=1, source_target_pairs={{0,1},{1,0},{2,3},{3,2},{4,5},{5,4},{6,7},{7,6},{8,9},{9,8},{10,11... | collective-permute-start | bytes 589832 | tf_op jit(solution)/shard_map/ppermute | solution.py:38
  (106 other events, 1649.2 us)
Sparse Core Ops, SparseCore 0:
  64.6 36.9 all-gather.5
  103.7 26.7 all-gather.7
  138.1 79.8 all-gather.9
  220.0 169.0 all-gather.11
  416.9 124.0 all-gather.13
  623.1 148.3 reduce-scatter.5
  775.5 148.0 reduce-scatter.7
  927.2 66.7 reduce-scatter.13
  997.6 165.8 reduce-scatter.9
  1175.7 48.4 reduce-scatter.11

commit v2 on v1

--- a/solution.py
+++ b/solution.py
@@ -63,11 +63,19 @@
     return in_order(own, shift(other, "c", 1), c, 0)
 
 
+def join_by_c(unit, c):
+    own, other = halves(unit, c, 0)
+    return own, shift(other, "c", 1)
+
+
+def join_by_x(own, got, c, x):
+    own, other = halves(in_order(own, got, c, 1), x, 0)
+    return own, shift(other, "x", 1)
+
+
 def join_columns(unit, c, x):
-    own, other = halves(unit, c, 0)
-    both = in_order(own, shift(other, "c", 1), c, 1)
-    own, other = halves(both, x, 0)
-    return in_order(own, shift(other, "x", 1), x, 1)
+    own, got = join_by_x(*join_by_c(unit, c), c, x)
+    return in_order(own, got, x, 1)
 
 
 def after(value, *others):
@@ -141,18 +149,27 @@
     return out
 
 
-def gather_tokens(own, *others):
-    beside = after(shift(own, "x", 1), *others)
-    sibling = shift(own, "c", 1)
-    return jnp.concatenate([own, beside, sibling, shift(beside, "c", 1)], axis=0)
-
-
-def scatter_tokens(partials):
+def group_tokens(own):
+    beside = shift(own, "x", 1)
+    return own, beside, shift(own, "c", 1), shift(beside, "c", 1)
+
+
+def scatter_by_c(partial, by_sequence):
+    count = partial.shape[0] // 4
+    mine = partial[:count]
+    if by_sequence:
+        beside, sent = partial[count : 2 * count], partial[2 * count :]
+    else:
+        beside, sent = partial[3 * count :], partial[count : 3 * count]
+    got = shift(sent, "c", 1).astype(f32)
+    return mine.astype(f32) + got[:count], beside.astype(f32) + got[count:]
+
+
+def scatter_tokens(partials, by_sequence):
     sums = []
     for partial in partials:
-        count = partial.shape[0] // 4
-        half = partial[: 2 * count].astype(f32) + shift(partial[2 * count :], "c", 1).astype(f32)
-        sums.append(half[:count] + shift(half[count:].astype(bf16), "x", 1).astype(f32))
+        mine, beside = scatter_by_c(partial, by_sequence)
+        sums.append(mine + shift(beside.astype(bf16), "x", 1).astype(f32))
     return jnp.concatenate(sums, axis=1)
 
 
@@ -321,7 +338,7 @@
 
 
 def attention_fwd_body(
-    chunk, blocks, qpos_ref, kpos_ref, len_ref, q_ref, k_ref, v_ref, o_ref, lse_ref,
+    chunk, blocks, part, qpos_ref, kpos_ref, len_ref, q_ref, k_ref, v_ref, o_ref, lse_ref,
     kn_ref, m_ref, l_ref, acc_ref,
 ):
     s, qb = pl.program_id(0), pl.program_id(2)
@@ -335,7 +352,7 @@
                     k_ref[yk, :, pl.ds(b * chunk, chunk)].astype(f32).T.astype(bf16)
                 )
 
-    qp = qpos_ref[s, qb]
+    qp = qpos_ref[s, part * (blocks // 2) + qb]
     length = len_ref[s]
     m_ref[...] = jnp.full_like(m_ref, floor_score)
     l_ref[...] = jnp.zeros_like(l_ref)
@@ -385,24 +402,25 @@
     lse_ref[0] = m_ref[0:REP, :] + jnp.log(l_ref[0:REP, :])
 
 
-def attention_fwd(queries, keys, values, qpos, kpos, lengths, chunk):
+def attention_fwd(queries, keys, values, qpos, kpos, lengths, chunk, part):
     tokens = queries.shape[1]
     groups = queries.shape[0] // (REP * HD)
     ys = keys.shape[0]
     half = tokens // 2
     blocks = half // chunk
-    grid = (2, groups, blocks)
-    q_spec = pl.BlockSpec((REP * HD, chunk), lambda s, g, b, *_: (g, s * blocks + b))
+    few = blocks // 2
+    q_spec = pl.BlockSpec((REP * HD, chunk), lambda s, g, b, *_: (g, s * blocks + part * few + b))
+    o_spec = pl.BlockSpec((REP * HD, chunk), lambda s, g, b, *_: (g, ((s + part) % 2) * few + b))
     kv_spec = pl.BlockSpec((ys, HD, half), lambda s, g, b, *_: (0, g, s))
-    lse_spec = pl.BlockSpec((1, REP, chunk), lambda s, g, b, *_: (g, 0, s * blocks + b))
-    pairs = 2 * groups * blocks * blocks * ys
+    lse_spec = pl.BlockSpec((1, REP, chunk), lambda s, g, b, *_: (g, 0, ((s + part) % 2) * few + b))
+    pairs = 2 * groups * few * blocks * ys
     return pl.pallas_call(
-        functools.partial(attention_fwd_body, chunk, blocks),
+        functools.partial(attention_fwd_body, chunk, blocks, part),
         grid_spec=pltpu.PrefetchScalarGridSpec(
             num_scalar_prefetch=3,
-            grid=grid,
+            grid=(2, groups, few),
             in_specs=[q_spec, kv_spec, kv_spec],
-            out_specs=[q_spec, lse_spec],
+            out_specs=[o_spec, lse_spec],
             scratch_shapes=[
                 pltpu.VMEM((ys * half, HD), bf16),
                 pltpu.VMEM((8, chunk), f32),
@@ -411,12 +429,12 @@
             ],
         ),
         out_shape=[
-            jax.ShapeDtypeStruct(queries.shape, bf16),
-            jax.ShapeDtypeStruct((groups, REP, tokens), f32),
+            jax.ShapeDtypeStruct((queries.shape[0], half), bf16),
+            jax.ShapeDtypeStruct((groups, REP, half), f32),
         ],
         cost_estimate=estimate(
-            pairs * REP * chunk * chunk * HD * 4 * 2,
-            queries.size * 4 + keys.size * 4,
+            pairs * REP * chunk * chunk * HD * 4 * 8,
+            queries.size * 2 + keys.size * 4,
             pairs * REP * chunk * chunk,
         ),
         name="attention_forward",
@@ -424,16 +442,22 @@
 
 
 def attention_bwd_body(
-    chunk, blocks, qpos_ref, kpos_ref, len_ref, q_ref, k_ref, v_ref, o_ref, do_ref, lse_ref,
-    dq_ref, dk_ref, dv_ref, kn_ref, vn_ref, dqa_ref, dka_ref, dva_ref, delta_ref,
+    chunk, blocks, part, n_before, qpos_ref, kpos_ref, len_ref, q_ref, k_ref, v_ref, o_ref, do_ref,
+    lse_ref, *refs,
 ):
+    before = refs[:n_before]
+    dq_ref, dk_ref, dv_ref, kn_ref, vn_ref, dqa_ref, dka_ref, dva_ref, delta_ref = refs[n_before:]
     s, qb = pl.program_id(0), pl.program_id(2)
     ys = k_ref.shape[0]
 
     @pl.when(qb == 0)
     def _():
-        dka_ref[...] = jnp.zeros_like(dka_ref)
-        dva_ref[...] = jnp.zeros_like(dva_ref)
+        if before:
+            dka_ref[...] = before[0][...]
+            dva_ref[...] = before[1][...]
+        else:
+            dka_ref[...] = jnp.zeros_like(dka_ref)
+            dva_ref[...] = jnp.zeros_like(dva_ref)
         for yk in range(ys):
             for b in range(blocks):
                 rows = pl.ds((yk * blocks + b) * chunk, chunk)
@@ -441,7 +465,7 @@
                 kn_ref[rows, :] = k_ref[yk, :, cols].astype(f32).T.astype(bf16)
                 vn_ref[rows, :] = v_ref[yk, :, cols].astype(f32).T.astype(bf16)
 
-    qp = qpos_ref[s, qb]
+    qp = qpos_ref[s, part * (blocks // 2) + qb]
     length = len_ref[s]
     dqa_ref[...] = jnp.zeros_like(dqa_ref)
     for h in range(REP):
@@ -497,29 +521,32 @@
 
     dq_ref[...] = dqa_ref[...] * 0.125
 
-    @pl.when(qb == blocks - 1)
+    @pl.when(qb == blocks // 2 - 1)
     def _():
-        dk_ref[...] = dka_ref[...].astype(bf16)
-        dv_ref[...] = dva_ref[...].astype(bf16)
-
-
-def attention_bwd(queries, keys, values, attended, grads, lse, qpos, kpos, lengths, chunk):
+        dk_ref[...] = dka_ref[...].astype(dk_ref.dtype)
+        dv_ref[...] = dva_ref[...].astype(dv_ref.dtype)
+
+
+def attention_bwd(queries, keys, values, attended, grads, lse, qpos, kpos, lengths, chunk, part, *before):
     tokens = queries.shape[1]
     groups = queries.shape[0] // (REP * HD)
     ys = keys.shape[0]
     half = tokens // 2
     blocks = half // chunk
-    q_spec = pl.BlockSpec((REP * HD, chunk), lambda s, g, b, *_: (g, s * blocks + b))
+    few = blocks // 2
+    q_spec = pl.BlockSpec((REP * HD, chunk), lambda s, g, b, *_: (g, s * blocks + part * few + b))
+    o_spec = pl.BlockSpec((REP * HD, chunk), lambda s, g, b, *_: (g, ((s + part) % 2) * few + b))
     kv_spec = pl.BlockSpec((ys, HD, half), lambda s, g, b, *_: (0, g, s))
-    lse_spec = pl.BlockSpec((1, REP, chunk), lambda s, g, b, *_: (g, 0, s * blocks + b))
-    pairs = 2 * groups * blocks * blocks * ys
+    lse_spec = pl.BlockSpec((1, REP, chunk), lambda s, g, b, *_: (g, 0, ((s + part) % 2) * few + b))
+    pairs = 2 * groups * few * blocks * ys
+    kind = bf16 if before else f32
     return pl.pallas_call(
-        functools.partial(attention_bwd_body, chunk, blocks),
+        functools.partial(attention_bwd_body, chunk, blocks, part, len(before)),
         grid_spec=pltpu.PrefetchScalarGridSpec(
             num_scalar_prefetch=3,
-            grid=(2, groups, blocks),
-            in_specs=[q_spec, kv_spec, kv_spec, q_spec, q_spec, lse_spec],
-            out_specs=[q_spec, kv_spec, kv_spec],
+            grid=(2, groups, few),
+            in_specs=[q_spec, kv_spec, kv_spec, o_spec, o_spec, lse_spec] + [kv_spec] * len(before),
+            out_specs=[o_spec, kv_spec, kv_spec],
             scratch_shapes=[
                 pltpu.VMEM((ys * half, HD), bf16),
                 pltpu.VMEM((ys * half, HD), bf16),
@@ -530,17 +557,18 @@
             ],
         ),
         out_shape=[
-            jax.ShapeDtypeStruct(queries.shape, f32),
-            jax.ShapeDtypeStruct(keys.shape, bf16),
-            jax.ShapeDtypeStruct(keys.shape, bf16),
+            jax.ShapeDtypeStruct((queries.shape[0], half), f32),
+            jax.ShapeDtypeStruct(keys.shape, kind),
+            jax.ShapeDtypeStruct(keys.shape, kind),
         ],
+        compiler_params=pltpu.CompilerParams(vmem_limit_bytes=VMEM_BYTES),
         cost_estimate=estimate(
-            pairs * REP * chunk * chunk * HD * 10 * 2,
-            queries.size * 10 + keys.size * 8,
+            pairs * REP * chunk * chunk * HD * 10 * 4,
+            queries.size * 6 + keys.size * 16,
             pairs * REP * chunk * chunk,
         ),
         name="attention_backward",
-    )(qpos, kpos, lengths, queries, keys, values, attended, grads, lse)
+    )(qpos, kpos, lengths, queries, keys, values, attended, grads, lse, *before)
 
 
 def rotate(vectors, cos_table, sin_table, back=False):
@@ -628,13 +656,15 @@
     nf = gate_w.shape[1] // 4
     gate_unit, up_unit, down_unit = (mlp_unit[:, i * nf : (i + 1) * nf] for i in range(3))
     qkv_slots = gather_slots(gather_column(qkv_unit))
-    out_column = hold(gather_column(hold(out_unit, qkv_unit)), *qkv_slots[1:])
+    own, beside, sibling, both_two = group_tokens(normed_own)
+    out_column = hold(gather_column(hold(out_unit, normed_own)), beside)
     qkv_w = jnp.concatenate(qkv_slots, axis=0)
-    out_w = jnp.concatenate(gather_slots(out_column), axis=0)
+    out_slots = gather_slots(out_column)
+    out_w = jnp.concatenate(out_slots, axis=0)
     gate_column = gather_column(hold(gate_unit, out_column))
     up_all, down_all = gather_whole(up_unit, y), gather_whole(down_unit, y)
 
-    normed_one = gather_tokens(normed_own, *qkv_slots[1:])
+    normed_one = jnp.concatenate([own, beside, sibling, both_two], axis=0)
     pre = contract(after(qkv_w, mlp_unit), normed_one, 0, 1)
     queries = (rotate(pre[:nq], cos_table, sin_table).astype(bf16)) * jnp.asarray(0.125, bf16)
     key_own = rotate(pre[nq : nq + nk], cos_table, sin_table).astype(bf16)
@@ -642,15 +672,33 @@
     both_own = jnp.concatenate([key_own, value_own], axis=0)
     both = jnp.stack([both_own] + [shift(both_own, "y", k) for k in range(1, ys)])
     keys, values = both[:, :nk], both[:, nk:]
-    gate_all = gather_slots(hold(gate_column, both))
+    gate_column = hold(gate_column, both)
+    cut = gate_column.shape[0] // 2
+    gate_first = [shift(gate_column[:cut], "y", k) for k in range(1, ys)]
+    gate_rest = [shift(gate_column[cut:], "y", k) for k in range(1, ys)]
     grad_own = to_slots(grad_out[0]) * live.astype(bf16)
     grad_rows = grad_own.astype(f32)
-    grad_low = gather_tokens(after(grad_own, normed_one))
-    attended, lse = attention_fwd(after(queries, grad_own, gate_all[0]), keys, values, qpos, kpos, lengths, chunk)
-    middle = inputs + scatter_tokens([contract(after(attended, grad_low, *gate_all[1:]), out_w, 0, 1).astype(bf16)])
+    own, beside, sibling, both_two = group_tokens(hold(grad_own, both_own))
+    grad_low = jnp.concatenate([own, sibling, both_two, beside], axis=0)
+
+    attended_one, lse_one = attention_fwd(
+        after(queries, grad_own, out_w), keys, values, qpos, kpos, lengths, chunk, 1
+    )
+    branch = contract(attended_one, out_w, 0, 1).astype(bf16)
+    from_sibling = shift(branch[:rows], "c", 1)
+    beside_sum = branch[rows:].astype(f32) + from_sibling.astype(f32)
+    from_beside = shift(beside_sum.astype(bf16), "x", 1)
+    attended_zero, lse_zero = attention_fwd(
+        after(queries, from_sibling, both_two), keys, values, qpos, kpos, lengths, chunk, 0
+    )
+    branch = contract(after(attended_zero, from_beside, *gate_first), out_w, 0, 1).astype(bf16)
+    middle = inputs + branch[:rows].astype(f32) + shift(branch[rows:], "c", 1).astype(f32) + from_beside.astype(f32)
+    gate_all = [gate_column] + [jnp.concatenate(two, axis=0) for two in zip(gate_first, gate_rest)]
+    attended = jnp.concatenate([attended_zero, attended_one], axis=1)
     scale_two = lax.rsqrt(jnp.mean(middle * middle, axis=1, keepdims=True) + epsilon)
     unit_two = middle * scale_two
-    normed_two = gather_tokens((unit_two * gain_two).astype(bf16))
+    own, beside, sibling, both_two = group_tokens((unit_two * gain_two).astype(bf16))
+    normed_two = jnp.concatenate([own, sibling, both_two, after(beside, *gate_rest)], axis=0)
 
     (gate_pre,) = rows_product(normed_two, gate_all, [], plain, 1, "gate")
     up_pre, hidden = rows_product(normed_two, up_all, [gate_pre], up_finish, 2, "up")
@@ -664,19 +712,19 @@
     grad_gate, grad_up = rows_product(
         after(grad_low, last), down_all, [gate_pre, up_pre], hidden_back, 2, "hidden_grad"
     )
-    last = columns_product(normed_two, by_y, ys, grad_gate, [], "gate_grad")
-    gate_grad = scatter_whole(last)
-    last = columns_product(after(normed_two, last), by_y, ys, grad_up, [], "up_grad")
-    up_grad = scatter_whole(last)
-    norm_parts = []
+    norm_parts, last = [], grad_gate
     for g, u in zip(gate_all, up_all):
         last = turned_product([after(grad_gate, last), grad_up], [g, u], "norm_grad")
         norm_parts.append(last)
-    grad_norm_two = scatter_tokens(norm_parts)
-    branch_parts = []
-    for w in down_all:
-        last = turned_product([after(hidden, last)], [w], "down")
-        branch_parts.append(last)
+    sums = [scatter_by_c(part, False) for part in norm_parts]
+    came = [shift(beside.astype(bf16), "x", 1) for _, beside in sums]
+    last = columns_product(after(normed_two, last), by_y, ys, grad_gate, [], "gate_grad")
+    gate_grad = scatter_whole(last)
+    came[0] = after(came[0], last)
+    last = columns_product(after(normed_two, last), by_y, ys, grad_up, [], "up_grad")
+    up_grad = scatter_whole(last)
+    came[-1] = after(came[-1], last)
+    grad_norm_two = jnp.concatenate([mine + got.astype(f32) for (mine, _), got in zip(sums, came)], axis=1)
     gain_two_grad = jnp.sum(grad_norm_two * unit_two, axis=0)
     def gain_back(terms):
         own, other = halves(scatter_gains(terms, unit), c, 0)
@@ -692,42 +740,80 @@
         size = width // ys
         return contract(lax.dynamic_slice_in_dim(activations, k * size, size, 1), grads, 0, 1)
 
-    grad_branch = gather_tokens(grad_middle.astype(bf16))
-    branch_two = scatter_tokens([after(part, grad_branch) for part in branch_parts])
+    own = grad_middle.astype(bf16)
+    beside, sibling = shift(own, "x", 1), shift(own, "c", 1)
+    grad_attn = contract(out_w, jnp.concatenate([own, sibling], axis=0), 0, 1).astype(bf16)
+    query_zero, grad_keys, grad_values = attention_bwd(
+        after(queries, down_grad), keys, values, attended_zero, grad_attn, lse_zero, qpos, kpos, lengths,
+        chunk, 0,
+    )
+    beside = hold(beside, query_zero)
+    both_two = shift(beside, "c", 1)
+    branch_parts, last = [], query_zero
+    for w in down_all:
+        last = turned_product([after(hidden, last)], [w], "down")
+        branch_parts.append(last)
+    sent = [part[rows : 3 * rows] for part in branch_parts]
+    got_c = [shift(part, "c", 1) for part in sent]
+    down_own, down_got = join_by_c(hold(down_grad, query_zero), c)
+    grad_attn = contract(out_w, jnp.concatenate([both_two, after(beside, last)], axis=0), 0, 1).astype(bf16)
+    query_one, grad_keys, grad_values = attention_bwd(
+        after(queries, gate_grad, down_got, *got_c), keys, values, attended_one, grad_attn, lse_one, qpos,
+        kpos, lengths, chunk, 1, grad_keys, grad_values,
+    )
+    got_x = [
+        shift((part[3 * rows :].astype(f32) + got[rows:].astype(f32)).astype(bf16), "x", 1)
+        for part, got in zip(branch_parts, got_c)
+    ]
+    down_own, down_got = join_by_x(down_own, down_got, c, x)
+    query_one = after(query_one, down_got, *got_x)
+    down_grad = in_order(down_own, down_got, x, 1)
+    branch_two = jnp.concatenate(
+        [
+            part[:rows].astype(f32) + from_c[:rows].astype(f32) + from_x.astype(f32)
+            for part, from_c, from_x in zip(branch_parts, got_c, got_x)
+        ],
+        axis=1,
+    )
     result = from_slots(((middle + branch_two) * live).astype(bf16))[None]
-    grad_attn = contract(out_w, after(grad_branch, last), 0, 1).astype(bf16)
-    output_grad = scatter_whole(
-        jnp.concatenate([attn_terms(grad_branch, attended, by_y[i]) for i in range(ys)], axis=0).astype(bf16)
-    )
-    grad_query, grad_keys, grad_values = attention_bwd(
-        after(queries, down_grad), keys, values, attended, grad_attn, lse, qpos, kpos, lengths, chunk
-    )
-    gain_two_back = gain_back(hold(gain_two_grad, grad_query))
+    grad_branch = jnp.concatenate([own, sibling, both_two, beside], axis=0)
+    grad_branch = jnp.concatenate([own, sibling, both_two, beside], axis=0)
+    gain_two_back = gain_back(hold(gain_two_grad, query_one))
+    def pick(table, *chunks):
+        return jnp.concatenate([table[:, i * rows : (i + 1) * rows] for i in chunks], axis=1)
+
     grad_both = jnp.concatenate([grad_keys, grad_values], axis=1)
-    grad_both = sum(
-        [grad_both[0].astype(f32)]
-        + [shift(grad_both[k], "y", -k).astype(f32) for k in range(1, ys)]
+    got = [shift(grad_both[k], "y", -k) for k in range(1, ys)]
+    grad_both = sum([grad_both[0].astype(f32)] + [term.astype(f32) for term in got])
+    turned_zero = rotate(query_zero, pick(cos_table, 0, 2), pick(sin_table, 0, 2), True).astype(bf16)
+    turned_one = rotate(query_one, pick(cos_table, 3, 1), pick(sin_table, 3, 1), True).astype(bf16)
+    grad_query = jnp.concatenate(
+        [turned_zero[:, :rows], turned_one[:, rows:], turned_zero[:, rows:], turned_one[:, :rows]], axis=1
     )
     grad_qkv = jnp.concatenate(
         [
-            rotate(grad_query, cos_table, sin_table, True).astype(bf16),
+            grad_query,
             rotate(grad_both[:nk], cos_table, sin_table, True).astype(bf16),
             grad_both[nk:].astype(bf16),
         ],
         axis=0,
     )
     qkv_sent = send_slots([attn_terms(normed_one, grad_qkv, k).astype(bf16) for k in range(1, ys)])
-    down_grad = finish(down_grad)
-    gate_grad = finish(after(gate_grad, grad_query))
-    grad_norm_one = scatter_tokens(
-        [contract(after(grad_qkv, down_grad, gate_grad, result), qkv_w, 0, 1).astype(bf16)]
-    )
+    partial = contract(grad_qkv, qkv_w, 0, 1).astype(bf16)
+    mine, beside_sum = scatter_by_c(partial, True)
+    from_beside = shift(beside_sum.astype(bf16), "x", 1)
+    output_grad = scatter_whole(
+        jnp.concatenate(
+            [attn_terms(hold(grad_branch, from_beside), attended, by_y[i]) for i in range(ys)], axis=0
+        ).astype(bf16)
+    )
+    gate_grad = finish(hold(gate_grad, from_beside))
+    grad_norm_one = mine + from_beside.astype(f32)
     qkv_grad = sum([attn_terms(normed_one, grad_qkv, 0)] + [t.astype(f32) for t in qkv_sent])
-    qkv_grad = scatter_column(qkv_grad.astype(bf16))
+    qkv_grad = scatter_column(hold(qkv_grad.astype(bf16), up_grad))
     gain_one_grad = jnp.sum(grad_norm_one * unit_one, axis=0)
     scaled_one = grad_norm_one * gain_one
-    up_grad = finish(up_grad)
-    scaled_one = after(scaled_one, up_grad)
+    up_grad = finish(hold(up_grad, from_beside))
     grad_inputs = grad_middle + scale_one * (
         scaled_one - unit_one * jnp.mean(scaled_one * unit_one, axis=1, keepdims=True)
     )

time: 1330 us -> 1230 us (0.925); the launches traced: 1330 us -> 1210 us
  waiting for transfers between devices: 582 us -> 366 us
  starting transfers between devices: 54.5 us -> 99.4 us
  other arithmetic: 102 us -> 132 us
  matrix products: 41.5 us -> 59.1 us
    ppermute x64 -> x66, waiting for transfers between devices: 511 us -> 302 us  [shift(): lax.ppermute(value, axis, [(i, (i + steps) % size) for i in range(size)])]
    ppermute x64 -> x66, starting transfers between devices: 53.6 us -> 98.2 us  [shift(): lax.ppermute(value, axis, [(i, (i + steps) % size) for i in range(size)])]
    reduce_scatter x4, waiting for transfers between devices: 0.04 us -> 44.2 us  [scatter_whole(): return lax.psum_scatter(terms, ('y', 'z'), scatter_dimension=0, tiled=True)]
    all_gather x3, waiting for transfers between devices: 33.8 us -> 0.03 us  [gather_column(): return lax.all_gather(unit, 'z', axis=0, tiled=True)]
    convert_element_type x2 -> x11, other arithmetic: 3.34 us -> 26.9 us  [the longest x2 8.97 us: body(): from_beside = shift(beside_sum.astype(bf16), 'x', 1)]
    dot_general x8 -> x10, matrix products: 41.5 us -> 59.1 us  [contract(): lax.dot_general(left, right, (((left_dim,), (right_dim,)), ((), ())), pre...]
    reduce_scatter x1, waiting for transfers between devices: 36.9 us -> 19.6 us  [scatter_column(): return lax.psum_scatter(total, 'z', scatter_dimension=0, tiled=True)]
    pallas_call x2 -> x4, Pallas kernels: 178 us -> 168 us  [the longest x2 89.2 us: attention_bwd(): pl.pallas_call(functools.partial(attention_bwd_body, chunk, blocks, part,...]
  transfers between devices with their start and end apart: 74 -> 76, of which waited for: 36 -> 31; matrix products, arithmetic and copies ran while one was open for 16% -> 22% of each run, Pallas kernels for 33% -> 35%
where the time goes in v2:
time: 1230 us; the launch traced here: 1210 us
  Pallas kernels  427 us (35%)
  waiting for transfers between devices  366 us (30%)
  other arithmetic  132 us (11%)
  local copies, waits for them, and re-layouts  106 us (9%)
  starting transfers between devices  99.4 us (8%)
  matrix products  59.1 us (5%)
  between operations  17.8 us (1%)
    ppermute x66, waiting for transfers between devices, shift(): lax.ppermute(value, axis, [(i, (i + steps) % size) for i in range(size)])  302 us
    ppermute x66, starting transfers between devices, shift(): lax.ppermute(value, axis, [(i, (i + steps) % size) for i in range(size)])  98.2 us
    pallas_call x2, Pallas kernels, attention_bwd(): pl.pallas_call(functools.partial(attention_bwd_body, chunk, blocks, part,...  89.2 us
    pallas_call x3, Pallas kernels, columns_product(): pl.pallas_call(kernel, grid_spec=pltpu.PrefetchScalarGridSpec(num_scalar_...  86.2 us
    pallas_call x3, Pallas kernels, rows_product(): pl.pallas_call(kernel, grid=(n // bn, t // bm), in_specs=[pl.BlockSpec((b...  80.8 us
    pallas_call x2, Pallas kernels, attention_fwd(): pl.pallas_call(functools.partial(attention_fwd_body, chunk, blocks, part)...  79.3 us
    pallas_call x4, Pallas kernels, turned_product(): pl.pallas_call(kernel, grid=(n // bn, t // bm), in_specs=[pl.BlockSpec((b...  75.1 us
    dot_general x10, matrix products, contract(): lax.dot_general(left, right, (((left_dim,), (right_dim,)), ((), ())), pre...  59.1 us
  transfers between devices with their start and end apart: 76, of which 31 were waited for; matrix products, arithmetic and copies ran while one was open for 22% of the time, Pallas kernels for 35%

profile of v2, /device:TPU:0, one launch (start us, length us, event | category | flops | bytes accessed | tf_op | source)
XLA Modules:
  0.0 1208.8 jit_solution(17049060020048021493)
XLA Ops:
  65.0 19.0 %collective-permute-done.5 = bf16[64,12288]{1,0:T(8,128)(2,1)} collective-permute-done((bf16[64,12288]{1,0:T(8,128)(2,1)}, bf16[64,12288]{1,0:T(8,128)(2,1)}, u32[]{:S(2)}, u32[]{:S(2)}) %collective-permute-start.5) | collective-permute-done | bytes 1572896 | tf_op jit(solution)/shard_map/ppermute | solution.py:38
  90.2 38.5 %collective-permute-done.13.refs_1_ = bf16[512,2048]{1,0:T(8,128)(2,1)} collective-permute-done((bf16[512,2048]{1,0:T(8,128)(2,1)}, bf16[512,2048]{1,0:T(8,128)(2,1)}, u32[]{:S(2)}, u32[]{:S(2)}) %collective-permute-start.13) | collective-permute-done | bytes 2097184 | tf_op jit(solution)/shard_map/ppermute | solution.py:38
  154.9 26.4 %collective-permute-done.4 = bf16[1024,768]{1,0:T(8,128)(2,1)S(1)} collective-permute-done((bf16[1024,768]{1,0:T(8,128)(2,1)}, bf16[1024,768]{1,0:T(8,128)(2,1)S(1)}, u32[]{:S(2)}, u32[]{:S(2)}) %collective-permute-start.4) | collective-permute-done | bytes 1572896 | tf_op jit(solution)/shard_map/ppermute | solution.py:38
  202.1 16.5 %collective-permute-done.17 = bf16[256,2048]{1,0:T(8,128)(2,1)} collective-permute-done((bf16[256,2048]{1,0:T(8,128)(2,1)}, bf16[256,2048]{1,0:T(8,128)(2,1)}, u32[]{:S(2)}, u32[]{:S(2)}) %collective-permute-start.17) | collective-permute-done | bytes 1048608 | tf_op jit(solution)/shard_map/ppermute | solution.py:38
  221.4 47.6 %attention_forward.2 = (bf16[512,1024]{1,0:T(8,128)(2,1)}, f32[2,4,1024]{2,1,0:T(4,128)}) custom-call(s32[2,4]{1,0:T(2,128)} %get-tuple-element.88.qpos_ref, s32[2,8]{1,0:T(2,128)} %stack.77.kpos_ref, s32[2]{0:T(128)} %pad_add_fusion.2.len_ref, bf16[512,2048]{1,0:T(8,128)(2,1)} %bitcast.78, bf16[2,128,2048]{2,1,0:T(8,128)(2,1)} %get-tuple-element.109.k_ref, ...), custom_call_target="tpu_custom_call" | custom-call | flops 34359738368 | bytes 4194304 | tf_op jit(solution)/shard_map/attention_forward/pallas_call | solution.py:417
  298.5 31.7 %attention_forward.3 = (bf16[512,1024]{1,0:T(8,128)(2,1)}, f32[2,4,1024]{2,1,0:T(4,128)}) custom-call(s32[2,4]{1,0:T(2,128)} %get-tuple-element.88.qpos_ref, s32[2,8]{1,0:T(2,128)} %stack.77.kpos_ref, s32[2]{0:T(128)} %pad_add_fusion.2.len_ref, bf16[512,2048]{1,0:T(8,128)(2,1)} %bitcast.79, bf16[2,128,2048]{2,1,0:T(8,128)(2,1)} %get-tuple-element.109.k_ref, ...), custom_call_target="tpu_custom_call" | custom-call | flops 34359738368 | bytes 4194304 | tf_op jit(solution)/shard_map/attention_forward/pallas_call | solution.py:417
  333.0 31.4 %collective-permute-done.22 = bf16[512,2048]{1,0:T(8,128)(2,1)} collective-permute-done((bf16[512,2048]{1,0:T(8,128)(2,1)}, bf16[512,2048]{1,0:T(8,128)(2,1)}, u32[]{:S(2)}, u32[]{:S(2)}) %collective-permute-start.22) | collective-permute-done | bytes 2097184 | tf_op jit(solution)/shard_map/ppermute | solution.py:38
  381.2 45.7 %collective-permute-done.25 = bf16[512,2048]{1,0:T(8,128)(2,1)} collective-permute-done((bf16[512,2048]{1,0:T(8,128)(2,1)}, bf16[512,2048]{1,0:T(8,128)(2,1)}, u32[]{:S(2)}, u32[]{:S(2)}) %collective-permute-start.25) | collective-permute-done | bytes 2097184 | tf_op jit(solution)/shard_map/ppermute | solution.py:38
  456.8 23.7 %gate.1.refs_3_ = bf16[2048,2048]{1,0:T(8,128)(2,1)} custom-call(bf16[2048,2048]{1,0:T(8,128)(2,1)} %pad_maximum_fusion.1.refs_0_.left_ref, bf16[1024,2048]{1,0:T(8,128)(2,1)} %hold.18.refs_1_.refs_2_, bf16[1024,2048]{1,0:T(8,128)(2,1)} %copy-done.34), custom_call_target="tpu_custom_call" | custom-call | flops 17179869184 | bytes 25165824 | tf_op jit(solution)/shard_map/gate/pallas_call | solution.py:241
  489.0 26.5 %up.1 = (bf16[2048,2048]{1,0:T(8,128)(2,1)}, bf16[2048,2048]{1,0:T(8,128)(2,1)}) custom-call(bf16[2048,2048]{1,0:T(8,128)(2,1)} %pad_maximum_fusion.1.refs_0_.left_ref, bf16[1024,2048]{1,0:T(8,128)(2,1)} %get-tuple-element.92.refs_1_.refs_3_, bf16[1024,2048]{1,0:T(8,128)(2,1)} %get-tuple-element.91.refs_2_.refs_3_, bf16[2048,2048]{1,0:T(8,128)(2,1)} %gate.1.refs_3_), custom_call_target="tpu_custom_call" | custom-call | flops 17179869184 | bytes 25165824 | tf_op jit(solution)/shard_map/up/pallas_call | solution.py:241
  515.5 28.6 %down_grad.1 = bf16[2048,2048]{1,0:T(8,128)(2,1)} custom-call(s32[2]{0:T(128)} %and_select_fusion.slots_ref, bf16[2048,2048]{1,0:T(8,128)(2,1)} %pad_maximum_fusion.2.left_ref.refs_0_, bf16[2048,2048]{1,0:T(8,128)(2,1)} %get-tuple-element.67.right_ref.refs_0_), custom_call_target="tpu_custom_call" | custom-call | flops 17179869184 | bytes 20971520 | tf_op jit(solution)/shard_map/down_grad/pallas_call | solution.py:305
  552.7 30.6 %hidden_grad.1 = (bf16[2048,2048]{1,0:T(8,128)(2,1)}, bf16[2048,2048]{1,0:T(8,128)(2,1)}) custom-call(bf16[2048,2048]{1,0:T(8,128)(2,1)} %pad_maximum_fusion.2.left_ref.refs_0_, bf16[1024,2048]{1,0:T(8,128)(2,1)} %get-tuple-element.90.refs_1_, bf16[1024,2048]{1,0:T(8,128)(2,1)} %get-tuple-element.89.refs_2_.refs_1_, bf16[2048,2048]{1,0:T(8,128)(2,1)} %gate.1.refs_3_, ...), custom_call_target="tpu_custom_call" | custom-call | flops 17179869184 | bytes 25165824 | tf_op jit(solution)/shard_map/hidden_grad/pallas_call | solution.py:241
  583.3 24.3 %norm_grad.2 = bf16[2048,1024]{1,0:T(8,128)(2,1)} custom-call(bf16[2048,2048]{1,0:T(8,128)(2,1)} %get-tuple-element.59.refs_0_.right_ref, bf16[2048,2048]{1,0:T(8,128)(2,1)} %get-tuple-element.58.refs_1_.right_ref, bf16[1024,2048]{1,0:T(8,128)(2,1)} %hold.18.refs_1_.refs_2_, bf16[1024,2048]{1,0:T(8,128)(2,1)} %get-tuple-element.92.refs_1_.refs_3_), custom_call_target="tpu_custom_call" | custom-call | flops 17179869184 | bytes 25165824 | tf_op jit(solution)/shard_map/norm_grad/pallas_call | solution.py:270
  607.6 23.9 %norm_grad.3 = bf16[2048,1024]{1,0:T(8,128)(2,1)} custom-call(bf16[2048,2048]{1,0:T(8,128)(2,1)} %get-tuple-element.59.refs_0_.right_ref, bf16[2048,2048]{1,0:T(8,128)(2,1)} %get-tuple-element.58.refs_1_.right_ref, bf16[1024,2048]{1,0:T(8,128)(2,1)} %copy-done.34, bf16[1024,2048]{1,0:T(8,128)(2,1)} %get-tuple-element.91.refs_2_.refs_3_), custom_call_target="tpu_custom_call" | custom-call | flops 17179869184 | bytes 25165824 | tf_op jit(solution)/shard_map/norm_grad/pallas_call | solution.py:270
  631.5 29.0 %gate_grad.1 = bf16[2048,2048]{1,0:T(8,128)(2,1)} custom-call(s32[2]{0:T(128)} %and_select_fusion.slots_ref, bf16[2048,2048]{1,0:T(8,128)(2,1)} %pad_maximum_fusion.1.refs_0_.left_ref, bf16[2048,2048]{1,0:T(8,128)(2,1)} %get-tuple-element.59.refs_0_.right_ref), custom_call_target="tpu_custom_call" | custom-call | flops 17179869184 | bytes 20971520 | tf_op jit(solution)/shard_map/gate_grad/pallas_call | solution.py:305
  674.6 28.6 %up_grad.1 = bf16[2048,2048]{1,0:T(8,128)(2,1)} custom-call(s32[2]{0:T(128)} %and_select_fusion.slots_ref, bf16[2048,2048]{1,0:T(8,128)(2,1)} %pad_maximum_fusion.1.refs_0_.left_ref, bf16[2048,2048]{1,0:T(8,128)(2,1)} %get-tuple-element.58.refs_1_.right_ref), custom_call_target="tpu_custom_call" | custom-call | flops 17179869184 | bytes 20971520 | tf_op jit(solution)/shard_map/up_grad/pallas_call | solution.py:305
  736.5 35.7 %attention_backward.2 = (f32[512,1024]{1,0:T(8,128)}, f32[2,128,2048]{2,1,0:T(8,128)}, f32[2,128,2048]{2,1,0:T(8,128)}) custom-call(s32[2,4]{1,0:T(2,128)} %get-tuple-element.88.qpos_ref, s32[2,8]{1,0:T(2,128)} %stack.77.kpos_ref, s32[2]{0:T(128)} %pad_add_fusion.2.len_ref, bf16[512,2048]{1,0:T(8,128)(2,1)} %bitcast.80, ...), custom_call_target="tpu_custom_call" | custom-call | flops 42949672960 | bytes 14680064 | tf_op jit(solution)/shard_map/attention_backward/pallas_call | solution.py:543
  817.2 18.9 %collective-permute-start.37 = (bf16[512,1024]{1,0:T(8,128)(2,1)}, bf16[512,1024]{1,0:T(8,128)(2,1)S(1)}, u32[]{:S(2)}, u32[]{:S(2)}) collective-permute-start(bf16[512,1024]{1,0:T(8,128)(2,1)} %add_convert_fusion.2), channel_id=1, source_target_pairs={{0,1},{1,0},{2,3},{3,2},{4,5},{5,4},{6,7},{7,6},{8,9},{9,8},{10,11... | collective-permute-start | bytes 3145736 | tf_op jit(solution)/shard_map/ppermute | solution.py:38
  851.3 53.5 %attention_backward.3 = (f32[512,1024]{1,0:T(8,128)}, bf16[2,128,2048]{2,1,0:T(8,128)(2,1)}, bf16[2,128,2048]{2,1,0:T(8,128)(2,1)}) custom-call(s32[2,4]{1,0:T(2,128)} %get-tuple-element.88.qpos_ref, s32[2,8]{1,0:T(2,128)} %stack.77.kpos_ref, s32[2]{0:T(128)} %pad_add_fusion.2.len_ref, bf16[512,2048]{1,0:T(8,128)(2,1)} %bitcast.81, ...), custom_call_target="tpu_custom_call" | custom-call | flops 42949672960 | bytes 14680064 | tf_op jit(solution)/shard_map/attention_backward/pallas_call | solution.py:543
  922.4 32.7 %collective-permute-done.42 = bf16[256,2048]{1,0:T(8,128)(2,1)S(1)} collective-permute-done((bf16[256,2048]{1,0:T(8,128)(2,1)S(1)}, bf16[256,2048]{1,0:T(8,128)(2,1)S(1)}, u32[]{:S(2)}, u32[]{:S(2)}) %collective-permute-start.42) | collective-permute-done | bytes 1048608 | tf_op jit(solution)/shard_map/ppermute | solution.py:38
  987.4 23.3 %collective-permute-done.51 = bf16[1024,768]{1,0:T(8,128)(2,1)} collective-permute-done((bf16[1024,768]{1,0:T(8,128)(2,1)}, bf16[1024,768]{1,0:T(8,128)(2,1)}, u32[]{:S(2)}, u32[]{:S(2)}) %collective-permute-start.51) | collective-permute-done | bytes 1572896 | tf_op jit(solution)/shard_map/ppermute | solution.py:38
  1046.7 19.6 %reduce-scatter.12.cloned.1.call-done = bf16[256,768]{1,0:T(8,128)(2,1)} async-done(((bf16[1024,768]{1,0:T(8,128)(2,1)}), bf16[256,768]{1,0:T(8,128)(2,1)}) %reduce-scatter.12.cloned.1.call-update) | async-done | bytes 393232 | tf_op jit(solution)/shard_map/reduce_scatter | solution.py:124
  1081.1 16.0 %collective-permute-done.53 = bf16[64,1536]{1,0:T(8,128)(2,1)S(1)} collective-permute-done((bf16[64,1536]{1,0:T(8,128)(2,1)S(1)}, bf16[64,1536]{1,0:T(8,128)(2,1)S(1)}, u32[]{:S(2)}, u32[]{:S(2)}) %collective-permute-start.53) | collective-permute-done | bytes 196640 | tf_op jit(solution)/shard_map/ppermute | solution.py:38
  1158.4 33.7 %reduce-scatter.14.cloned.1.call-done = bf16[256,512]{1,0:T(8,128)(2,1)} async-done(((bf16[2048,512]{1,0:T(8,128)(2,1)}), bf16[256,512]{1,0:T(8,128)(2,1)}) %reduce-scatter.14.cloned.1.call-update) | async-done | bytes 262160 | tf_op jit(solution)/shard_map/reduce_scatter | solution.py:120
  (504 shorter events, 485.7 us)
Async XLA Ops:
  7.2 121.5 %all-gather.8.cloned.1.call-start = ((), (), s32[]{:S(2)}) async-start(), calls=%async_computation.6 | async-start | bytes 1310720 | tf_op jit(solution)/shard_map/all_gather | solution.py:101
  63.6 65.1 %collective-permute-start.13 = (bf16[512,2048]{1,0:T(8,128)(2,1)}, bf16[512,2048]{1,0:T(8,128)(2,1)}, u32[]{:S(2)}, u32[]{:S(2)}) collective-permute-start(bf16[512,2048]{1,0:T(8,128)(2,1)} %fusion.4.refs_1_), channel_id=1, source_target_pairs={{0,1},{1,0},{2,3},{3,2},{4,5},{5,4},{6,7},{7,6},{8,9},{9,8},{10,11... | collective-permute-start | bytes 6291464 | tf_op jit(solution)/shard_map/ppermute | solution.py:38
  64.9 79.7 %all-gather.6.cloned.1.call-start = ((), (), s32[]{:S(2)}) async-start(), calls=%async_computation.5 | async-start | bytes 1966080 | tf_op jit(solution)/shard_map/all_gather | solution.py:101
  90.1 194.9 %all-gather.10.cloned.1.call-start = ((), (), s32[]{:S(2)}) async-start(), calls=%async_computation.7 | async-start | bytes 5242880 | tf_op jit(solution)/shard_map/all_gather | solution.py:101
  134.0 346.5 %all-gather.12.cloned.1.call-start = ((), (), s32[]{:S(2)}) async-start(), calls=%async_computation.8 | async-start | bytes 9437184 | tf_op jit(solution)/shard_map/all_gather | solution.py:115
  134.6 409.6 %all-gather.14.cloned.1.call-start = ((), (), s32[]{:S(2)}) async-start(), calls=%async_computation.10 | async-start | bytes 9437184 | tf_op jit(solution)/shard_map/all_gather | solution.py:115
  196.2 72.7 %collective-permute-start.16 = (bf16[1024,512]{1,0:T(8,128)(2,1)}, bf16[1024,512]{1,0:T(8,128)(2,1)}, u32[]{:S(2)}, u32[]{:S(2)}) collective-permute-start(bf16[1024,512]{1,0:T(8,128)(2,1)} %hold.15.refs_1_), channel_id=1, source_target_pairs={{0,2},{2,0},{1,3},{3,1},{4,6},{6,4},{5,7},{7,5},{8,10},{10,8},{9,1... | collective-permute-start | bytes 3145736 | tf_op jit(solution)/shard_map/ppermute | solution.py:38
  200.6 76.1 %collective-permute-start.19 = (bf16[512,2048]{1,0:T(8,128)(2,1)}, bf16[512,2048]{1,0:T(8,128)(2,1)}, u32[]{:S(2)}, u32[]{:S(2)}) collective-permute-start(bf16[512,2048]{1,0:T(8,128)(2,1)} %hold.16), channel_id=1, source_target_pairs={{0,1},{1,0},{2,3},{3,2},{4,5},{5,4},{6,7},{7,6},{8,9},{9,8},{10,11... | collective-permute-start | bytes 6291464 | tf_op jit(solution)/shard_map/ppermute | solution.py:38
  277.3 459.2 %reduce-scatter.6.cloned.1.call-start = ((), (), s32[]{:S(2)}) async-start(), calls=%async_computation.9 | async-start | bytes 9437184 | tf_op jit(solution)/shard_map/reduce_scatter | solution.py:120
  285.0 48.0 %collective-permute-start.21 = (bf16[512,2048]{1,0:T(8,128)(2,1)}, bf16[512,2048]{1,0:T(8,128)(2,1)}, u32[]{:S(2)}, u32[]{:S(2)}) collective-permute-start(bf16[512,2048]{1,0:T(8,128)(2,1)} %add_convert_fusion), channel_id=1, source_target_pairs={{0,1},{1,0},{2,3},{3,2},{4,5},{5,4},{6,7},{7,6},{8,9},{9,8},{10,11... | collective-permute-start | bytes 6291464 | tf_op jit(solution)/shard_map/ppermute | solution.py:38
  289.9 74.5 %collective-permute-start.22 = (bf16[512,2048]{1,0:T(8,128)(2,1)}, bf16[512,2048]{1,0:T(8,128)(2,1)}, u32[]{:S(2)}, u32[]{:S(2)}) collective-permute-start(bf16[512,2048]{1,0:T(8,128)(2,1)} %get-tuple-element.96), channel_id=1, source_target_pairs={{0,2},{2,0},{1,3},{3,1},{4,6},{6,4},{5,7},{7,5},{8,10},{10,8},{9,1... | collective-permute-start | bytes 6291464 | tf_op jit(solution)/shard_map/ppermute | solution.py:38
  378.9 48.0 %collective-permute-start.25 = (bf16[512,2048]{1,0:T(8,128)(2,1)}, bf16[512,2048]{1,0:T(8,128)(2,1)}, u32[]{:S(2)}, u32[]{:S(2)}) collective-permute-start(bf16[512,2048]{1,0:T(8,128)(2,1)} %multiply_convert_fusion), channel_id=1, source_target_pairs={{0,1},{1,0},{2,3},{3,2},{4,5},{5,4},{6,7},{7,6},{8,9},{9,8},{10,11... | collective-permute-start | bytes 6291464 | tf_op jit(solution)/shard_map/ppermute | solution.py:38
  380.4 47.0 %collective-permute-start.28 = (bf16[512,2048]{1,0:T(8,128)(2,1)S(1)}, bf16[512,2048]{1,0:T(8,128)(2,1)}, u32[]{:S(2)}, u32[]{:S(2)}) collective-permute-start(bf16[512,2048]{1,0:T(8,128)(2,1)S(1)} %copy-done.9), channel_id=1, source_target_pairs={{0,4},{4,0},{1,5},{5,1},{2,6},{6,2},{3,7},{7,3},{8,12},{12,8},{9,1... | collective-permute-start | bytes 6291464 | tf_op jit(solution)/shard_map/ppermute | solution.py:38
  380.4 65.9 %collective-permute-start.27 = (bf16[512,2048]{1,0:T(8,128)(2,1)}, bf16[512,2048]{1,0:T(8,128)(2,1)}, u32[]{:S(2)}, u32[]{:S(2)}) collective-permute-start(bf16[512,2048]{1,0:T(8,128)(2,1)} %get-tuple-element.95), channel_id=1, source_target_pairs={{0,2},{2,0},{1,3},{3,1},{4,6},{6,4},{5,7},{7,5},{8,10},{10,8},{9,1... | collective-permute-start | bytes 6291464 | tf_op jit(solution)/shard_map/ppermute | solution.py:38
  381.0 67.2 %collective-permute-start.24 = (bf16[512,2048]{1,0:T(8,128)(2,1)}, bf16[512,2048]{1,0:T(8,128)(2,1)}, u32[]{:S(2)}, u32[]{:S(2)}) collective-permute-start(bf16[512,2048]{1,0:T(8,128)(2,1)} %multiply_convert_fusion), channel_id=1, source_target_pairs={{0,4},{4,0},{1,5},{5,1},{2,6},{6,2},{3,7},{7,3},{8,12},{12,8},{9,1... | collective-permute-start | bytes 6291464 | tf_op jit(solution)/shard_map/ppermute | solution.py:38
  544.1 301.3 %reduce-scatter.8.cloned.1.call-start = ((), (), s32[]{:S(2)}) async-start(), calls=%async_computation.11 | async-start | bytes 9437184 | tf_op jit(solution)/shard_map/reduce_scatter | solution.py:120
  660.4 359.4 %reduce-scatter.10.cloned.1.call-start = ((), (), s32[]{:S(2)}) async-start(), calls=%async_computation.12 | async-start | bytes 9437184 | tf_op jit(solution)/shard_map/reduce_scatter | solution.py:120
  726.9 339.3 %reduce-scatter.12.cloned.1.call-start = ((), (), s32[]{:S(2)}) async-start(), calls=%async_computation.13 | async-start | bytes 1966080 | tf_op jit(solution)/shard_map/reduce_scatter | solution.py:124
  727.4 78.4 %collective-permute-start.39 = (bf16[512,2048]{1,0:T(8,128)(2,1)S(1)}, bf16[512,2048]{1,0:T(8,128)(2,1)}, u32[]{:S(2)}, u32[]{:S(2)}) collective-permute-start(bf16[512,2048]{1,0:T(8,128)(2,1)S(1)} %get-tuple-element.81), channel_id=1, source_target_pairs={{0,1},{1,0},{2,3},{3,2},{4,5},{5,4},{6,7},{7,6},{8,9},{9,8},{10,11... | collective-permute-start | bytes 6291464 | tf_op jit(solution)/shard_map/ppermute | solution.py:38
  817.2 138.5 %collective-permute-start.37 = (bf16[512,1024]{1,0:T(8,128)(2,1)}, bf16[512,1024]{1,0:T(8,128)(2,1)S(1)}, u32[]{:S(2)}, u32[]{:S(2)}) collective-permute-start(bf16[512,1024]{1,0:T(8,128)(2,1)} %add_convert_fusion.2), channel_id=1, source_target_pairs={{0,1},{1,0},{2,3},{3,2},{4,5},{5,4},{6,7},{7,6},{8,9},{9,8},{10,11... | collective-permute-start | bytes 3145736 | tf_op jit(solution)/shard_map/ppermute | solution.py:38
  907.5 47.6 %collective-permute-start.42 = (bf16[256,2048]{1,0:T(8,128)(2,1)S(1)}, bf16[256,2048]{1,0:T(8,128)(2,1)S(1)}, u32[]{:S(2)}, u32[]{:S(2)}) collective-permute-start(bf16[256,2048]{1,0:T(8,128)(2,1)S(1)} %slice_bitcast_fusion), channel_id=1, source_target_pairs={{0,2},{2,0},{1,3},{3,1},{4,6},{6,4},{5,7},{7,5},{8,10},{10,8},{9,1... | collective-permute-start | bytes 3145736 | tf_op jit(solution)/shard_map/ppermute | solution.py:38
  984.4 52.0 %collective-permute-start.43 = (bf16[1024,2048]{1,0:T(8,128)(2,1)}, bf16[1024,2048]{1,0:T(8,128)(2,1)}, u32[]{:S(2)}, u32[]{:S(2)}) collective-permute-start(bf16[1024,2048]{1,0:T(8,128)(2,1)} %slice.542), channel_id=1, source_target_pairs={{0,4},{4,0},{1,5},{5,1},{2,6},{6,2},{3,7},{7,3},{8,12},{12,8},{9,1... | collective-permute-start | bytes 12582920 | tf_op jit(solution)/shard_map/ppermute | solution.py:38
  1019.8 172.3 %reduce-scatter.14.cloned.1.call-start = ((), (), s32[]{:S(2)}) async-start(), calls=%async_computation.14 | async-start | bytes 2359296 | tf_op jit(solution)/shard_map/reduce_scatter | solution.py:120
  1045.1 53.7 %collective-permute-start.44 = (bf16[512,2048]{1,0:T(8,128)(2,1)}, bf16[512,2048]{1,0:T(8,128)(2,1)}, u32[]{:S(2)}, u32[]{:S(2)}) collective-permute-start(bf16[512,2048]{1,0:T(8,128)(2,1)} %fusion.17), channel_id=1, source_target_pairs={{0,1},{1,0},{2,3},{3,2},{4,5},{5,4},{6,7},{7,6},{8,9},{9,8},{10,11... | collective-permute-start | bytes 6291464 | tf_op jit(solution)/shard_map/ppermute | solution.py:38
  (119 other events, 1594.0 us)
Sparse Core Ops, SparseCore 0:
  65.0 28.7 all-gather.7
  95.9 36.5 all-gather.5
  134.1 82.2 all-gather.9
  218.4 147.2 all-gather.11
  367.6 136.4 all-gather.13
  544.2 149.0 reduce-scatter.5
  697.4 147.9 reduce-scatter.7
  849.0 170.7 reduce-scatter.9
  1022.8 43.4 reduce-scatter.11
  1113.1 78.9 reduce-scatter.13

commit v3 on v2

--- a/solution.py
+++ b/solution.py
@@ -337,9 +337,16 @@
     return grad * up * sigmoid * (1.0 + gate * (1.0 - sigmoid)), grad * gate * sigmoid
 
 
+def seen(chunk, first, qp, length):
+    shape = (chunk, REP * chunk)
+    at_key = first + lax.broadcasted_iota(jnp.int32, shape, 0)
+    at_query = qp * chunk + (lax.broadcasted_iota(jnp.int32, shape, 1) & (chunk - 1))
+    return (at_key <= at_query) & (at_key < length)
+
+
 def attention_fwd_body(
     chunk, blocks, part, qpos_ref, kpos_ref, len_ref, q_ref, k_ref, v_ref, o_ref, lse_ref,
-    kn_ref, m_ref, l_ref, acc_ref,
+    kn_ref, q4_ref, m_ref, l_ref, acc_ref,
 ):
     s, qb = pl.program_id(0), pl.program_id(2)
     ys = k_ref.shape[0]
@@ -354,6 +361,8 @@
 
     qp = qpos_ref[s, part * (blocks // 2) + qb]
     length = len_ref[s]
+    for h in range(REP):
+        q4_ref[:, h * chunk : (h + 1) * chunk] = q_ref[h * HD : (h + 1) * HD, :]
     m_ref[...] = jnp.full_like(m_ref, floor_score)
     l_ref[...] = jnp.zeros_like(l_ref)
     acc_ref[...] = jnp.zeros_like(acc_ref)
@@ -369,26 +378,18 @@
             def work(masked):
                 kn = kn_ref[pl.ds(pl.multiple_of((yk * blocks + b) * chunk, chunk), chunk), :]
                 vt = v_ref[yk, :, pl.ds(pl.multiple_of(b * chunk, chunk), chunk)]
+                scores = jnp.dot(kn, q4_ref[...], preferred_element_type=f32)
                 if masked:
-                    at_key = first + lax.broadcasted_iota(jnp.int32, (chunk, chunk), 0)
-                    at_query = qp * chunk + lax.broadcasted_iota(jnp.int32, (chunk, chunk), 1)
-                    allowed = (at_key <= at_query) & (at_key < length)
-                for h in range(REP):
-                    rows = slice(h * HD, (h + 1) * HD)
-                    scores = jnp.dot(kn, q_ref[rows, :], preferred_element_type=f32)
-                    if masked:
-                        scores = jnp.where(allowed, scores, masked_score)
-                    m_old = m_ref[h : h + 1, :]
-                    m_new = jnp.maximum(m_old, jnp.max(scores, axis=0, keepdims=True))
-                    alpha = jnp.exp(m_old - m_new)
-                    probs = jnp.exp(scores - m_new)
-                    m_ref[h : h + 1, :] = m_new
-                    l_ref[h : h + 1, :] = l_ref[h : h + 1, :] * alpha + jnp.sum(
-                        probs, axis=0, keepdims=True
-                    )
-                    acc_ref[rows, :] = acc_ref[rows, :] * alpha + jnp.dot(
-                        vt, probs.astype(bf16), preferred_element_type=f32
-                    )
+                    scores = jnp.where(seen(chunk, first, qp, length), scores, masked_score)
+                m_old = m_ref[...]
+                m_new = jnp.maximum(m_old, jnp.max(scores, axis=0, keepdims=True))
+                alpha = jnp.exp(m_old - m_new)
+                probs = jnp.exp(scores - m_new)
+                m_ref[...] = m_new
+                l_ref[...] = l_ref[...] * alpha + jnp.sum(probs, axis=0, keepdims=True)
+                acc_ref[...] = acc_ref[...] * alpha + jnp.dot(
+                    vt, probs.astype(bf16), preferred_element_type=f32
+                )
 
             pl.when(live & partly)(lambda: work(True))
             pl.when(live & jnp.logical_not(partly))(lambda: work(False))
@@ -396,10 +397,12 @@
 
         lax.fori_loop(0, blocks, step, 0)
 
+    out = (acc_ref[...] / l_ref[...]).astype(bf16)
+    lse = m_ref[...] + jnp.log(l_ref[...])
     for h in range(REP):
-        rows = slice(h * HD, (h + 1) * HD)
-        o_ref[rows, :] = (acc_ref[rows, :] / l_ref[h : h + 1, :]).astype(bf16)
-    lse_ref[0] = m_ref[0:REP, :] + jnp.log(l_ref[0:REP, :])
+        columns = slice(h * chunk, (h + 1) * chunk)
+        o_ref[h * HD : (h + 1) * HD, :] = out[:, columns]
+        lse_ref[0, h : h + 1, :] = lse[:, columns]
 
 
 def attention_fwd(queries, keys, values, qpos, kpos, lengths, chunk, part):
@@ -423,11 +426,13 @@
             out_specs=[o_spec, lse_spec],
             scratch_shapes=[
                 pltpu.VMEM((ys * half, HD), bf16),
-                pltpu.VMEM((8, chunk), f32),
-                pltpu.VMEM((8, chunk), f32),
-                pltpu.VMEM((REP * HD, chunk), f32),
+                pltpu.VMEM((HD, REP * chunk), bf16),
+                pltpu.VMEM((1, REP * chunk), f32),
+                pltpu.VMEM((1, REP * chunk), f32),
+                pltpu.VMEM((HD, REP * chunk), f32),
             ],
         ),
+        compiler_params=pltpu.CompilerParams(vmem_limit_bytes=VMEM_BYTES),
         out_shape=[
             jax.ShapeDtypeStruct((queries.shape[0], half), bf16),
             jax.ShapeDtypeStruct((groups, REP, half), f32),
@@ -446,7 +451,7 @@
     lse_ref, *refs,
 ):
     before = refs[:n_before]
-    dq_ref, dk_ref, dv_ref, kn_ref, vn_ref, dqa_ref, dka_ref, dva_ref, delta_ref = refs[n_before:]
+    dq_ref, dk_ref, dv_ref, kn_ref, vn_ref, q4_ref, do4_ref, dqa_ref, dka_ref, dva_ref, row_ref = refs[n_before:]
     s, qb = pl.program_id(0), pl.program_id(2)
     ys = k_ref.shape[0]
 
@@ -469,8 +474,11 @@
     length = len_ref[s]
     dqa_ref[...] = jnp.zeros_like(dqa_ref)
     for h in range(REP):
-        rows = slice(h * HD, (h + 1) * HD)
-        delta_ref[h : h + 1, :] = jnp.sum(
+        rows, columns = slice(h * HD, (h + 1) * HD), slice(h * chunk, (h + 1) * chunk)
+        q4_ref[:, columns] = q_ref[rows, :]
+        do4_ref[:, columns] = do_ref[rows, :]
+        row_ref[0:1, columns] = lse_ref[0, h : h + 1, :]
+        row_ref[1:2, columns] = jnp.sum(
             do_ref[rows, :].astype(f32) * o_ref[rows, :].astype(f32), axis=0, keepdims=True
         )
 
@@ -485,33 +493,21 @@
             def work(masked):
                 at = pl.ds(pl.multiple_of((yk * blocks + b) * chunk, chunk), chunk)
                 cols = pl.ds(pl.multiple_of(b * chunk, chunk), chunk)
-                kn, vn = kn_ref[at, :], vn_ref[at, :]
-                kt = k_ref[yk, :, cols]
+                q4, do4 = q4_ref[...], do4_ref[...]
+                scores = jnp.dot(kn_ref[at, :], q4, preferred_element_type=f32)
                 if masked:
-                    at_key = first + lax.broadcasted_iota(jnp.int32, (chunk, chunk), 0)
-                    at_query = qp * chunk + lax.broadcasted_iota(jnp.int32, (chunk, chunk), 1)
-                    allowed = (at_key <= at_query) & (at_key < length)
-                dk = dka_ref[yk, :, cols]
-                dv = dva_ref[yk, :, cols]
-                for h in range(REP):
-                    rows = slice(h * HD, (h + 1) * HD)
-                    qt, dot = q_ref[rows, :], do_ref[rows, :]
-                    scores = jnp.dot(kn, qt, preferred_element_type=f32)
-                    if masked:
-                        scores = jnp.where(allowed, scores, masked_score)
-                    probs = jnp.exp(scores - lse_ref[0, h : h + 1, :])
-                    grad_probs = jnp.dot(vn, dot, preferred_element_type=f32)
-                    grad_scores = (probs * (grad_probs - delta_ref[h : h + 1, :])).astype(bf16)
-                    dqa_ref[rows, :] += jnp.dot(kt, grad_scores, preferred_element_type=f32)
-                    dk += lax.dot_general(
-                        qt, grad_scores, (((1,), (1,)), ((), ())), preferred_element_type=f32
-                    )
-                    dv += lax.dot_general(
-                        dot, probs.astype(bf16), (((1,), (1,)), ((), ())),
-                        preferred_element_type=f32,
-                    )
-                dka_ref[yk, :, cols] = dk
-                dva_ref[yk, :, cols] = dv
+                    scores = jnp.where(seen(chunk, first, qp, length), scores, masked_score)
+                probs = jnp.exp(scores - row_ref[0:1, :])
+                grad_probs = jnp.dot(vn_ref[at, :], do4, preferred_element_type=f32)
+                grad_scores = (probs * (grad_probs - row_ref[1:2, :])).astype(bf16)
+                across = (((1,), (1,)), ((), ()))
+                dva_ref[yk, :, cols] += lax.dot_general(
+                    do4, probs.astype(bf16), across, preferred_element_type=f32
+                )
+                dqa_ref[...] += jnp.dot(k_ref[yk, :, cols], grad_scores, preferred_element_type=f32)
+                dka_ref[yk, :, cols] += lax.dot_general(
+                    q4, grad_scores, across, preferred_element_type=f32
+                )
 
             pl.when(live & partly)(lambda: work(True))
             pl.when(live & jnp.logical_not(partly))(lambda: work(False))
@@ -519,7 +515,8 @@
 
         lax.fori_loop(0, blocks, step, 0)
 
-    dq_ref[...] = dqa_ref[...] * 0.125
+    for h in range(REP):
+        dq_ref[h * HD : (h + 1) * HD, :] = dqa_ref[:, h * chunk : (h + 1) * chunk] * 0.125
 
     @pl.when(qb == blocks // 2 - 1)
     def _():
@@ -550,10 +547,12 @@
             scratch_shapes=[
                 pltpu.VMEM((ys * half, HD), bf16),
                 pltpu.VMEM((ys * half, HD), bf16),
-                pltpu.VMEM((REP * HD, chunk), f32),
+                pltpu.VMEM((HD, REP * chunk), bf16),
+                pltpu.VMEM((HD, REP * chunk), bf16),
+                pltpu.VMEM((HD, REP * chunk), f32),
                 pltpu.VMEM((ys, HD, half), f32),
                 pltpu.VMEM((ys, HD, half), f32),
-                pltpu.VMEM((8, chunk), f32),
+                pltpu.VMEM((2, REP * chunk), f32),
             ],
         ),
         out_shape=[
@@ -758,7 +757,7 @@
     down_own, down_got = join_by_c(hold(down_grad, query_zero), c)
     grad_attn = contract(out_w, jnp.concatenate([both_two, after(beside, last)], axis=0), 0, 1).astype(bf16)
     query_one, grad_keys, grad_values = attention_bwd(
-        after(queries, gate_grad, down_got, *got_c), keys, values, attended_one, grad_attn, lse_one, qpos,
+        after(queries, down_got, *got_c), keys, values, attended_one, grad_attn, lse_one, qpos,
         kpos, lengths, chunk, 1, grad_keys, grad_values,
     )
     got_x = [
@@ -766,7 +765,7 @@
         for part, got in zip(branch_parts, got_c)
     ]
     down_own, down_got = join_by_x(down_own, down_got, c, x)
-    query_one = after(query_one, down_got, *got_x)
+    query_one = after(query_one, gate_grad, down_got, *got_x)
     down_grad = in_order(down_own, down_got, x, 1)
     branch_two = jnp.concatenate(
         [
@@ -801,16 +800,16 @@
     qkv_sent = send_slots([attn_terms(normed_one, grad_qkv, k).astype(bf16) for k in range(1, ys)])
     partial = contract(grad_qkv, qkv_w, 0, 1).astype(bf16)
     mine, beside_sum = scatter_by_c(partial, True)
-    from_beside = shift(beside_sum.astype(bf16), "x", 1)
-    output_grad = scatter_whole(
-        jnp.concatenate(
-            [attn_terms(hold(grad_branch, from_beside), attended, by_y[i]) for i in range(ys)], axis=0
-        ).astype(bf16)
-    )
+    beside_sum = beside_sum.astype(bf16)
+    from_beside = shift(beside_sum, "x", 1)
     gate_grad = finish(hold(gate_grad, from_beside))
     grad_norm_one = mine + from_beside.astype(f32)
+    held = hold(attended, from_beside)
+    output_grad = scatter_whole(
+        jnp.concatenate([attn_terms(grad_branch, held, by_y[i]) for i in range(ys)], axis=0).astype(bf16)
+    )
     qkv_grad = sum([attn_terms(normed_one, grad_qkv, 0)] + [t.astype(f32) for t in qkv_sent])
-    qkv_grad = scatter_column(hold(qkv_grad.astype(bf16), up_grad))
+    qkv_grad = scatter_column(hold(qkv_grad.astype(bf16), up_grad, beside_sum))
     gain_one_grad = jnp.sum(grad_norm_one * unit_one, axis=0)
     scaled_one = grad_norm_one * gain_one
     up_grad = finish(hold(up_grad, from_beside))

time: 1230 us -> 1180 us (0.959); the launches traced: 1210 us -> 1180 us
  Pallas kernels: 427 us -> 390 us
    ppermute x66, waiting for transfers between devices: 302 us -> 339 us  [shift(): lax.ppermute(value, axis, [(i, (i + steps) % size) for i in range(size)])]
    pallas_call x2, Pallas kernels: 79.3 us -> 53.8 us  [attention_fwd(): pl.pallas_call(functools.partial(attention_fwd_body, chunk, blocks, part)...]
    reduce_scatter x4, waiting for transfers between devices: 44.2 us -> 22.6 us  [scatter_whole(): return lax.psum_scatter(terms, ('y', 'z'), scatter_dimension=0, tiled=True)]
    reduce_scatter x1, waiting for transfers between devices: 19.6 us -> 0.01 us  [scatter_column(): return lax.psum_scatter(total, 'z', scatter_dimension=0, tiled=True)]
    pallas_call x2, Pallas kernels: 89.2 us -> 76.5 us  [attention_bwd(): pl.pallas_call(functools.partial(attention_bwd_body, chunk, blocks, part,...]
    unnamed x166 -> x177, local copies, waits for them, and re-layouts: 41.2 us -> 47 us
  transfers between devices with their start and end apart: 76 -> 76, of which waited for: 31 -> 32; matrix products, arithmetic and copies ran while one was open for 22% -> 24% of each run, Pallas kernels for 35% -> 33%
where the time goes in v3:
time: 1180 us
  Pallas kernels  390 us (33%)
  waiting for transfers between devices  363 us (31%)
  other arithmetic  136 us (12%)
  local copies, waits for them, and re-layouts  113 us (10%)
  starting transfers between devices  91 us (8%)
  matrix products  64.5 us (5%)
  between operations  17.9 us (2%)
    ppermute x66, waiting for transfers between devices, shift(): lax.ppermute(value, axis, [(i, (i + steps) % size) for i in range(size)])  339 us
    ppermute x66, starting transfers between devices, shift(): lax.ppermute(value, axis, [(i, (i + steps) % size) for i in range(size)])  90.2 us
    pallas_call x3, Pallas kernels, columns_product(): pl.pallas_call(kernel, grid_spec=pltpu.PrefetchScalarGridSpec(num_scalar_...  86.3 us
    pallas_call x3, Pallas kernels, rows_product(): pl.pallas_call(kernel, grid=(n // bn, t // bm), in_specs=[pl.BlockSpec((b...  80.8 us
    pallas_call x2, Pallas kernels, attention_bwd(): pl.pallas_call(functools.partial(attention_bwd_body, chunk, blocks, part,...  76.5 us
    pallas_call x4, Pallas kernels, turned_product(): pl.pallas_call(kernel, grid=(n // bn, t // bm), in_specs=[pl.BlockSpec((b...  75.5 us
    dot_general x10, matrix products, contract(): lax.dot_general(left, right, (((left_dim,), (right_dim,)), ((), ())), pre...  64.5 us
    pallas_call x2, Pallas kernels, attention_fwd(): pl.pallas_call(functools.partial(attention_fwd_body, chunk, blocks, part)...  53.8 us
  transfers between devices with their start and end apart: 76, of which 32 were waited for; matrix products, arithmetic and copies ran while one was open for 24% of the time, Pallas kernels for 33%

profile of v3, /device:TPU:0, one launch (start us, length us, event | category | flops | bytes accessed | tf_op | source)
XLA Modules:
  0.0 1175.8 jit_solution(1685531138079491849)
XLA Ops:
  68.8 19.0 %collective-permute-done.5 = bf16[64,12288]{1,0:T(8,128)(2,1)} collective-permute-done((bf16[64,12288]{1,0:T(8,128)(2,1)}, bf16[64,12288]{1,0:T(8,128)(2,1)}, u32[]{:S(2)}, u32[]{:S(2)}) %collective-permute-start.5) | collective-permute-done | bytes 1572896 | tf_op jit(solution)/shard_map/ppermute | solution.py:38
  94.0 38.5 %collective-permute-done.13.refs_1_ = bf16[512,2048]{1,0:T(8,128)(2,1)} collective-permute-done((bf16[512,2048]{1,0:T(8,128)(2,1)}, bf16[512,2048]{1,0:T(8,128)(2,1)}, u32[]{:S(2)}, u32[]{:S(2)}) %collective-permute-start.13) | collective-permute-done | bytes 2097184 | tf_op jit(solution)/shard_map/ppermute | solution.py:38
  158.7 26.4 %collective-permute-done.4 = bf16[1024,768]{1,0:T(8,128)(2,1)S(1)} collective-permute-done((bf16[1024,768]{1,0:T(8,128)(2,1)}, bf16[1024,768]{1,0:T(8,128)(2,1)S(1)}, u32[]{:S(2)}, u32[]{:S(2)}) %collective-permute-start.4) | collective-permute-done | bytes 1572896 | tf_op jit(solution)/shard_map/ppermute | solution.py:38
  205.9 16.6 %collective-permute-done.17 = bf16[256,2048]{1,0:T(8,128)(2,1)} collective-permute-done((bf16[256,2048]{1,0:T(8,128)(2,1)}, bf16[256,2048]{1,0:T(8,128)(2,1)}, u32[]{:S(2)}, u32[]{:S(2)}) %collective-permute-start.17) | collective-permute-done | bytes 1048608 | tf_op jit(solution)/shard_map/ppermute | solution.py:38
  225.2 34.0 %attention_forward.2 = (bf16[512,1024]{1,0:T(8,128)(2,1)}, f32[2,4,1024]{2,1,0:T(4,128)}) custom-call(s32[2,4]{1,0:T(2,128)} %get-tuple-element.88.qpos_ref, s32[2,8]{1,0:T(2,128)} %stack.77.kpos_ref, s32[2]{0:T(128)} %pad_add_fusion.2.len_ref, bf16[512,2048]{1,0:T(8,128)(2,1)} %bitcast.76, bf16[2,128,2048]{2,1,0:T(8,128)(2,1)} %get-tuple-element.109.k_ref, ...), custom_call_target="tpu_custom_call" | custom-call | flops 34359738368 | bytes 4194304 | tf_op jit(solution)/shard_map/attention_forward/pallas_call | solution.py:420
  282.8 19.7 %attention_forward.3 = (bf16[512,1024]{1,0:T(8,128)(2,1)}, f32[2,4,1024]{2,1,0:T(4,128)}) custom-call(s32[2,4]{1,0:T(2,128)} %get-tuple-element.88.qpos_ref, s32[2,8]{1,0:T(2,128)} %stack.77.kpos_ref, s32[2]{0:T(128)} %pad_add_fusion.2.len_ref, bf16[512,2048]{1,0:T(8,128)(2,1)} %bitcast.77, bf16[2,128,2048]{2,1,0:T(8,128)(2,1)} %get-tuple-element.109.k_ref, ...), custom_call_target="tpu_custom_call" | custom-call | flops 34359738368 | bytes 4194304 | tf_op jit(solution)/shard_map/attention_forward/pallas_call | solution.py:420
  302.5 20.4 %collective-permute-done.21 = bf16[512,2048]{1,0:T(8,128)(2,1)} collective-permute-done((bf16[512,2048]{1,0:T(8,128)(2,1)}, bf16[512,2048]{1,0:T(8,128)(2,1)}, u32[]{:S(2)}, u32[]{:S(2)}) %collective-permute-start.21) | collective-permute-done | bytes 2097184 | tf_op jit(solution)/shard_map/ppermute | solution.py:38
  322.9 45.1 %collective-permute-done.22 = bf16[512,2048]{1,0:T(8,128)(2,1)S(1)} collective-permute-done((bf16[512,2048]{1,0:T(8,128)(2,1)S(1)}, bf16[512,2048]{1,0:T(8,128)(2,1)S(1)}, u32[]{:S(2)}, u32[]{:S(2)}) %collective-permute-start.22) | collective-permute-done | bytes 2097184 | tf_op jit(solution)/shard_map/ppermute | solution.py:38
  385.4 45.7 %collective-permute-done.25 = bf16[512,2048]{1,0:T(8,128)(2,1)} collective-permute-done((bf16[512,2048]{1,0:T(8,128)(2,1)}, bf16[512,2048]{1,0:T(8,128)(2,1)}, u32[]{:S(2)}, u32[]{:S(2)}) %collective-permute-start.25) | collective-permute-done | bytes 2097184 | tf_op jit(solution)/shard_map/ppermute | solution.py:38
  454.9 23.7 %gate.1.refs_3_ = bf16[2048,2048]{1,0:T(8,128)(2,1)} custom-call(bf16[2048,2048]{1,0:T(8,128)(2,1)} %pad_maximum_fusion.1.refs_0_.left_ref, bf16[1024,2048]{1,0:T(8,128)(2,1)} %hold.18.refs_1_.refs_2_, bf16[1024,2048]{1,0:T(8,128)(2,1)} %copy-done.39), custom_call_target="tpu_custom_call" | custom-call | flops 17179869184 | bytes 25165824 | tf_op jit(solution)/shard_map/gate/pallas_call | solution.py:241
  487.1 26.7 %up.1 = (bf16[2048,2048]{1,0:T(8,128)(2,1)}, bf16[2048,2048]{1,0:T(8,128)(2,1)}) custom-call(bf16[2048,2048]{1,0:T(8,128)(2,1)} %pad_maximum_fusion.1.refs_0_.left_ref, bf16[1024,2048]{1,0:T(8,128)(2,1)} %get-tuple-element.92.refs_1_.refs_3_, bf16[1024,2048]{1,0:T(8,128)(2,1)} %get-tuple-element.91.refs_2_.refs_3_, bf16[2048,2048]{1,0:T(8,128)(2,1)} %gate.1.refs_3_), custom_call_target="tpu_custom_call" | custom-call | flops 17179869184 | bytes 25165824 | tf_op jit(solution)/shard_map/up/pallas_call | solution.py:241
  513.8 28.7 %down_grad.1 = bf16[2048,2048]{1,0:T(8,128)(2,1)} custom-call(s32[2]{0:T(128)} %and_select_fusion.slots_ref, bf16[2048,2048]{1,0:T(8,128)(2,1)} %pad_maximum_fusion.2.left_ref.refs_0_, bf16[2048,2048]{1,0:T(8,128)(2,1)} %get-tuple-element.67.right_ref.refs_0_), custom_call_target="tpu_custom_call" | custom-call | flops 17179869184 | bytes 20971520 | tf_op jit(solution)/shard_map/down_grad/pallas_call | solution.py:305
  551.2 30.4 %hidden_grad.1 = (bf16[2048,2048]{1,0:T(8,128)(2,1)}, bf16[2048,2048]{1,0:T(8,128)(2,1)}) custom-call(bf16[2048,2048]{1,0:T(8,128)(2,1)} %pad_maximum_fusion.2.left_ref.refs_0_, bf16[1024,2048]{1,0:T(8,128)(2,1)} %get-tuple-element.90.refs_1_, bf16[1024,2048]{1,0:T(8,128)(2,1)} %get-tuple-element.89.refs_2_.refs_1_, bf16[2048,2048]{1,0:T(8,128)(2,1)} %gate.1.refs_3_, ...), custom_call_target="tpu_custom_call" | custom-call | flops 17179869184 | bytes 25165824 | tf_op jit(solution)/shard_map/hidden_grad/pallas_call | solution.py:241
  581.6 24.2 %norm_grad.2 = bf16[2048,1024]{1,0:T(8,128)(2,1)} custom-call(bf16[2048,2048]{1,0:T(8,128)(2,1)} %get-tuple-element.59.refs_0_.right_ref, bf16[2048,2048]{1,0:T(8,128)(2,1)} %get-tuple-element.58.refs_1_.right_ref, bf16[1024,2048]{1,0:T(8,128)(2,1)} %hold.18.refs_1_.refs_2_, bf16[1024,2048]{1,0:T(8,128)(2,1)} %get-tuple-element.92.refs_1_.refs_3_), custom_call_target="tpu_custom_call" | custom-call | flops 17179869184 | bytes 25165824 | tf_op jit(solution)/shard_map/norm_grad/pallas_call | solution.py:270
  605.8 23.9 %norm_grad.3 = bf16[2048,1024]{1,0:T(8,128)(2,1)} custom-call(bf16[2048,2048]{1,0:T(8,128)(2,1)} %get-tuple-element.59.refs_0_.right_ref, bf16[2048,2048]{1,0:T(8,128)(2,1)} %get-tuple-element.58.refs_1_.right_ref, bf16[1024,2048]{1,0:T(8,128)(2,1)} %copy-done.39, bf16[1024,2048]{1,0:T(8,128)(2,1)} %get-tuple-element.91.refs_2_.refs_3_), custom_call_target="tpu_custom_call" | custom-call | flops 17179869184 | bytes 25165824 | tf_op jit(solution)/shard_map/norm_grad/pallas_call | solution.py:270
  629.7 28.9 %gate_grad.1 = bf16[2048,2048]{1,0:T(8,128)(2,1)} custom-call(s32[2]{0:T(128)} %and_select_fusion.slots_ref, bf16[2048,2048]{1,0:T(8,128)(2,1)} %pad_maximum_fusion.1.refs_0_.left_ref, bf16[2048,2048]{1,0:T(8,128)(2,1)} %get-tuple-element.59.refs_0_.right_ref), custom_call_target="tpu_custom_call" | custom-call | flops 17179869184 | bytes 20971520 | tf_op jit(solution)/shard_map/gate_grad/pallas_call | solution.py:305
  673.4 28.7 %up_grad.1 = bf16[2048,2048]{1,0:T(8,128)(2,1)} custom-call(s32[2]{0:T(128)} %and_select_fusion.slots_ref, bf16[2048,2048]{1,0:T(8,128)(2,1)} %pad_maximum_fusion.1.refs_0_.left_ref, bf16[2048,2048]{1,0:T(8,128)(2,1)} %get-tuple-element.58.refs_1_.right_ref), custom_call_target="tpu_custom_call" | custom-call | flops 17179869184 | bytes 20971520 | tf_op jit(solution)/shard_map/up_grad/pallas_call | solution.py:305
  738.7 27.8 %attention_backward.2 = (f32[512,1024]{1,0:T(8,128)}, f32[2,128,2048]{2,1,0:T(8,128)}, f32[2,128,2048]{2,1,0:T(8,128)}) custom-call(s32[2,4]{1,0:T(2,128)} %get-tuple-element.88.qpos_ref, s32[2,8]{1,0:T(2,128)} %stack.77.kpos_ref, s32[2]{0:T(128)} %pad_add_fusion.2.len_ref, bf16[512,2048]{1,0:T(8,128)(2,1)} %bitcast.78, ...), custom_call_target="tpu_custom_call" | custom-call | flops 42949672960 | bytes 14680064 | tf_op jit(solution)/shard_map/attention_backward/pallas_call | solution.py:540
  812.6 21.6 %collective-permute-start.37 = (bf16[512,1024]{1,0:T(8,128)(2,1)}, bf16[512,1024]{1,0:T(8,128)(2,1)}, u32[]{:S(2)}, u32[]{:S(2)}) collective-permute-start(bf16[512,1024]{1,0:T(8,128)(2,1)} %add_convert_fusion.2), channel_id=1, source_target_pairs={{0,1},{1,0},{2,3},{3,2},{4,5},{5,4},{6,7},{7,6},{8,9},{9,8},{10,11... | collective-permute-start | bytes 3145736 | tf_op jit(solution)/shard_map/ppermute | solution.py:38
  839.5 48.7 %attention_backward.3 = (f32[512,1024]{1,0:T(8,128)}, bf16[2,128,2048]{2,1,0:T(8,128)(2,1)}, bf16[2,128,2048]{2,1,0:T(8,128)(2,1)}) custom-call(s32[2,4]{1,0:T(2,128)} %get-tuple-element.88.qpos_ref, s32[2,8]{1,0:T(2,128)} %stack.77.kpos_ref, s32[2]{0:T(128)} %pad_add_fusion.2.len_ref, bf16[512,2048]{1,0:T(8,128)(2,1)} %bitcast.79, ...), custom_call_target="tpu_custom_call" | custom-call | flops 42949672960 | bytes 14680064 | tf_op jit(solution)/shard_map/attention_backward/pallas_call | solution.py:540
  900.9 17.5 %collective-permute-done.42 = bf16[256,2048]{1,0:T(8,128)(2,1)S(1)} collective-permute-done((bf16[256,2048]{1,0:T(8,128)(2,1)S(1)}, bf16[256,2048]{1,0:T(8,128)(2,1)S(1)}, u32[]{:S(2)}, u32[]{:S(2)}) %collective-permute-start.42) | collective-permute-done | bytes 1048608 | tf_op jit(solution)/shard_map/ppermute | solution.py:38
  1022.3 17.8 %collective-permute-done.44.refs_1_ = bf16[512,2048]{1,0:T(8,128)(2,1)} collective-permute-done((bf16[512,2048]{1,0:T(8,128)(2,1)}, bf16[512,2048]{1,0:T(8,128)(2,1)}, u32[]{:S(2)}, u32[]{:S(2)}) %collective-permute-start.44) | collective-permute-done | bytes 2097184 | tf_op jit(solution)/shard_map/ppermute | solution.py:38
  1071.0 16.3 %collective-permute-start.48 = (f32[256]{0:T(256)S(1)}, f32[256]{0:T(256)S(1)}, u32[]{:S(2)}, u32[]{:S(2)}) collective-permute-start(f32[256]{0:T(256)S(1)} %bitcast.112), channel_id=1, source_target_pairs={{0,8},{8,16},{16,24},{24,0},{1,9},{9,17},{17,25},{25,1},{2,10},{10... | collective-permute-start | bytes 3080 | tf_op jit(solution)/shard_map/ppermute | solution.py:38
  1136.9 22.6 %reduce-scatter.14.cloned.1.call-done = bf16[256,512]{1,0:T(8,128)(2,1)} async-done(((bf16[2048,512]{1,0:T(8,128)(2,1)}), bf16[256,512]{1,0:T(8,128)(2,1)}) %reduce-scatter.14.cloned.1.call-update) | async-done | bytes 262160 | tf_op jit(solution)/shard_map/reduce_scatter | solution.py:120
  (514 shorter events, 504.9 us)
Async XLA Ops:
  7.2 125.3 %all-gather.8.cloned.1.call-start = ((), (), s32[]{:S(2)}) async-start(), calls=%async_computation.6 | async-start | bytes 1310720 | tf_op jit(solution)/shard_map/all_gather | solution.py:101
  67.4 65.0 %collective-permute-start.13 = (bf16[512,2048]{1,0:T(8,128)(2,1)}, bf16[512,2048]{1,0:T(8,128)(2,1)}, u32[]{:S(2)}, u32[]{:S(2)}) collective-permute-start(bf16[512,2048]{1,0:T(8,128)(2,1)} %fusion.4.refs_1_), channel_id=1, source_target_pairs={{0,1},{1,0},{2,3},{3,2},{4,5},{5,4},{6,7},{7,6},{8,9},{9,8},{10,11... | collective-permute-start | bytes 6291464 | tf_op jit(solution)/shard_map/ppermute | solution.py:38
  68.7 79.7 %all-gather.6.cloned.1.call-start = ((), (), s32[]{:S(2)}) async-start(), calls=%async_computation.5 | async-start | bytes 1966080 | tf_op jit(solution)/shard_map/all_gather | solution.py:101
  93.9 181.0 %all-gather.10.cloned.1.call-start = ((), (), s32[]{:S(2)}) async-start(), calls=%async_computation.7 | async-start | bytes 5242880 | tf_op jit(solution)/shard_map/all_gather | solution.py:101
  137.8 340.8 %all-gather.12.cloned.1.call-start = ((), (), s32[]{:S(2)}) async-start(), calls=%async_computation.8 | async-start | bytes 9437184 | tf_op jit(solution)/shard_map/all_gather | solution.py:115
  138.4 404.2 %all-gather.14.cloned.1.call-start = ((), (), s32[]{:S(2)}) async-start(), calls=%async_computation.10 | async-start | bytes 9437184 | tf_op jit(solution)/shard_map/all_gather | solution.py:115
  200.0 59.2 %collective-permute-start.16 = (bf16[1024,512]{1,0:T(8,128)(2,1)}, bf16[1024,512]{1,0:T(8,128)(2,1)}, u32[]{:S(2)}, u32[]{:S(2)}) collective-permute-start(bf16[1024,512]{1,0:T(8,128)(2,1)} %hold.15.refs_1_), channel_id=1, source_target_pairs={{0,2},{2,0},{1,3},{3,1},{4,6},{6,4},{5,7},{7,5},{8,10},{10,8},{9,1... | collective-permute-start | bytes 3145736 | tf_op jit(solution)/shard_map/ppermute | solution.py:38
  204.5 62.3 %collective-permute-start.19 = (bf16[512,2048]{1,0:T(8,128)(2,1)}, bf16[512,2048]{1,0:T(8,128)(2,1)}, u32[]{:S(2)}, u32[]{:S(2)}) collective-permute-start(bf16[512,2048]{1,0:T(8,128)(2,1)} %hold.16), channel_id=1, source_target_pairs={{0,1},{1,0},{2,3},{3,2},{4,5},{5,4},{6,7},{7,6},{8,9},{9,8},{10,11... | collective-permute-start | bytes 6291464 | tf_op jit(solution)/shard_map/ppermute | solution.py:38
  267.3 471.4 %reduce-scatter.6.cloned.1.call-start = ((), (), s32[]{:S(2)}) async-start(), calls=%async_computation.9 | async-start | bytes 9437184 | tf_op jit(solution)/shard_map/reduce_scatter | solution.py:120
  275.0 48.0 %collective-permute-start.21 = (bf16[512,2048]{1,0:T(8,128)(2,1)}, bf16[512,2048]{1,0:T(8,128)(2,1)}, u32[]{:S(2)}, u32[]{:S(2)}) collective-permute-start(bf16[512,2048]{1,0:T(8,128)(2,1)} %add_convert_fusion), channel_id=1, source_target_pairs={{0,1},{1,0},{2,3},{3,2},{4,5},{5,4},{6,7},{7,6},{8,9},{9,8},{10,11... | collective-permute-start | bytes 6291464 | tf_op jit(solution)/shard_map/ppermute | solution.py:38
  279.9 88.2 %collective-permute-start.22 = (bf16[512,2048]{1,0:T(8,128)(2,1)S(1)}, bf16[512,2048]{1,0:T(8,128)(2,1)S(1)}, u32[]{:S(2)}, u32[]{:S(2)}) collective-permute-start(bf16[512,2048]{1,0:T(8,128)(2,1)S(1)} %get-tuple-element.96), channel_id=1, source_target_pairs={{0,2},{2,0},{1,3},{3,1},{4,6},{6,4},{5,7},{7,5},{8,10},{10,8},{9,1... | collective-permute-start | bytes 6291464 | tf_op jit(solution)/shard_map/ppermute | solution.py:38
  383.2 48.0 %collective-permute-start.25 = (bf16[512,2048]{1,0:T(8,128)(2,1)}, bf16[512,2048]{1,0:T(8,128)(2,1)}, u32[]{:S(2)}, u32[]{:S(2)}) collective-permute-start(bf16[512,2048]{1,0:T(8,128)(2,1)} %multiply_convert_fusion), channel_id=1, source_target_pairs={{0,1},{1,0},{2,3},{3,2},{4,5},{5,4},{6,7},{7,6},{8,9},{9,8},{10,11... | collective-permute-start | bytes 6291464 | tf_op jit(solution)/shard_map/ppermute | solution.py:38
  384.7 47.0 %collective-permute-start.28 = (bf16[512,2048]{1,0:T(8,128)(2,1)S(1)}, bf16[512,2048]{1,0:T(8,128)(2,1)}, u32[]{:S(2)}, u32[]{:S(2)}) collective-permute-start(bf16[512,2048]{1,0:T(8,128)(2,1)S(1)} %copy-done.9), channel_id=1, source_target_pairs={{0,4},{4,0},{1,5},{5,1},{2,6},{6,2},{3,7},{7,3},{8,12},{12,8},{9,1... | collective-permute-start | bytes 6291464 | tf_op jit(solution)/shard_map/ppermute | solution.py:38
  384.7 59.6 %collective-permute-start.27 = (bf16[512,2048]{1,0:T(8,128)(2,1)}, bf16[512,2048]{1,0:T(8,128)(2,1)}, u32[]{:S(2)}, u32[]{:S(2)}) collective-permute-start(bf16[512,2048]{1,0:T(8,128)(2,1)} %get-tuple-element.95), channel_id=1, source_target_pairs={{0,2},{2,0},{1,3},{3,1},{4,6},{6,4},{5,7},{7,5},{8,10},{10,8},{9,1... | collective-permute-start | bytes 6291464 | tf_op jit(solution)/shard_map/ppermute | solution.py:38
  385.2 60.9 %collective-permute-start.24 = (bf16[512,2048]{1,0:T(8,128)(2,1)}, bf16[512,2048]{1,0:T(8,128)(2,1)}, u32[]{:S(2)}, u32[]{:S(2)}) collective-permute-start(bf16[512,2048]{1,0:T(8,128)(2,1)} %multiply_convert_fusion), channel_id=1, source_target_pairs={{0,4},{4,0},{1,5},{5,1},{2,6},{6,2},{3,7},{7,3},{8,12},{12,8},{9,1... | collective-permute-start | bytes 6291464 | tf_op jit(solution)/shard_map/ppermute | solution.py:38
  542.5 377.2 %reduce-scatter.8.cloned.1.call-start = ((), (), s32[]{:S(2)}) async-start(), calls=%async_computation.11 | async-start | bytes 9437184 | tf_op jit(solution)/shard_map/reduce_scatter | solution.py:120
  658.6 363.6 %reduce-scatter.10.cloned.1.call-start = ((), (), s32[]{:S(2)}) async-start(), calls=%async_computation.12 | async-start | bytes 9437184 | tf_op jit(solution)/shard_map/reduce_scatter | solution.py:120
  672.4 44.5 %collective-permute-start.30 = (bf16[512,1024]{1,0:T(8,128)(2,1)S(1)}, bf16[512,1024]{1,0:T(8,128)(2,1)}, u32[]{:S(2)}, u32[]{:S(2)}) collective-permute-start(bf16[512,1024]{1,0:T(8,128)(2,1)S(1)} %fusion.35), channel_id=1, source_target_pairs={{0,1},{1,0},{2,3},{3,2},{4,5},{5,4},{6,7},{7,6},{8,9},{9,8},{10,11... | collective-permute-start | bytes 3145736 | tf_op jit(solution)/shard_map/ppermute | solution.py:38
  727.6 73.0 %collective-permute-start.39 = (bf16[512,2048]{1,0:T(8,128)(2,1)}, bf16[512,2048]{1,0:T(8,128)(2,1)S(1)}, u32[]{:S(2)}, u32[]{:S(2)}) collective-permute-start(bf16[512,2048]{1,0:T(8,128)(2,1)} %get-tuple-element.81), channel_id=1, source_target_pairs={{0,1},{1,0},{2,3},{3,2},{4,5},{5,4},{6,7},{7,6},{8,9},{9,8},{10,11... | collective-permute-start | bytes 6291464 | tf_op jit(solution)/shard_map/ppermute | solution.py:38
  805.0 306.2 %reduce-scatter.12.cloned.1.call-start = ((), (), s32[]{:S(2)}) async-start(), calls=%async_computation.13 | async-start | bytes 1966080 | tf_op jit(solution)/shard_map/reduce_scatter | solution.py:124
  812.6 121.3 %collective-permute-start.37 = (bf16[512,1024]{1,0:T(8,128)(2,1)}, bf16[512,1024]{1,0:T(8,128)(2,1)}, u32[]{:S(2)}, u32[]{:S(2)}) collective-permute-start(bf16[512,1024]{1,0:T(8,128)(2,1)} %add_convert_fusion.2), channel_id=1, source_target_pairs={{0,1},{1,0},{2,3},{3,2},{4,5},{5,4},{6,7},{7,6},{8,9},{9,8},{10,11... | collective-permute-start | bytes 3145736 | tf_op jit(solution)/shard_map/ppermute | solution.py:38
  992.3 47.9 %collective-permute-start.44 = (bf16[512,2048]{1,0:T(8,128)(2,1)}, bf16[512,2048]{1,0:T(8,128)(2,1)}, u32[]{:S(2)}, u32[]{:S(2)}) collective-permute-start(bf16[512,2048]{1,0:T(8,128)(2,1)} %fusion.17.refs_2_), channel_id=1, source_target_pairs={{0,1},{1,0},{2,3},{3,2},{4,5},{5,4},{6,7},{7,6},{8,9},{9,8},{10,11... | collective-permute-start | bytes 6291464 | tf_op jit(solution)/shard_map/ppermute | solution.py:38
  1022.3 137.2 %reduce-scatter.14.cloned.1.call-start = ((), (), s32[]{:S(2)}) async-start(), calls=%async_computation.14 | async-start | bytes 2359296 | tf_op jit(solution)/shard_map/reduce_scatter | solution.py:120
  1058.5 46.8 %collective-permute-start.62 = (bf16[128,2048]{1,0:T(8,128)(2,1)}, bf16[128,2048]{1,0:T(8,128)(2,1)}, u32[]{:S(2)}, u32[]{:S(2)}) collective-permute-start(bf16[128,2048]{1,0:T(8,128)(2,1)} %get-tuple-element.123), channel_id=1, source_target_pairs={{0,4},{4,0},{1,5},{5,1},{2,6},{6,2},{3,7},{7,3},{8,12},{12,8},{9,1... | collective-permute-start | bytes 1572872 | tf_op jit(solution)/shard_map/ppermute | solution.py:38
  (125 other events, 1658.4 us)
Sparse Core Ops, SparseCore 0:
  68.8 28.7 all-gather.7
  99.7 36.5 all-gather.5
  137.9 82.2 all-gather.9
  222.2 163.1 all-gather.11
  387.4 136.4 all-gather.13
  542.6 148.4 reduce-scatter.5
  695.2 147.9 reduce-scatter.7
  846.9 156.0 reduce-scatter.9
  1022.4 48.7 reduce-scatter.11
  1092.7 66.7 reduce-scatter.13

commit v4 on v3

--- a/solution.py
+++ b/solution.py
@@ -804,7 +804,7 @@
     from_beside = shift(beside_sum, "x", 1)
     gate_grad = finish(hold(gate_grad, from_beside))
     grad_norm_one = mine + from_beside.astype(f32)
-    held = hold(attended, from_beside)
+    held = hold(attended, beside_sum)
     output_grad = scatter_whole(
         jnp.concatenate([attn_terms(grad_branch, held, by_y[i]) for i in range(ys)], axis=0).astype(bf16)
     )

time: 1180 us -> 1190 us (level)
  waiting for transfers between devices: 363 us -> 385 us
  Pallas kernels: 390 us -> 377 us
    ppermute x66, waiting for transfers between devices: 339 us -> 384 us  [shift(): lax.ppermute(value, axis, [(i, (i + steps) % size) for i in range(size)])]
    reduce_scatter x4, waiting for transfers between devices: 22.6 us -> 0.05 us  [scatter_whole(): return lax.psum_scatter(terms, ('y', 'z'), scatter_dimension=0, tiled=True)]
    unnamed x177 -> x179, local copies, waits for them, and re-layouts: 47 us -> 49.1 us
  transfers between devices with their start and end apart: 76 -> 76, of which waited for: 32 -> 32; matrix products, arithmetic and copies ran while one was open for 24% -> 23% of each run, Pallas kernels for 33% -> 32%
where the time goes in v4:
time: 1190 us; the launch traced here: 1180 us
  waiting for transfers between devices  385 us (32%)
  Pallas kernels  377 us (32%)
  other arithmetic  132 us (11%)
  local copies, waits for them, and re-layouts  113 us (9%)
  starting transfers between devices  92 us (8%)
  matrix products  62.5 us (5%)
  between operations  18.1 us (2%)
    ppermute x66, waiting for transfers between devices, shift(): lax.ppermute(value, axis, [(i, (i + steps) % size) for i in range(size)])  384 us
    ppermute x66, starting transfers between devices, shift(): lax.ppermute(value, axis, [(i, (i + steps) % size) for i in range(size)])  91.2 us
    pallas_call x3, Pallas kernels, columns_product(): pl.pallas_call(kernel, grid_spec=pltpu.PrefetchScalarGridSpec(num_scalar_...  86.1 us
    pallas_call x3, Pallas kernels, rows_product(): pl.pallas_call(kernel, grid=(n // bn, t // bm), in_specs=[pl.BlockSpec((b...  80.8 us
    pallas_call x4, Pallas kernels, turned_product(): pl.pallas_call(kernel, grid=(n // bn, t // bm), in_specs=[pl.BlockSpec((b...  75.3 us
    pallas_call x2, Pallas kernels, attention_bwd(): pl.pallas_call(functools.partial(attention_bwd_body, chunk, blocks, part,...  68.9 us
    dot_general x10, matrix products, contract(): lax.dot_general(left, right, (((left_dim,), (right_dim,)), ((), ())), pre...  62.5 us
    unnamed x179, local copies, waits for them, and re-layouts  49.1 us
  transfers between devices with their start and end apart: 76, of which 32 were waited for; matrix products, arithmetic and copies ran while one was open for 23% of the time, Pallas kernels for 32%

profile of v4, /device:TPU:0, one launch (start us, length us, event | category | flops | bytes accessed | tf_op | source)
XLA Modules:
  0.0 1178.4 jit_solution(3112310382683124860)
XLA Ops:
  68.8 19.0 %collective-permute-done.5 = bf16[64,12288]{1,0:T(8,128)(2,1)} collective-permute-done((bf16[64,12288]{1,0:T(8,128)(2,1)}, bf16[64,12288]{1,0:T(8,128)(2,1)}, u32[]{:S(2)}, u32[]{:S(2)}) %collective-permute-start.5) | collective-permute-done | bytes 1572896 | tf_op jit(solution)/shard_map/ppermute | solution.py:38
  94.0 38.5 %collective-permute-done.13.refs_1_ = bf16[512,2048]{1,0:T(8,128)(2,1)} collective-permute-done((bf16[512,2048]{1,0:T(8,128)(2,1)}, bf16[512,2048]{1,0:T(8,128)(2,1)}, u32[]{:S(2)}, u32[]{:S(2)}) %collective-permute-start.13) | collective-permute-done | bytes 2097184 | tf_op jit(solution)/shard_map/ppermute | solution.py:38
  158.6 26.4 %collective-permute-done.4 = bf16[1024,768]{1,0:T(8,128)(2,1)S(1)} collective-permute-done((bf16[1024,768]{1,0:T(8,128)(2,1)}, bf16[1024,768]{1,0:T(8,128)(2,1)S(1)}, u32[]{:S(2)}, u32[]{:S(2)}) %collective-permute-start.4) | collective-permute-done | bytes 1572896 | tf_op jit(solution)/shard_map/ppermute | solution.py:38
  205.8 16.6 %collective-permute-done.17 = bf16[256,2048]{1,0:T(8,128)(2,1)} collective-permute-done((bf16[256,2048]{1,0:T(8,128)(2,1)}, bf16[256,2048]{1,0:T(8,128)(2,1)}, u32[]{:S(2)}, u32[]{:S(2)}) %collective-permute-start.17) | collective-permute-done | bytes 1048608 | tf_op jit(solution)/shard_map/ppermute | solution.py:38
  225.1 26.2 %attention_forward.2 = (bf16[512,1024]{1,0:T(8,128)(2,1)}, f32[2,4,1024]{2,1,0:T(4,128)}) custom-call(s32[2,4]{1,0:T(2,128)} %get-tuple-element.88.qpos_ref, s32[2,8]{1,0:T(2,128)} %stack.77.kpos_ref, s32[2]{0:T(128)} %pad_add_fusion.2.len_ref, bf16[512,2048]{1,0:T(8,128)(2,1)} %bitcast.76, bf16[2,128,2048]{2,1,0:T(8,128)(2,1)} %get-tuple-element.109.k_ref, ...), custom_call_target="tpu_custom_call" | custom-call | flops 34359738368 | bytes 4194304 | tf_op jit(solution)/shard_map/attention_forward/pallas_call | solution.py:420
  279.6 22.4 %attention_forward.3 = (bf16[512,1024]{1,0:T(8,128)(2,1)}, f32[2,4,1024]{2,1,0:T(4,128)}) custom-call(s32[2,4]{1,0:T(2,128)} %get-tuple-element.88.qpos_ref, s32[2,8]{1,0:T(2,128)} %stack.77.kpos_ref, s32[2]{0:T(128)} %pad_add_fusion.2.len_ref, bf16[512,2048]{1,0:T(8,128)(2,1)} %bitcast.77, bf16[2,128,2048]{2,1,0:T(8,128)(2,1)} %get-tuple-element.109.k_ref, ...), custom_call_target="tpu_custom_call" | custom-call | flops 34359738368 | bytes 4194304 | tf_op jit(solution)/shard_map/attention_forward/pallas_call | solution.py:420
  302.0 16.3 %collective-permute-done.21 = bf16[512,2048]{1,0:T(8,128)(2,1)} collective-permute-done((bf16[512,2048]{1,0:T(8,128)(2,1)}, bf16[512,2048]{1,0:T(8,128)(2,1)}, u32[]{:S(2)}, u32[]{:S(2)}) %collective-permute-start.21) | collective-permute-done | bytes 2097184 | tf_op jit(solution)/shard_map/ppermute | solution.py:38
  318.3 49.7 %collective-permute-done.22 = bf16[512,2048]{1,0:T(8,128)(2,1)S(1)} collective-permute-done((bf16[512,2048]{1,0:T(8,128)(2,1)S(1)}, bf16[512,2048]{1,0:T(8,128)(2,1)S(1)}, u32[]{:S(2)}, u32[]{:S(2)}) %collective-permute-start.22) | collective-permute-done | bytes 2097184 | tf_op jit(solution)/shard_map/ppermute | solution.py:38
  385.4 45.7 %collective-permute-done.25 = bf16[512,2048]{1,0:T(8,128)(2,1)} collective-permute-done((bf16[512,2048]{1,0:T(8,128)(2,1)}, bf16[512,2048]{1,0:T(8,128)(2,1)}, u32[]{:S(2)}, u32[]{:S(2)}) %collective-permute-start.25) | collective-permute-done | bytes 2097184 | tf_op jit(solution)/shard_map/ppermute | solution.py:38
  454.9 23.7 %gate.1.refs_3_ = bf16[2048,2048]{1,0:T(8,128)(2,1)} custom-call(bf16[2048,2048]{1,0:T(8,128)(2,1)} %pad_maximum_fusion.1.refs_0_.left_ref, bf16[1024,2048]{1,0:T(8,128)(2,1)} %hold.18.refs_1_.refs_2_, bf16[1024,2048]{1,0:T(8,128)(2,1)} %copy-done.37), custom_call_target="tpu_custom_call" | custom-call | flops 17179869184 | bytes 25165824 | tf_op jit(solution)/shard_map/gate/pallas_call | solution.py:241
  487.0 26.7 %up.1 = (bf16[2048,2048]{1,0:T(8,128)(2,1)}, bf16[2048,2048]{1,0:T(8,128)(2,1)}) custom-call(bf16[2048,2048]{1,0:T(8,128)(2,1)} %pad_maximum_fusion.1.refs_0_.left_ref, bf16[1024,2048]{1,0:T(8,128)(2,1)} %get-tuple-element.92.refs_1_.refs_3_, bf16[1024,2048]{1,0:T(8,128)(2,1)} %get-tuple-element.91.refs_2_.refs_3_, bf16[2048,2048]{1,0:T(8,128)(2,1)} %gate.1.refs_3_), custom_call_target="tpu_custom_call" | custom-call | flops 17179869184 | bytes 25165824 | tf_op jit(solution)/shard_map/up/pallas_call | solution.py:241
  513.7 28.7 %down_grad.1 = bf16[2048,2048]{1,0:T(8,128)(2,1)} custom-call(s32[2]{0:T(128)} %and_select_fusion.slots_ref, bf16[2048,2048]{1,0:T(8,128)(2,1)} %pad_maximum_fusion.2.left_ref.refs_0_, bf16[2048,2048]{1,0:T(8,128)(2,1)} %get-tuple-element.67.right_ref.refs_0_), custom_call_target="tpu_custom_call" | custom-call | flops 17179869184 | bytes 20971520 | tf_op jit(solution)/shard_map/down_grad/pallas_call | solution.py:305
  551.0 30.5 %hidden_grad.1 = (bf16[2048,2048]{1,0:T(8,128)(2,1)}, bf16[2048,2048]{1,0:T(8,128)(2,1)}) custom-call(bf16[2048,2048]{1,0:T(8,128)(2,1)} %pad_maximum_fusion.2.left_ref.refs_0_, bf16[1024,2048]{1,0:T(8,128)(2,1)} %get-tuple-element.90.refs_1_, bf16[1024,2048]{1,0:T(8,128)(2,1)} %get-tuple-element.89.refs_2_.refs_1_, bf16[2048,2048]{1,0:T(8,128)(2,1)} %gate.1.refs_3_, ...), custom_call_target="tpu_custom_call" | custom-call | flops 17179869184 | bytes 25165824 | tf_op jit(solution)/shard_map/hidden_grad/pallas_call | solution.py:241
  581.6 24.2 %norm_grad.2 = bf16[2048,1024]{1,0:T(8,128)(2,1)} custom-call(bf16[2048,2048]{1,0:T(8,128)(2,1)} %get-tuple-element.59.refs_0_.right_ref, bf16[2048,2048]{1,0:T(8,128)(2,1)} %get-tuple-element.58.refs_1_.right_ref, bf16[1024,2048]{1,0:T(8,128)(2,1)} %hold.18.refs_1_.refs_2_, bf16[1024,2048]{1,0:T(8,128)(2,1)} %get-tuple-element.92.refs_1_.refs_3_), custom_call_target="tpu_custom_call" | custom-call | flops 17179869184 | bytes 25165824 | tf_op jit(solution)/shard_map/norm_grad/pallas_call | solution.py:270
  605.8 23.9 %norm_grad.3 = bf16[2048,1024]{1,0:T(8,128)(2,1)} custom-call(bf16[2048,2048]{1,0:T(8,128)(2,1)} %get-tuple-element.59.refs_0_.right_ref, bf16[2048,2048]{1,0:T(8,128)(2,1)} %get-tuple-element.58.refs_1_.right_ref, bf16[1024,2048]{1,0:T(8,128)(2,1)} %copy-done.37, bf16[1024,2048]{1,0:T(8,128)(2,1)} %get-tuple-element.91.refs_2_.refs_3_), custom_call_target="tpu_custom_call" | custom-call | flops 17179869184 | bytes 25165824 | tf_op jit(solution)/shard_map/norm_grad/pallas_call | solution.py:270
  629.7 28.8 %gate_grad.1 = bf16[2048,2048]{1,0:T(8,128)(2,1)} custom-call(s32[2]{0:T(128)} %and_select_fusion.slots_ref, bf16[2048,2048]{1,0:T(8,128)(2,1)} %pad_maximum_fusion.1.refs_0_.left_ref, bf16[2048,2048]{1,0:T(8,128)(2,1)} %get-tuple-element.59.refs_0_.right_ref), custom_call_target="tpu_custom_call" | custom-call | flops 17179869184 | bytes 20971520 | tf_op jit(solution)/shard_map/gate_grad/pallas_call | solution.py:305
  673.3 28.6 %up_grad.1 = bf16[2048,2048]{1,0:T(8,128)(2,1)} custom-call(s32[2]{0:T(128)} %and_select_fusion.slots_ref, bf16[2048,2048]{1,0:T(8,128)(2,1)} %pad_maximum_fusion.1.refs_0_.left_ref, bf16[2048,2048]{1,0:T(8,128)(2,1)} %get-tuple-element.58.refs_1_.right_ref), custom_call_target="tpu_custom_call" | custom-call | flops 17179869184 | bytes 20971520 | tf_op jit(solution)/shard_map/up_grad/pallas_call | solution.py:305
  701.9 14.9 %collective-permute-done.30 = bf16[512,1024]{1,0:T(8,128)(2,1)} collective-permute-done((bf16[512,1024]{1,0:T(8,128)(2,1)S(1)}, bf16[512,1024]{1,0:T(8,128)(2,1)}, u32[]{:S(2)}, u32[]{:S(2)}) %collective-permute-start.30) | collective-permute-done | bytes 1048608 | tf_op jit(solution)/shard_map/ppermute | solution.py:38
  738.7 31.5 %attention_backward.2 = (f32[512,1024]{1,0:T(8,128)}, f32[2,128,2048]{2,1,0:T(8,128)}, f32[2,128,2048]{2,1,0:T(8,128)}) custom-call(s32[2,4]{1,0:T(2,128)} %get-tuple-element.88.qpos_ref, s32[2,8]{1,0:T(2,128)} %stack.77.kpos_ref, s32[2]{0:T(128)} %pad_add_fusion.2.len_ref, bf16[512,2048]{1,0:T(8,128)(2,1)} %bitcast.78, ...), custom_call_target="tpu_custom_call" | custom-call | flops 42949672960 | bytes 14680064 | tf_op jit(solution)/shard_map/attention_backward/pallas_call | solution.py:540
  770.2 13.8 %down.2 = bf16[2048,1024]{1,0:T(8,128)(2,1)} custom-call(bf16[2048,2048]{1,0:T(8,128)(2,1)} %get-tuple-element.67.right_ref.refs_0_, bf16[1024,2048]{1,0:T(8,128)(2,1)} %get-tuple-element.90.refs_1_), custom_call_target="tpu_custom_call" | custom-call | flops 8589934592 | bytes 12582912 | tf_op jit(solution)/shard_map/down/pallas_call | solution.py:270
  828.0 37.4 %attention_backward.3 = (f32[512,1024]{1,0:T(8,128)}, bf16[2,128,2048]{2,1,0:T(8,128)(2,1)}, bf16[2,128,2048]{2,1,0:T(8,128)(2,1)}) custom-call(s32[2,4]{1,0:T(2,128)} %get-tuple-element.88.qpos_ref, s32[2,8]{1,0:T(2,128)} %stack.77.kpos_ref, s32[2]{0:T(128)} %pad_add_fusion.2.len_ref, bf16[512,2048]{1,0:T(8,128)(2,1)} %bitcast.79, ...), custom_call_target="tpu_custom_call" | custom-call | flops 42949672960 | bytes 14680064 | tf_op jit(solution)/shard_map/attention_backward/pallas_call | solution.py:540
  889.0 22.9 %collective-permute-done.42 = bf16[256,2048]{1,0:T(8,128)(2,1)S(1)} collective-permute-done((bf16[256,2048]{1,0:T(8,128)(2,1)S(1)}, bf16[256,2048]{1,0:T(8,128)(2,1)S(1)}, u32[]{:S(2)}, u32[]{:S(2)}) %collective-permute-start.42) | collective-permute-done | bytes 1048608 | tf_op jit(solution)/shard_map/ppermute | solution.py:38
  956.5 41.7 %collective-permute-done.51 = bf16[1024,768]{1,0:T(8,128)(2,1)} collective-permute-done((bf16[1024,768]{1,0:T(8,128)(2,1)}, bf16[1024,768]{1,0:T(8,128)(2,1)}, u32[]{:S(2)}, u32[]{:S(2)}) %collective-permute-start.51) | collective-permute-done | bytes 1572896 | tf_op jit(solution)/shard_map/ppermute | solution.py:38
  1049.5 28.3 %collective-permute-done.44.refs_1_ = bf16[512,2048]{1,0:T(8,128)(2,1)} collective-permute-done((bf16[512,2048]{1,0:T(8,128)(2,1)}, bf16[512,2048]{1,0:T(8,128)(2,1)}, u32[]{:S(2)}, u32[]{:S(2)}) %collective-permute-start.44) | collective-permute-done | bytes 2097184 | tf_op jit(solution)/shard_map/ppermute | solution.py:38
  (516 shorter events, 494.0 us)
Async XLA Ops:
  7.2 125.3 %all-gather.8.cloned.1.call-start = ((), (), s32[]{:S(2)}) async-start(), calls=%async_computation.6 | async-start | bytes 1310720 | tf_op jit(solution)/shard_map/all_gather | solution.py:101
  67.4 65.0 %collective-permute-start.13 = (bf16[512,2048]{1,0:T(8,128)(2,1)}, bf16[512,2048]{1,0:T(8,128)(2,1)}, u32[]{:S(2)}, u32[]{:S(2)}) collective-permute-start(bf16[512,2048]{1,0:T(8,128)(2,1)} %fusion.4.refs_1_), channel_id=1, source_target_pairs={{0,1},{1,0},{2,3},{3,2},{4,5},{5,4},{6,7},{7,6},{8,9},{9,8},{10,11... | collective-permute-start | bytes 6291464 | tf_op jit(solution)/shard_map/ppermute | solution.py:38
  68.7 79.5 %all-gather.6.cloned.1.call-start = ((), (), s32[]{:S(2)}) async-start(), calls=%async_computation.5 | async-start | bytes 1966080 | tf_op jit(solution)/shard_map/all_gather | solution.py:101
  93.9 178.1 %all-gather.10.cloned.1.call-start = ((), (), s32[]{:S(2)}) async-start(), calls=%async_computation.7 | async-start | bytes 5242880 | tf_op jit(solution)/shard_map/all_gather | solution.py:101
  137.8 340.7 %all-gather.12.cloned.1.call-start = ((), (), s32[]{:S(2)}) async-start(), calls=%async_computation.8 | async-start | bytes 9437184 | tf_op jit(solution)/shard_map/all_gather | solution.py:115
  138.4 404.1 %all-gather.14.cloned.1.call-start = ((), (), s32[]{:S(2)}) async-start(), calls=%async_computation.10 | async-start | bytes 9437184 | tf_op jit(solution)/shard_map/all_gather | solution.py:115
  199.9 54.6 %collective-permute-start.16 = (bf16[1024,512]{1,0:T(8,128)(2,1)}, bf16[1024,512]{1,0:T(8,128)(2,1)}, u32[]{:S(2)}, u32[]{:S(2)}) collective-permute-start(bf16[1024,512]{1,0:T(8,128)(2,1)} %hold.15.refs_1_), channel_id=1, source_target_pairs={{0,2},{2,0},{1,3},{3,1},{4,6},{6,4},{5,7},{7,5},{8,10},{10,8},{9,1... | collective-permute-start | bytes 3145736 | tf_op jit(solution)/shard_map/ppermute | solution.py:38
  204.3 57.8 %collective-permute-start.19 = (bf16[512,2048]{1,0:T(8,128)(2,1)}, bf16[512,2048]{1,0:T(8,128)(2,1)}, u32[]{:S(2)}, u32[]{:S(2)}) collective-permute-start(bf16[512,2048]{1,0:T(8,128)(2,1)} %hold.16), channel_id=1, source_target_pairs={{0,1},{1,0},{2,3},{3,2},{4,5},{5,4},{6,7},{7,6},{8,9},{9,8},{10,11... | collective-permute-start | bytes 6291464 | tf_op jit(solution)/shard_map/ppermute | solution.py:38
  262.6 476.0 %reduce-scatter.6.cloned.1.call-start = ((), (), s32[]{:S(2)}) async-start(), calls=%async_computation.9 | async-start | bytes 9437184 | tf_op jit(solution)/shard_map/reduce_scatter | solution.py:120
  270.3 48.0 %collective-permute-start.21 = (bf16[512,2048]{1,0:T(8,128)(2,1)}, bf16[512,2048]{1,0:T(8,128)(2,1)}, u32[]{:S(2)}, u32[]{:S(2)}) collective-permute-start(bf16[512,2048]{1,0:T(8,128)(2,1)} %add_convert_fusion), channel_id=1, source_target_pairs={{0,1},{1,0},{2,3},{3,2},{4,5},{5,4},{6,7},{7,6},{8,9},{9,8},{10,11... | collective-permute-start | bytes 6291464 | tf_op jit(solution)/shard_map/ppermute | solution.py:38
  276.1 91.9 %collective-permute-start.22 = (bf16[512,2048]{1,0:T(8,128)(2,1)S(1)}, bf16[512,2048]{1,0:T(8,128)(2,1)S(1)}, u32[]{:S(2)}, u32[]{:S(2)}) collective-permute-start(bf16[512,2048]{1,0:T(8,128)(2,1)S(1)} %get-tuple-element.96), channel_id=1, source_target_pairs={{0,2},{2,0},{1,3},{3,1},{4,6},{6,4},{5,7},{7,5},{8,10},{10,8},{9,1... | collective-permute-start | bytes 6291464 | tf_op jit(solution)/shard_map/ppermute | solution.py:38
  383.1 48.0 %collective-permute-start.25 = (bf16[512,2048]{1,0:T(8,128)(2,1)}, bf16[512,2048]{1,0:T(8,128)(2,1)}, u32[]{:S(2)}, u32[]{:S(2)}) collective-permute-start(bf16[512,2048]{1,0:T(8,128)(2,1)} %multiply_convert_fusion), channel_id=1, source_target_pairs={{0,1},{1,0},{2,3},{3,2},{4,5},{5,4},{6,7},{7,6},{8,9},{9,8},{10,11... | collective-permute-start | bytes 6291464 | tf_op jit(solution)/shard_map/ppermute | solution.py:38
  384.7 47.0 %collective-permute-start.28 = (bf16[512,2048]{1,0:T(8,128)(2,1)S(1)}, bf16[512,2048]{1,0:T(8,128)(2,1)}, u32[]{:S(2)}, u32[]{:S(2)}) collective-permute-start(bf16[512,2048]{1,0:T(8,128)(2,1)S(1)} %copy-done.9), channel_id=1, source_target_pairs={{0,4},{4,0},{1,5},{5,1},{2,6},{6,2},{3,7},{7,3},{8,12},{12,8},{9,1... | collective-permute-start | bytes 6291464 | tf_op jit(solution)/shard_map/ppermute | solution.py:38
  384.7 59.6 %collective-permute-start.27 = (bf16[512,2048]{1,0:T(8,128)(2,1)}, bf16[512,2048]{1,0:T(8,128)(2,1)}, u32[]{:S(2)}, u32[]{:S(2)}) collective-permute-start(bf16[512,2048]{1,0:T(8,128)(2,1)} %get-tuple-element.95), channel_id=1, source_target_pairs={{0,2},{2,0},{1,3},{3,1},{4,6},{6,4},{5,7},{7,5},{8,10},{10,8},{9,1... | collective-permute-start | bytes 6291464 | tf_op jit(solution)/shard_map/ppermute | solution.py:38
  385.1 61.0 %collective-permute-start.24 = (bf16[512,2048]{1,0:T(8,128)(2,1)}, bf16[512,2048]{1,0:T(8,128)(2,1)}, u32[]{:S(2)}, u32[]{:S(2)}) collective-permute-start(bf16[512,2048]{1,0:T(8,128)(2,1)} %multiply_convert_fusion), channel_id=1, source_target_pairs={{0,4},{4,0},{1,5},{5,1},{2,6},{6,2},{3,7},{7,3},{8,12},{12,8},{9,1... | collective-permute-start | bytes 6291464 | tf_op jit(solution)/shard_map/ppermute | solution.py:38
  542.4 370.8 %reduce-scatter.8.cloned.1.call-start = ((), (), s32[]{:S(2)}) async-start(), calls=%async_computation.11 | async-start | bytes 9437184 | tf_op jit(solution)/shard_map/reduce_scatter | solution.py:120
  658.5 357.6 %reduce-scatter.10.cloned.1.call-start = ((), (), s32[]{:S(2)}) async-start(), calls=%async_computation.12 | async-start | bytes 9437184 | tf_op jit(solution)/shard_map/reduce_scatter | solution.py:120
  727.5 76.6 %collective-permute-start.39 = (bf16[512,2048]{1,0:T(8,128)(2,1)}, bf16[512,2048]{1,0:T(8,128)(2,1)S(1)}, u32[]{:S(2)}, u32[]{:S(2)}) collective-permute-start(bf16[512,2048]{1,0:T(8,128)(2,1)} %get-tuple-element.81), channel_id=1, source_target_pairs={{0,1},{1,0},{2,3},{3,2},{4,5},{5,4},{6,7},{7,6},{8,9},{9,8},{10,11... | collective-permute-start | bytes 6291464 | tf_op jit(solution)/shard_map/ppermute | solution.py:38
  806.5 328.6 %reduce-scatter.12.cloned.1.call-start = ((), (), s32[]{:S(2)}) async-start(), calls=%async_computation.13 | async-start | bytes 1966080 | tf_op jit(solution)/shard_map/reduce_scatter | solution.py:124
  816.0 106.2 %collective-permute-start.37 = (bf16[512,1024]{1,0:T(8,128)(2,1)}, bf16[512,1024]{1,0:T(8,128)(2,1)}, u32[]{:S(2)}, u32[]{:S(2)}) collective-permute-start(bf16[512,1024]{1,0:T(8,128)(2,1)} %add_convert_fusion.2), channel_id=1, source_target_pairs={{0,1},{1,0},{2,3},{3,2},{4,5},{5,4},{6,7},{7,6},{8,9},{9,8},{10,11... | collective-permute-start | bytes 3145736 | tf_op jit(solution)/shard_map/ppermute | solution.py:38
  942.7 63.0 %collective-permute-start.43 = (bf16[1024,2048]{1,0:T(8,128)(2,1)}, bf16[1024,2048]{1,0:T(8,128)(2,1)}, u32[]{:S(2)}, u32[]{:S(2)}) collective-permute-start(bf16[1024,2048]{1,0:T(8,128)(2,1)} %slice.542), channel_id=1, source_target_pairs={{0,4},{4,0},{1,5},{5,1},{2,6},{6,2},{3,7},{7,3},{8,12},{12,8},{9,1... | collective-permute-start | bytes 12582920 | tf_op jit(solution)/shard_map/ppermute | solution.py:38
  950.0 48.3 %collective-permute-start.51 = (bf16[1024,768]{1,0:T(8,128)(2,1)}, bf16[1024,768]{1,0:T(8,128)(2,1)}, u32[]{:S(2)}, u32[]{:S(2)}) collective-permute-start(bf16[1024,768]{1,0:T(8,128)(2,1)} %fusion.39), channel_id=1, source_target_pairs={{0,2},{2,0},{1,3},{3,1},{4,6},{6,4},{5,7},{7,5},{8,10},{10,8},{9,1... | collective-permute-start | bytes 4718600 | tf_op jit(solution)/shard_map/ppermute | solution.py:38
  1016.2 145.8 %reduce-scatter.14.cloned.1.call-start = ((), (), s32[]{:S(2)}) async-start(), calls=%async_computation.14 | async-start | bytes 2359296 | tf_op jit(solution)/shard_map/reduce_scatter | solution.py:120
  1030.5 47.3 %collective-permute-start.44 = (bf16[512,2048]{1,0:T(8,128)(2,1)}, bf16[512,2048]{1,0:T(8,128)(2,1)}, u32[]{:S(2)}, u32[]{:S(2)}) collective-permute-start(bf16[512,2048]{1,0:T(8,128)(2,1)} %fusion.17.refs_2_.refs_1_), channel_id=1, source_target_pairs={{0,1},{1,0},{2,3},{3,2},{4,5},{5,4},{6,7},{7,6},{8,9},{9,8},{10,11... | collective-permute-start | bytes 6291464 | tf_op jit(solution)/shard_map/ppermute | solution.py:38
  (126 other events, 1794.9 us)
Sparse Core Ops, SparseCore 0:
  68.8 28.7 all-gather.7
  99.7 36.5 all-gather.5
  137.9 82.2 all-gather.9
  222.2 166.4 all-gather.11
  390.7 133.0 all-gather.13
  542.5 148.4 reduce-scatter.5
  695.1 148.0 reduce-scatter.7
  846.8 161.1 reduce-scatter.9
  1016.3 49.9 reduce-scatter.11
  1070.1 66.6 reduce-scatter.13

commit v5 on v4

--- a/solution.py
+++ b/solution.py
@@ -109,11 +109,8 @@
     return [shift(term, "y", -(k + 1)) for k, term in enumerate(terms)]
 
 
-def gather_whole(unit, y):
-    zs, ys = lax.axis_size("z"), lax.axis_size("y")
-    size = zs * unit.shape[0]
-    whole = lax.all_gather(unit, ("y", "z"), axis=0, tiled=True)
-    return [lax.dynamic_slice_in_dim(whole, ((y - k) % ys) * size, size, 0) for k in range(ys)]
+def gather_whole(unit):
+    return lax.all_gather(unit, ("y", "z"), axis=0, tiled=True)
 
 
 def scatter_whole(terms):
@@ -218,14 +215,15 @@
     return size if size <= most else fit(size // 2, most)
 
 
-def rows_product(left, parts, extras, finish, n_out, name):
+def rows_product(left, parts, places, extras, finish, n_out, name):
     t, d = left.shape
     n = parts[0].shape[1]
-    depth = parts[0].shape[0]
+    depth = d // len(parts)
     bm, bn = fit(t, 512), fit(n, 1024)
     n_parts, n_extra = len(parts), len(extras)
 
-    def kernel(*refs):
+    def kernel(places_ref, *refs):
+        del places_ref
         left_ref = refs[0]
         product = None
         for p in range(n_parts):
@@ -237,28 +235,31 @@
         for ref, value in zip(refs[1 + n_parts + n_extra :], got):
             ref[...] = value.astype(bf16)
 
-    tile = pl.BlockSpec((bm, bn), lambda j, i: (i, j))
+    tile = pl.BlockSpec((bm, bn), lambda j, i, w: (i, j))
     return pl.pallas_call(
         kernel,
-        grid=(n // bn, t // bm),
-        in_specs=[pl.BlockSpec((bm, d), lambda j, i: (i, 0))]
-        + [pl.BlockSpec((depth, bn), lambda j, i: (0, j))] * n_parts
-        + [tile] * n_extra,
-        out_specs=[tile] * n_out,
+        grid_spec=pltpu.PrefetchScalarGridSpec(
+            num_scalar_prefetch=1,
+            grid=(n // bn, t // bm),
+            in_specs=[pl.BlockSpec((bm, d), lambda j, i, w: (i, 0))]
+            + [pl.BlockSpec((depth, bn), lambda j, i, w, p=p: (w[p], j)) for p in range(n_parts)]
+            + [tile] * n_extra,
+            out_specs=[tile] * n_out,
+        ),
         out_shape=[jax.ShapeDtypeStruct((t, n), bf16)] * n_out,
         compiler_params=pltpu.CompilerParams(vmem_limit_bytes=VMEM_BYTES),
         cost_estimate=estimate(2 * t * d * n, 2 * (t * d + d * n + t * n)),
         name=name,
-    )(left, *parts, *extras)
-
-
-def turned_product(lefts, rights, name):
+    )(places, left, *parts, *extras)
+
+
+def turned_product(lefts, rights, places, n, name):
     t, f = lefts[0].shape
-    n = rights[0].shape[0]
     bm, bn = fit(t, 512), fit(n, 1024)
     count = len(lefts)
 
-    def kernel(*refs):
+    def kernel(places_ref, *refs):
+        del places_ref
         product = None
         for p in range(count):
             term = lax.dot_general(
@@ -269,15 +270,18 @@
 
     return pl.pallas_call(
         kernel,
-        grid=(n // bn, t // bm),
-        in_specs=[pl.BlockSpec((bm, f), lambda j, i: (i, 0))] * count
-        + [pl.BlockSpec((bn, f), lambda j, i: (j, 0))] * count,
-        out_specs=pl.BlockSpec((bm, bn), lambda j, i: (i, j)),
+        grid_spec=pltpu.PrefetchScalarGridSpec(
+            num_scalar_prefetch=1,
+            grid=(n // bn, t // bm),
+            in_specs=[pl.BlockSpec((bm, f), lambda j, i, w: (i, 0))] * count
+            + [pl.BlockSpec((bn, f), lambda j, i, w, p=p: (w[p] * (n // bn) + j, 0)) for p in range(count)],
+            out_specs=pl.BlockSpec((bm, bn), lambda j, i, w: (i, j)),
+        ),
         out_shape=jax.ShapeDtypeStruct((t, n), bf16),
         compiler_params=pltpu.CompilerParams(vmem_limit_bytes=VMEM_BYTES),
         cost_estimate=estimate(2 * count * t * f * n, 2 * count * (t * f + f * n)),
         name=name,
-    )(*lefts, *rights)
+    )(places, *lefts, *rights)
 
 
 def columns_product(left, slots, n_parts, right, others, name):
@@ -661,7 +665,7 @@
     out_slots = gather_slots(out_column)
     out_w = jnp.concatenate(out_slots, axis=0)
     gate_column = gather_column(hold(gate_unit, out_column))
-    up_all, down_all = gather_whole(up_unit, y), gather_whole(down_unit, y)
+    up_all, down_all = gather_whole(up_unit), gather_whole(down_unit)
 
     normed_one = jnp.concatenate([own, beside, sibling, both_two], axis=0)
     pre = contract(after(qkv_w, mlp_unit), normed_one, 0, 1)
@@ -699,21 +703,24 @@
     own, beside, sibling, both_two = group_tokens((unit_two * gain_two).astype(bf16))
     normed_two = jnp.concatenate([own, sibling, both_two, after(beside, *gate_rest)], axis=0)
 
-    (gate_pre,) = rows_product(normed_two, gate_all, [], plain, 1, "gate")
-    up_pre, hidden = rows_product(normed_two, up_all, [gate_pre], up_finish, 2, "up")
+    by_y = (y - jnp.arange(ys, dtype=jnp.int32)) % ys
+    at_start = jnp.zeros((ys,), jnp.int32)
+    part_rows = width // ys
+    (gate_pre,) = rows_product(normed_two, gate_all, at_start, [], plain, 1, "gate")
+    up_pre, hidden = rows_product(normed_two, [up_all] * ys, by_y, [gate_pre], up_finish, 2, "up")
 
     def finish(total):
         return join_columns(total, c, x)
 
-    by_y = (y - jnp.arange(ys, dtype=jnp.int32)) % ys
     last = columns_product(grad_low, by_y, ys, hidden, [], "down_grad")
     down_grad = scatter_whole(last)
     grad_gate, grad_up = rows_product(
-        after(grad_low, last), down_all, [gate_pre, up_pre], hidden_back, 2, "hidden_grad"
+        after(grad_low, last), [down_all] * ys, by_y, [gate_pre, up_pre], hidden_back, 2, "hidden_grad"
     )
     norm_parts, last = [], grad_gate
-    for g, u in zip(gate_all, up_all):
-        last = turned_product([after(grad_gate, last), grad_up], [g, u], "norm_grad")
+    for k, g in enumerate(gate_all):
+        places = jnp.stack([at_start[k], by_y[k]])
+        last = turned_product([after(grad_gate, last), grad_up], [g, up_all], places, part_rows, "norm_grad")
         norm_parts.append(last)
     sums = [scatter_by_c(part, False) for part in norm_parts]
     came = [shift(beside.astype(bf16), "x", 1) for _, beside in sums]
@@ -749,8 +756,8 @@
     beside = hold(beside, query_zero)
     both_two = shift(beside, "c", 1)
     branch_parts, last = [], query_zero
-    for w in down_all:
-        last = turned_product([after(hidden, last)], [w], "down")
+    for k in range(ys):
+        last = turned_product([after(hidden, last)], [down_all], by_y[k][None], part_rows, "down")
         branch_parts.append(last)
     sent = [part[rows : 3 * rows] for part in branch_parts]
     got_c = [shift(part, "c", 1) for part in sent]

time: 1190 us -> 1160 us (0.975)
  local copies, waits for them, and re-layouts: 113 us -> 88.1 us
  Pallas kernels: 377 us -> 390 us
    dynamic_slice x2 -> x0, local copies, waits for them, and re-layouts: 17 us -> none  [gather_whole(): lax.dynamic_slice_in_dim(whole, (y - k) % ys * size, size, 0)]
    unnamed x179 -> x169, local copies, waits for them, and re-layouts: 49.1 us -> 43.5 us
  transfers between devices with their start and end apart: 76 -> 76, of which waited for: 32 -> 33; matrix products, arithmetic and copies ran while one was open for 23% -> 22% of each run, Pallas kernels for 32% -> 34%
where the time goes in v5:
time: 1160 us; the launch traced here: 1150 us
  Pallas kernels  390 us (34%)
  waiting for transfers between devices  376 us (32%)
  other arithmetic  135 us (12%)
  local copies, waits for them, and re-layouts  88.1 us (8%)
  starting transfers between devices  83.8 us (7%)
  matrix products  62.5 us (5%)
  between operations  17.7 us (2%)
    ppermute x66, waiting for transfers between devices, shift(): lax.ppermute(value, axis, [(i, (i + steps) % size) for i in range(size)])  375 us
    pallas_call x3, Pallas kernels, columns_product(): pl.pallas_call(kernel, grid_spec=pltpu.PrefetchScalarGridSpec(num_scalar_...  85.9 us
    pallas_call x3, Pallas kernels, rows_product(): pl.pallas_call(kernel, grid_spec=pltpu.PrefetchScalarGridSpec(num_scalar_...  83.3 us
    ppermute x66, starting transfers between devices, shift(): lax.ppermute(value, axis, [(i, (i + steps) % size) for i in range(size)])  82.8 us
    pallas_call x4, Pallas kernels, turned_product(): pl.pallas_call(kernel, grid_spec=pltpu.PrefetchScalarGridSpec(num_scalar_...  77.4 us
    pallas_call x2, Pallas kernels, attention_bwd(): pl.pallas_call(functools.partial(attention_bwd_body, chunk, blocks, part,...  74.6 us
    dot_general x10, matrix products, contract(): lax.dot_general(left, right, (((left_dim,), (right_dim,)), ((), ())), pre...  62.5 us
    pallas_call x2, Pallas kernels, attention_fwd(): pl.pallas_call(functools.partial(attention_fwd_body, chunk, blocks, part)...  52.4 us
  transfers between devices with their start and end apart: 76, of which 33 were waited for; matrix products, arithmetic and copies ran while one was open for 22% of the time, Pallas kernels for 34%

profile of v5, /device:TPU:0, one launch (start us, length us, event | category | flops | bytes accessed | tf_op | source)
XLA Modules:
  0.0 1152.9 jit_solution(17608616016384093547)
XLA Ops:
  65.0 19.0 %collective-permute-done.5 = bf16[64,12288]{1,0:T(8,128)(2,1)} collective-permute-done((bf16[64,12288]{1,0:T(8,128)(2,1)}, bf16[64,12288]{1,0:T(8,128)(2,1)}, u32[]{:S(2)}, u32[]{:S(2)}) %collective-permute-start.5) | collective-permute-done | bytes 1572896 | tf_op jit(solution)/shard_map/ppermute | solution.py:38
  90.2 38.5 %collective-permute-done.13.refs_1_ = bf16[512,2048]{1,0:T(8,128)(2,1)} collective-permute-done((bf16[512,2048]{1,0:T(8,128)(2,1)}, bf16[512,2048]{1,0:T(8,128)(2,1)}, u32[]{:S(2)}, u32[]{:S(2)}) %collective-permute-start.13) | collective-permute-done | bytes 2097184 | tf_op jit(solution)/shard_map/ppermute | solution.py:38
  154.9 26.4 %collective-permute-done.4 = bf16[1024,768]{1,0:T(8,128)(2,1)S(1)} collective-permute-done((bf16[1024,768]{1,0:T(8,128)(2,1)}, bf16[1024,768]{1,0:T(8,128)(2,1)S(1)}, u32[]{:S(2)}, u32[]{:S(2)}) %collective-permute-start.4) | collective-permute-done | bytes 1572896 | tf_op jit(solution)/shard_map/ppermute | solution.py:38
  202.1 16.5 %collective-permute-done.17 = bf16[256,2048]{1,0:T(8,128)(2,1)} collective-permute-done((bf16[256,2048]{1,0:T(8,128)(2,1)}, bf16[256,2048]{1,0:T(8,128)(2,1)}, u32[]{:S(2)}, u32[]{:S(2)}) %collective-permute-start.17) | collective-permute-done | bytes 1048608 | tf_op jit(solution)/shard_map/ppermute | solution.py:38
  221.3 26.1 %attention_forward.2 = (bf16[512,1024]{1,0:T(8,128)(2,1)}, f32[2,4,1024]{2,1,0:T(4,128)}) custom-call(s32[2,4]{1,0:T(2,128)} %get-tuple-element.88.qpos_ref, s32[2,8]{1,0:T(2,128)} %stack.83.kpos_ref, s32[2]{0:T(128)} %pad_add_fusion.4.len_ref, bf16[512,2048]{1,0:T(8,128)(2,1)} %bitcast.76, bf16[2,128,2048]{2,1,0:T(8,128)(2,1)} %get-tuple-element.105.k_ref, ...), custom_call_target="tpu_custom_call" | custom-call | flops 34359738368 | bytes 4194304 | tf_op jit(solution)/shard_map/attention_forward/pallas_call | solution.py:424
  276.4 26.3 %attention_forward.3 = (bf16[512,1024]{1,0:T(8,128)(2,1)}, f32[2,4,1024]{2,1,0:T(4,128)}) custom-call(s32[2,4]{1,0:T(2,128)} %get-tuple-element.88.qpos_ref, s32[2,8]{1,0:T(2,128)} %stack.83.kpos_ref, s32[2]{0:T(128)} %pad_add_fusion.4.len_ref, bf16[512,2048]{1,0:T(8,128)(2,1)} %bitcast.77, bf16[2,128,2048]{2,1,0:T(8,128)(2,1)} %get-tuple-element.105.k_ref, ...), custom_call_target="tpu_custom_call" | custom-call | flops 34359738368 | bytes 4194304 | tf_op jit(solution)/shard_map/attention_forward/pallas_call | solution.py:424
  314.5 49.7 %collective-permute-done.22 = bf16[512,2048]{1,0:T(8,128)(2,1)S(1)} collective-permute-done((bf16[512,2048]{1,0:T(8,128)(2,1)}, bf16[512,2048]{1,0:T(8,128)(2,1)S(1)}, u32[]{:S(2)}, u32[]{:S(2)}) %collective-permute-start.22) | collective-permute-done | bytes 2097184 | tf_op jit(solution)/shard_map/ppermute | solution.py:38
  380.2 45.4 %collective-permute-done.25 = bf16[512,2048]{1,0:T(8,128)(2,1)S(1)} collective-permute-done((bf16[512,2048]{1,0:T(8,128)(2,1)S(1)}, bf16[512,2048]{1,0:T(8,128)(2,1)S(1)}, u32[]{:S(2)}, u32[]{:S(2)}) %collective-permute-start.25) | collective-permute-done | bytes 2097184 | tf_op jit(solution)/shard_map/ppermute | solution.py:38
  426.1 14.2 %pad_maximum_fusion.2.left_ref.refs_0_ = bf16[2048,2048]{1,0:T(8,128)(2,1)} fusion(bf16[512,2048]{1,0:T(8,128)(2,1)} %collective-permute-done.19, bf16[512,2048]{1,0:T(8,128)(2,1)} %collective-permute-done.20, bf16[512,2048]{1,0:T(8,128)(2,1)S(1)} %collective-permute-done.28, bf16[512,2048]{1,0:T(8,128)(2,1)S(1)} %copy-done.9), kind=kLoop, calls=%fused_computation.2 | loop fusion | flops 33554432 | bytes 16777216 | tf_op jit(solution)/shard_map/concatenate | solution.py:685
  446.3 24.6 %gate.1.refs_3_ = bf16[2048,2048]{1,0:T(8,128)(2,1)} custom-call(s32[2]{0:T(128)} %broadcast.234.places_ref, bf16[2048,2048]{1,0:T(8,128)(2,1)} %pad_maximum_fusion.1.refs_0_.left_ref, bf16[1024,2048]{1,0:T(8,128)(2,1)} %hold.18.refs_1_.refs_2_, bf16[1024,2048]{1,0:T(8,128)(2,1)} %copy-done.35), custom_call_target="tpu_custom_call" | custom-call | flops 17179869184 | bytes 25165824 | tf_op jit(solution)/shard_map/gate/pallas_call | solution.py:239
  470.8 27.3 %up.1 = (bf16[2048,2048]{1,0:T(8,128)(2,1)}, bf16[2048,2048]{1,0:T(8,128)(2,1)}) custom-call(s32[2]{0:T(128)} %and_select_fusion.places_ref.slots_ref, bf16[2048,2048]{1,0:T(8,128)(2,1)} %pad_maximum_fusion.1.refs_0_.left_ref, bf16[2048,2048]{1,0:T(8,128)(2,1)} %all-gather.12.cloned.1.call-done.refs_1_.refs_2_.refs_3_, ...), custom_call_target="tpu_custom_call" | custom-call | flops 17179869184 | bytes 25165824 | tf_op jit(solution)/shard_map/up/pallas_call | solution.py:239
  498.2 28.5 %down_grad.1 = bf16[2048,2048]{1,0:T(8,128)(2,1)} custom-call(s32[2]{0:T(128)} %and_select_fusion.places_ref.slots_ref, bf16[2048,2048]{1,0:T(8,128)(2,1)} %pad_maximum_fusion.2.left_ref.refs_0_, bf16[2048,2048]{1,0:T(8,128)(2,1)} %get-tuple-element.67.right_ref.refs_0_), custom_call_target="tpu_custom_call" | custom-call | flops 17179869184 | bytes 20971520 | tf_op jit(solution)/shard_map/down_grad/pallas_call | solution.py:309
  530.4 31.4 %hidden_grad.1 = (bf16[2048,2048]{1,0:T(8,128)(2,1)}, bf16[2048,2048]{1,0:T(8,128)(2,1)}) custom-call(s32[2]{0:T(128)} %and_select_fusion.places_ref.slots_ref, bf16[2048,2048]{1,0:T(8,128)(2,1)} %pad_maximum_fusion.2.left_ref.refs_0_, bf16[2048,2048]{1,0:T(8,128)(2,1)} %all-gather.14.cloned.1.call-done.refs_1_.refs_2_, ...), custom_call_target="tpu_custom_call" | custom-call | flops 17179869184 | bytes 25165824 | tf_op jit(solution)/shard_map/hidden_grad/pallas_call | solution.py:239
  561.8 24.7 %norm_grad.2 = bf16[2048,1024]{1,0:T(8,128)(2,1)} custom-call(s32[2]{0:T(128)} %pad_add_fusion.3.places_ref, bf16[2048,2048]{1,0:T(8,128)(2,1)} %get-tuple-element.59.refs_0_.right_ref, bf16[2048,2048]{1,0:T(8,128)(2,1)} %get-tuple-element.58.refs_1_.right_ref, bf16[1024,2048]{1,0:T(8,128)(2,1)} %hold.18.refs_1_.refs_2_, ...), custom_call_target="tpu_custom_call" | custom-call | flops 17179869184 | bytes 25165824 | tf_op jit(solution)/shard_map/norm_grad/pallas_call | solution.py:271
  586.5 24.6 %norm_grad.3 = bf16[2048,1024]{1,0:T(8,128)(2,1)} custom-call(s32[2]{0:T(128)} %pad_add_fusion.2.places_ref, bf16[2048,2048]{1,0:T(8,128)(2,1)} %get-tuple-element.59.refs_0_.right_ref, bf16[2048,2048]{1,0:T(8,128)(2,1)} %get-tuple-element.58.refs_1_.right_ref, bf16[1024,2048]{1,0:T(8,128)(2,1)} %copy-done.35, ...), custom_call_target="tpu_custom_call" | custom-call | flops 17179869184 | bytes 25165824 | tf_op jit(solution)/shard_map/norm_grad/pallas_call | solution.py:271
  611.1 28.7 %gate_grad.1 = bf16[2048,2048]{1,0:T(8,128)(2,1)} custom-call(s32[2]{0:T(128)} %and_select_fusion.places_ref.slots_ref, bf16[2048,2048]{1,0:T(8,128)(2,1)} %pad_maximum_fusion.1.refs_0_.left_ref, bf16[2048,2048]{1,0:T(8,128)(2,1)} %get-tuple-element.59.refs_0_.right_ref), custom_call_target="tpu_custom_call" | custom-call | flops 17179869184 | bytes 20971520 | tf_op jit(solution)/shard_map/gate_grad/pallas_call | solution.py:309
  655.0 28.7 %up_grad.1 = bf16[2048,2048]{1,0:T(8,128)(2,1)} custom-call(s32[2]{0:T(128)} %and_select_fusion.places_ref.slots_ref, bf16[2048,2048]{1,0:T(8,128)(2,1)} %pad_maximum_fusion.1.refs_0_.left_ref, bf16[2048,2048]{1,0:T(8,128)(2,1)} %get-tuple-element.58.refs_1_.right_ref), custom_call_target="tpu_custom_call" | custom-call | flops 17179869184 | bytes 20971520 | tf_op jit(solution)/shard_map/up_grad/pallas_call | solution.py:309
  683.7 14.2 %collective-permute-done.30 = bf16[512,1024]{1,0:T(8,128)(2,1)S(1)} collective-permute-done((bf16[512,1024]{1,0:T(8,128)(2,1)}, bf16[512,1024]{1,0:T(8,128)(2,1)S(1)}, u32[]{:S(2)}, u32[]{:S(2)}) %collective-permute-start.30) | collective-permute-done | bytes 1048608 | tf_op jit(solution)/shard_map/ppermute | solution.py:38
  717.5 37.1 %attention_backward.2 = (f32[512,1024]{1,0:T(8,128)}, f32[2,128,2048]{2,1,0:T(8,128)}, f32[2,128,2048]{2,1,0:T(8,128)}) custom-call(s32[2,4]{1,0:T(2,128)} %get-tuple-element.88.qpos_ref, s32[2,8]{1,0:T(2,128)} %stack.83.kpos_ref, s32[2]{0:T(128)} %pad_add_fusion.4.len_ref, bf16[512,2048]{1,0:T(8,128)(2,1)} %bitcast.78, ...), custom_call_target="tpu_custom_call" | custom-call | flops 42949672960 | bytes 14680064 | tf_op jit(solution)/shard_map/attention_backward/pallas_call | solution.py:544
  807.2 37.4 %attention_backward.3 = (f32[512,1024]{1,0:T(8,128)}, bf16[2,128,2048]{2,1,0:T(8,128)(2,1)}, bf16[2,128,2048]{2,1,0:T(8,128)(2,1)}) custom-call(s32[2,4]{1,0:T(2,128)} %get-tuple-element.88.qpos_ref, s32[2,8]{1,0:T(2,128)} %stack.83.kpos_ref, s32[2]{0:T(128)} %pad_add_fusion.4.len_ref, bf16[512,2048]{1,0:T(8,128)(2,1)} %bitcast.79, ...), custom_call_target="tpu_custom_call" | custom-call | flops 42949672960 | bytes 14680064 | tf_op jit(solution)/shard_map/attention_backward/pallas_call | solution.py:544
  867.0 24.7 %collective-permute-done.42 = bf16[256,2048]{1,0:T(8,128)(2,1)S(1)} collective-permute-done((bf16[256,2048]{1,0:T(8,128)(2,1)S(1)}, bf16[256,2048]{1,0:T(8,128)(2,1)S(1)}, u32[]{:S(2)}, u32[]{:S(2)}) %collective-permute-start.42) | collective-permute-done | bytes 1048608 | tf_op jit(solution)/shard_map/ppermute | solution.py:38
  935.2 42.3 %collective-permute-done.51 = bf16[1024,768]{1,0:T(8,128)(2,1)} collective-permute-done((bf16[1024,768]{1,0:T(8,128)(2,1)}, bf16[1024,768]{1,0:T(8,128)(2,1)}, u32[]{:S(2)}, u32[]{:S(2)}) %collective-permute-start.51) | collective-permute-done | bytes 1572896 | tf_op jit(solution)/shard_map/ppermute | solution.py:38
  1028.8 28.1 %collective-permute-done.44.refs_1_ = bf16[512,2048]{1,0:T(8,128)(2,1)} collective-permute-done((bf16[512,2048]{1,0:T(8,128)(2,1)}, bf16[512,2048]{1,0:T(8,128)(2,1)}, u32[]{:S(2)}, u32[]{:S(2)}) %collective-permute-start.44) | collective-permute-done | bytes 2097184 | tf_op jit(solution)/shard_map/ppermute | solution.py:38
  1075.5 15.9 %collective-permute-start.48 = (f32[256]{0:T(256)S(1)}, f32[256]{0:T(256)S(1)}, u32[]{:S(2)}, u32[]{:S(2)}) collective-permute-start(f32[256]{0:T(256)S(1)} %bitcast.112), channel_id=1, source_target_pairs={{0,8},{8,16},{16,24},{24,0},{1,9},{9,17},{17,25},{25,1},{2,10},{10... | collective-permute-start | bytes 3080 | tf_op jit(solution)/shard_map/ppermute | solution.py:38
  (507 shorter events, 454.8 us)
Async XLA Ops:
  7.2 121.5 %all-gather.8.cloned.1.call-start = ((), (), s32[]{:S(2)}) async-start(), calls=%async_computation.6 | async-start | bytes 1310720 | tf_op jit(solution)/shard_map/all_gather | solution.py:101
  63.6 65.1 %collective-permute-start.13 = (bf16[512,2048]{1,0:T(8,128)(2,1)}, bf16[512,2048]{1,0:T(8,128)(2,1)}, u32[]{:S(2)}, u32[]{:S(2)}) collective-permute-start(bf16[512,2048]{1,0:T(8,128)(2,1)} %fusion.4.refs_1_), channel_id=1, source_target_pairs={{0,1},{1,0},{2,3},{3,2},{4,5},{5,4},{6,7},{7,6},{8,9},{9,8},{10,11... | collective-permute-start | bytes 6291464 | tf_op jit(solution)/shard_map/ppermute | solution.py:38
  64.9 79.6 %all-gather.6.cloned.1.call-start = ((), (), s32[]{:S(2)}) async-start(), calls=%async_computation.5 | async-start | bytes 1966080 | tf_op jit(solution)/shard_map/all_gather | solution.py:101
  90.2 178.1 %all-gather.10.cloned.1.call-start = ((), (), s32[]{:S(2)}) async-start(), calls=%async_computation.7 | async-start | bytes 5242880 | tf_op jit(solution)/shard_map/all_gather | solution.py:101
  134.0 336.8 %all-gather.12.cloned.1.call-start = ((), (), s32[]{:S(2)}) async-start(), calls=%async_computation.8 | async-start | bytes 9437184 | tf_op jit(solution)/shard_map/all_gather | solution.py:113
  134.6 395.8 %all-gather.14.cloned.1.call-start = ((), (), s32[]{:S(2)}) async-start(), calls=%async_computation.10 | async-start | bytes 9437184 | tf_op jit(solution)/shard_map/all_gather | solution.py:113
  196.2 54.6 %collective-permute-start.16 = (bf16[1024,512]{1,0:T(8,128)(2,1)}, bf16[1024,512]{1,0:T(8,128)(2,1)}, u32[]{:S(2)}, u32[]{:S(2)}) collective-permute-start(bf16[1024,512]{1,0:T(8,128)(2,1)} %hold.15.refs_1_), channel_id=1, source_target_pairs={{0,2},{2,0},{1,3},{3,1},{4,6},{6,4},{5,7},{7,5},{8,10},{10,8},{9,1... | collective-permute-start | bytes 3145736 | tf_op jit(solution)/shard_map/ppermute | solution.py:38
  200.6 57.7 %collective-permute-start.19 = (bf16[512,2048]{1,0:T(8,128)(2,1)}, bf16[512,2048]{1,0:T(8,128)(2,1)}, u32[]{:S(2)}, u32[]{:S(2)}) collective-permute-start(bf16[512,2048]{1,0:T(8,128)(2,1)} %hold.16), channel_id=1, source_target_pairs={{0,1},{1,0},{2,3},{3,2},{4,5},{5,4},{6,7},{7,6},{8,9},{9,8},{10,11... | collective-permute-start | bytes 6291464 | tf_op jit(solution)/shard_map/ppermute | solution.py:38
  258.9 458.6 %reduce-scatter.6.cloned.1.call-start = ((), (), s32[]{:S(2)}) async-start(), calls=%async_computation.9 | async-start | bytes 9437184 | tf_op jit(solution)/shard_map/reduce_scatter | solution.py:117
  266.5 48.0 %collective-permute-start.21 = (bf16[512,2048]{1,0:T(8,128)(2,1)}, bf16[512,2048]{1,0:T(8,128)(2,1)}, u32[]{:S(2)}, u32[]{:S(2)}) collective-permute-start(bf16[512,2048]{1,0:T(8,128)(2,1)} %add_convert_fusion), channel_id=1, source_target_pairs={{0,1},{1,0},{2,3},{3,2},{4,5},{5,4},{6,7},{7,6},{8,9},{9,8},{10,11... | collective-permute-start | bytes 6291464 | tf_op jit(solution)/shard_map/ppermute | solution.py:38
  273.2 91.0 %collective-permute-start.22 = (bf16[512,2048]{1,0:T(8,128)(2,1)}, bf16[512,2048]{1,0:T(8,128)(2,1)S(1)}, u32[]{:S(2)}, u32[]{:S(2)}) collective-permute-start(bf16[512,2048]{1,0:T(8,128)(2,1)} %get-tuple-element.92), channel_id=1, source_target_pairs={{0,2},{2,0},{1,3},{3,1},{4,6},{6,4},{5,7},{7,5},{8,10},{10,8},{9,1... | collective-permute-start | bytes 6291464 | tf_op jit(solution)/shard_map/ppermute | solution.py:38
  377.9 47.7 %collective-permute-start.25 = (bf16[512,2048]{1,0:T(8,128)(2,1)S(1)}, bf16[512,2048]{1,0:T(8,128)(2,1)S(1)}, u32[]{:S(2)}, u32[]{:S(2)}) collective-permute-start(bf16[512,2048]{1,0:T(8,128)(2,1)S(1)} %multiply_convert_fusion), channel_id=1, source_target_pairs={{0,1},{1,0},{2,3},{3,2},{4,5},{5,4},{6,7},{7,6},{8,9},{9,8},{10,11... | collective-permute-start | bytes 6291464 | tf_op jit(solution)/shard_map/ppermute | solution.py:38
  379.4 46.7 %collective-permute-start.28 = (bf16[512,2048]{1,0:T(8,128)(2,1)S(1)}, bf16[512,2048]{1,0:T(8,128)(2,1)S(1)}, u32[]{:S(2)}, u32[]{:S(2)}) collective-permute-start(bf16[512,2048]{1,0:T(8,128)(2,1)S(1)} %copy-done.9), channel_id=1, source_target_pairs={{0,4},{4,0},{1,5},{5,1},{2,6},{6,2},{3,7},{7,3},{8,12},{12,8},{9,1... | collective-permute-start | bytes 6291464 | tf_op jit(solution)/shard_map/ppermute | solution.py:38
  379.5 61.0 %collective-permute-start.27 = (bf16[512,2048]{1,0:T(8,128)(2,1)S(1)}, bf16[512,2048]{1,0:T(8,128)(2,1)S(1)}, u32[]{:S(2)}, u32[]{:S(2)}) collective-permute-start(bf16[512,2048]{1,0:T(8,128)(2,1)S(1)} %copy-done.32), channel_id=1, source_target_pairs={{0,2},{2,0},{1,3},{3,1},{4,6},{6,4},{5,7},{7,5},{8,10},{10,8},{9,1... | collective-permute-start | bytes 6291464 | tf_op jit(solution)/shard_map/ppermute | solution.py:38
  380.0 60.8 %collective-permute-start.24 = (bf16[512,2048]{1,0:T(8,128)(2,1)S(1)}, bf16[512,2048]{1,0:T(8,128)(2,1)S(1)}, u32[]{:S(2)}, u32[]{:S(2)}) collective-permute-start(bf16[512,2048]{1,0:T(8,128)(2,1)S(1)} %multiply_convert_fusion), channel_id=1, source_target_pairs={{0,4},{4,0},{1,5},{5,1},{2,6},{6,2},{3,7},{7,3},{8,12},{12,8},{9,1... | collective-permute-start | bytes 6291464 | tf_op jit(solution)/shard_map/ppermute | solution.py:38
  526.7 366.3 %reduce-scatter.8.cloned.1.call-start = ((), (), s32[]{:S(2)}) async-start(), calls=%async_computation.11 | async-start | bytes 9437184 | tf_op jit(solution)/shard_map/reduce_scatter | solution.py:117
  639.8 355.6 %reduce-scatter.10.cloned.1.call-start = ((), (), s32[]{:S(2)}) async-start(), calls=%async_computation.12 | async-start | bytes 9437184 | tf_op jit(solution)/shard_map/reduce_scatter | solution.py:117
  707.4 82.0 %collective-permute-start.39 = (bf16[512,2048]{1,0:T(8,128)(2,1)S(1)}, bf16[512,2048]{1,0:T(8,128)(2,1)}, u32[]{:S(2)}, u32[]{:S(2)}) collective-permute-start(bf16[512,2048]{1,0:T(8,128)(2,1)S(1)} %get-tuple-element.81), channel_id=1, source_target_pairs={{0,1},{1,0},{2,3},{3,2},{4,5},{5,4},{6,7},{7,6},{8,9},{9,8},{10,11... | collective-permute-start | bytes 6291464 | tf_op jit(solution)/shard_map/ppermute | solution.py:38
  790.7 319.9 %reduce-scatter.12.cloned.1.call-start = ((), (), s32[]{:S(2)}) async-start(), calls=%async_computation.13 | async-start | bytes 1966080 | tf_op jit(solution)/shard_map/reduce_scatter | solution.py:121
  800.1 100.4 %collective-permute-start.37 = (bf16[512,1024]{1,0:T(8,128)(2,1)}, bf16[512,1024]{1,0:T(8,128)(2,1)}, u32[]{:S(2)}, u32[]{:S(2)}) collective-permute-start(bf16[512,1024]{1,0:T(8,128)(2,1)} %add_convert_fusion.2), channel_id=1, source_target_pairs={{0,1},{1,0},{2,3},{3,2},{4,5},{5,4},{6,7},{7,6},{8,9},{9,8},{10,11... | collective-permute-start | bytes 3145736 | tf_op jit(solution)/shard_map/ppermute | solution.py:38
  922.0 62.9 %collective-permute-start.43 = (bf16[1024,2048]{1,0:T(8,128)(2,1)}, bf16[1024,2048]{1,0:T(8,128)(2,1)}, u32[]{:S(2)}, u32[]{:S(2)}) collective-permute-start(bf16[1024,2048]{1,0:T(8,128)(2,1)} %slice.546), channel_id=1, source_target_pairs={{0,4},{4,0},{1,5},{5,1},{2,6},{6,2},{3,7},{7,3},{8,12},{12,8},{9,1... | collective-permute-start | bytes 12582920 | tf_op jit(solution)/shard_map/ppermute | solution.py:38
  929.2 48.2 %collective-permute-start.51 = (bf16[1024,768]{1,0:T(8,128)(2,1)}, bf16[1024,768]{1,0:T(8,128)(2,1)}, u32[]{:S(2)}, u32[]{:S(2)}) collective-permute-start(bf16[1024,768]{1,0:T(8,128)(2,1)} %fusion.39), channel_id=1, source_target_pairs={{0,2},{2,0},{1,3},{3,1},{4,6},{6,4},{5,7},{7,5},{8,10},{10,8},{9,1... | collective-permute-start | bytes 4718600 | tf_op jit(solution)/shard_map/ppermute | solution.py:38
  995.4 141.5 %reduce-scatter.14.cloned.1.call-start = ((), (), s32[]{:S(2)}) async-start(), calls=%async_computation.14 | async-start | bytes 2359296 | tf_op jit(solution)/shard_map/reduce_scatter | solution.py:117
  1009.7 47.2 %collective-permute-start.44 = (bf16[512,2048]{1,0:T(8,128)(2,1)}, bf16[512,2048]{1,0:T(8,128)(2,1)}, u32[]{:S(2)}, u32[]{:S(2)}) collective-permute-start(bf16[512,2048]{1,0:T(8,128)(2,1)} %fusion.17.refs_2_.refs_1_), channel_id=1, source_target_pairs={{0,1},{1,0},{2,3},{3,2},{4,5},{5,4},{6,7},{7,6},{8,9},{9,8},{10,11... | collective-permute-start | bytes 6291464 | tf_op jit(solution)/shard_map/ppermute | solution.py:38
  (121 other events, 1670.8 us)
Sparse Core Ops, SparseCore 0:
  65.0 28.7 all-gather.7
  95.9 36.5 all-gather.5
  134.2 82.2 all-gather.9
  218.4 165.5 all-gather.11
  386.0 129.8 all-gather.13
  526.8 149.1 reduce-scatter.5
  680.1 148.0 reduce-scatter.7
  831.8 155.9 reduce-scatter.9
  995.5 47.4 reduce-scatter.11
  1046.7 66.4 reduce-scatter.13
